TPU v7x, 512 devices: a whole 4x4x16 slice. The times are simulated.
512 devices in a mesh: gx: 32 (over z, core), gy: 16 (over x, y).
Axes of the slice: x: 4, y: 4, z: 16, core: 2. Of those that a mesh axis runs over, the one named last changes fastest.
Arguments:
- adjoint: float32 [3, 8, 512, 2048], P(None, None, 'gx', 'gy'), may hold values from -12 to 12
- checkpoints: bfloat16 [1, 3, 8, 512, 2048], P(None, None, None, 'gx', 'gy'), may hold values from -3 to 3
- wall_faces: int32 [2, 64, 256], P(None, 'gx', 'gy'), may hold values 0 or 1
Outputs:
- velocity: float32 [3, 8, 512, 2048], P(None, None, 'gx', 'gy')
- pressure: float32 [8, 512, 2048], P(None, 'gx', 'gy')
Inputs may be any that keep to these rules, and one draw needn't show every extreme that they name: `wall_faces`: 1 marks a no-slip face, 0 an open one.
All inputs are finite; a program needn't handle non-finite values. No bound on the sum of `wall_faces` on one device may be relied on, other than what follows from the above.
Results may differ from a plain program's by a relative error of at most 0.0003.
Values sent between devices are 32-bit elements; how exact they have to be, the bound alone decides.
No kernel may reach another device: no remote copies, remote signals or barrier semaphores. Data moves between devices by JAX's collectives and lax.ppermute only.
A program may use at most 64 MiB of HBM per device.

v0:
```python
import jax
import jax.numpy as jnp
import numpy as np
from jax import lax
from jax.sharding import PartitionSpec as P

ITERS = 4


node_points = np.array(
    [
        -1.0,
        -0.8717401485096066,
        -0.5917001814331423,
        -0.2092992179024789,
        0.2092992179024789,
        0.5917001814331423,
        0.8717401485096066,
        1.0,
    ]
)
node_weights = np.array(
    [
        0.03571428571428571,
        0.2107042271435061,
        0.3411226924835044,
        0.4124587946587038,
        0.4124587946587038,
        0.3411226924835044,
        0.2107042271435061,
        0.03571428571428571,
    ]
)
time_step = 0.05
viscosity = 0.02
highest = lax.Precision.HIGHEST


def with_halo(value, sides, width):
    for axis, dim in sides:
        size, length = (lax.axis_size(axis), value.shape[dim])
        up = [(i, (i + 1) % size) for i in range(size)]
        down = [(j, i) for i, j in up]
        last = lax.slice_in_dim(value, length - width, length, axis=dim)
        initial = lax.slice_in_dim(value, 0, width, axis=dim)
        before = lax.ppermute(last, axis, up)
        after = lax.ppermute(initial, axis, down)
        value = jnp.concatenate([before, value, after], axis=dim)
    return value


def derivative_table(points):
    identity = np.eye(points.shape[0])
    spacing = points[:, None] - points[None, :] + identity
    barycentric = 1.0 / np.prod(spacing, axis=1)
    matrix = barycentric[None, :] / barycentric[:, None] / spacing
    matrix = matrix * (1.0 - identity)
    return matrix - identity * np.sum(matrix, axis=1)[:, None]


def along_rows(nodal, matrix):
    blocked = jnp.asarray(np.kron(np.eye(nodal.shape[2] // 8), matrix), jnp.float32)
    return jnp.einsum("xk,czky->czxy", blocked, nodal, precision=highest)


def along_columns(nodal, matrix):
    size_y = nodal.shape[3]
    block_width = 128 if size_y % 128 == 0 else size_y
    blocked = jnp.asarray(np.kron(np.eye(block_width // 8), matrix).T, jnp.float32)
    grouped = nodal.reshape(
        nodal.shape[0], nodal.shape[1], nodal.shape[2], size_y // block_width, block_width
    )
    result = jnp.einsum("czxgk,kb->czxgb", grouped, blocked, precision=highest)
    return result.reshape(nodal.shape)


def along_depth(nodal, matrix):
    return jnp.einsum("ck,akxy->acxy", jnp.asarray(matrix, jnp.float32), nodal, precision=highest)


def mass_weights(size_x, size_y):
    weights = jnp.asarray(node_weights, jnp.float32)
    across_x = jnp.tile(weights, size_x // 8)
    across_y = jnp.tile(weights, size_y // 8)
    return weights[:, None, None] * across_x[None, :, None] * across_y[None, None, :]


def edge_flags(length):
    place = jnp.arange(length) % 8
    return ((place == 0) | (place == 7)).astype(jnp.float32)


def share_counts(size_x, size_y):
    return (1.0 + edge_flags(size_x))[:, None] * (1.0 + edge_flags(size_y))[None, :]


def boundary_masks(wall_faces, size_x, size_y):
    walls = jnp.repeat(jnp.repeat(wall_faces.astype(jnp.float32), 8, axis=1), 8, axis=2)
    interior = (1.0 - edge_flags(size_x))[:, None] * (1.0 - edge_flags(size_y))[None, :]
    middle = jnp.ones((6, size_x, size_y), jnp.float32)
    velocity_mask = jnp.concatenate(
        [(interior * (1.0 - walls[0]))[None], middle, (interior * (1.0 - walls[1]))[None]], axis=0
    )
    pressure_mask = jnp.concatenate(
        [(interior * walls[0])[None], middle, (interior * walls[1])[None]], axis=0
    )
    return (velocity_mask, pressure_mask)


def sum_rows(padded):
    size_x = padded.shape[2] - 2
    place = jnp.arange(size_x) % 8
    upper = (place == 7).astype(jnp.float32)[:, None]
    lower = (place == 0).astype(jnp.float32)[:, None]
    return padded[:, :, 1:-1, :] + upper * padded[:, :, 2:, :] + lower * padded[:, :, :-2, :]


def sum_columns(padded):
    size_y = padded.shape[3] - 2
    place = jnp.arange(size_y) % 8
    upper = (place == 7).astype(jnp.float32)
    lower = (place == 0).astype(jnp.float32)
    return padded[:, :, :, 1:-1] + upper * padded[:, :, :, 2:] + lower * padded[:, :, :, :-2]


def assemble_velocity(nodal):
    padded = with_halo(nodal, (("gx", 2), ("gy", 3)), 1)
    return sum_columns(sum_rows(padded))


def assemble_pressure(nodal):
    padded = with_halo(nodal, (("gx", 2), ("gy", 3)), 1)
    return sum_columns(sum_rows(padded))


def stiffness(nodal, wmass):
    derivative = derivative_table(node_points)
    transposed = derivative.T
    return (
        along_rows(wmass * along_rows(nodal, derivative), transposed)
        + along_columns(wmass * along_columns(nodal, derivative), transposed)
        + along_depth(wmass * along_depth(nodal, derivative), transposed)
    )


def inner(former, latter, inverse_share):
    return jnp.sum(former * latter * inverse_share)


def solve_pressure(source, pressure_mask, wmass, inverse_share):
    pressure = jnp.zeros_like(source)
    resid = source
    direction = source
    norm_now = jnp.zeros((), jnp.float32)
    for round_index in range(ITERS):
        image = pressure_mask * assemble_pressure(stiffness(direction, wmass))
        if round_index == 0:
            norm_now, curve = lax.psum(
                (inner(resid, resid, inverse_share), inner(direction, image, inverse_share)),
                ("gx", "gy"),
            )
        else:
            curve = lax.psum(inner(direction, image, inverse_share), ("gx", "gy"))
        step_length = norm_now / curve
        pressure = pressure + step_length * direction
        resid = resid - step_length * image
        if round_index + 1 < ITERS:
            norm_next = lax.psum(inner(resid, resid, inverse_share), ("gx", "gy"))
            direction = resid + norm_next / norm_now * direction
            norm_now = norm_next
    return pressure


def adjoint_step(velocity, forward, velocity_mask, pressure_mask, wmass, amass, inverse_share):
    derivative = derivative_table(node_points)
    flow = forward.astype(jnp.float32)
    flow_dx = along_rows(flow, derivative)
    flow_dy = along_columns(flow, derivative)
    flow_dz = along_depth(flow, derivative)
    velocity_dx = along_rows(velocity, derivative)
    velocity_dy = along_columns(velocity, derivative)
    velocity_dz = along_depth(velocity, derivative)
    transport = flow[0:1] * velocity_dx + flow[1:2] * velocity_dy + flow[2:3] * velocity_dz
    stretch = jnp.concatenate(
        [
            jnp.sum(velocity * flow_dx, axis=0, keepdims=True),
            jnp.sum(velocity * flow_dy, axis=0, keepdims=True),
            jnp.sum(velocity * flow_dz, axis=0, keepdims=True),
        ],
        axis=0,
    )
    advect = transport - stretch
    forcing = wmass * (velocity + time_step * advect) - time_step * viscosity * stiffness(
        velocity, wmass
    )
    moved = velocity_mask * assemble_velocity(forcing) / amass
    diverge = (
        along_rows(moved[0:1], derivative)
        + along_columns(moved[1:2], derivative)
        + along_depth(moved[2:3], derivative)
    )
    source = -pressure_mask * assemble_pressure(wmass * diverge)
    pressure = solve_pressure(source, pressure_mask, wmass, inverse_share)
    slopes = jnp.concatenate(
        [
            along_rows(pressure, derivative),
            along_columns(pressure, derivative),
            along_depth(pressure, derivative),
        ],
        axis=0,
    )
    correction = assemble_velocity(wmass * slopes) / amass
    return (velocity_mask * (moved - correction), pressure)


def local(adjoint, checkpoints, wall_faces):
    size_x = adjoint.shape[2]
    size_y = adjoint.shape[3]
    wmass = mass_weights(size_x, size_y)
    counts = share_counts(size_x, size_y)
    inverse_share = 1.0 / counts
    amass = wmass * counts
    velocity_mask, pressure_mask = boundary_masks(wall_faces, size_x, size_y)
    velocity = adjoint
    velocity, pressure = adjoint_step(
        velocity, checkpoints[0], velocity_mask, pressure_mask, wmass, amass, inverse_share
    )
    return (velocity, pressure[0])


def solution(mesh):
    return jax.shard_map(
        local,
        mesh=mesh,
        in_specs=(P(None, None, "gx", "gy"), P(None, None, None, "gx", "gy"), P(None, "gx", "gy")),
        out_specs=(P(None, None, "gx", "gy"), P(None, "gx", "gy")),
        check_vma=False,
    )
```

profile of v0, /device:TPU:1, one launch (start us, length us, event | category | flops | bytes accessed | tf_op | source)
XLA Modules:
  0.0 876.8 jit_solution(5244411411854615604)
XLA Ops:
  1.3 1.3 convolution_bitcast_fusion.3
  9.0 3.0 collective-permute-start
  12.1 3.9 collective-permute-start.1
  17.0 1.9 collective-permute-start.2
  18.9 6.7 collective-permute-start.3
  25.6 2.2 collective-permute-done.2
  27.8 1.5 collective-permute-done.3
  32.4 1.8 collective-permute-start.4
  34.3 3.5 collective-permute-start.5
  38.7 1.9 collective-permute-start.6
  40.6 7.4 collective-permute-start.7
  48.1 1.6 collective-permute-done.7
  53.3 6.4 collective-permute-start.9
  60.6 1.9 collective-permute-start.10
  62.6 7.4 collective-permute-start.11
  70.0 1.6 collective-permute-done.11
  72.6 108.5 %all-reduce = (f32[]{:T(128)}, f32[]{:T(128)}) all-reduce(f32[]{:T(128)} %get-tuple-element.3, f32[]{:T(128)} %get-tuple-element.2), channel_id=1, replica_groups=mesh['gx'=32,'gy'=16] {'gx','gy'}, use_global_device_ids=true, to_apply=%region_4.5 | all-reduce | flops 2 | bytes 16 | tf_op jit(solution)/shard_map/psum | solution.py:158
  183.2 98.5 %psum.58 = f32[]{:T(128)} all-reduce(f32[]{:T(128)} %multiply_reduce_fusion.4), channel_id=1, replica_groups=mesh['gx'=32,'gy'=16] {'gx','gy'}, use_global_device_ids=true, to_apply=%region_8.9 | all-reduce | flops 1 | bytes 8 | tf_op jit(solution)/shard_map/psum | solution.py:168
  284.5 2.3 collective-permute-start.12
  287.6 2.3 collective-permute-done.13
  289.9 2.2 collective-permute-start.14
  292.2 6.4 collective-permute-start.15
  298.6 1.4 collective-permute-done.14
  299.9 0.9 collective-permute-done.15
  301.8 102.7 %psum.59 = f32[]{:T(128)} all-reduce(f32[]{:T(128)} %get-tuple-element.10), channel_id=1, replica_groups=mesh['gx'=32,'gy'=16] {'gx','gy'}, use_global_device_ids=true, to_apply=%region_10.11 | all-reduce | flops 1 | bytes 8 | tf_op jit(solution)/shard_map/psum | solution.py:163
  406.6 99.3 %psum.60 = f32[]{:T(128)} all-reduce(f32[]{:T(128)} %get-tuple-element.8), channel_id=1, replica_groups=mesh['gx'=32,'gy'=16] {'gx','gy'}, use_global_device_ids=true, to_apply=%region_12.13 | all-reduce | flops 1 | bytes 8 | tf_op jit(solution)/shard_map/psum | solution.py:168
  508.6 1.4 collective-permute-start.16
  510.8 2.3 collective-permute-done.17
  513.3 2.3 collective-permute-start.18
  515.6 6.3 collective-permute-start.19
  522.4 1.1 collective-permute-done.19
  524.5 104.3 %psum.61 = f32[]{:T(128)} all-reduce(f32[]{:T(128)} %get-tuple-element.6), channel_id=1, replica_groups=mesh['gx'=32,'gy'=16] {'gx','gy'}, use_global_device_ids=true, to_apply=%region_14.15 | all-reduce | flops 1 | bytes 8 | tf_op jit(solution)/shard_map/psum | solution.py:163
  630.8 98.4 %psum.62 = f32[]{:T(128)} all-reduce(f32[]{:T(128)} %multiply_reduce_fusion), channel_id=1, replica_groups=mesh['gx'=32,'gy'=16] {'gx','gy'}, use_global_device_ids=true, to_apply=%region_16.17 | all-reduce | flops 1 | bytes 8 | tf_op jit(solution)/shard_map/psum | solution.py:168
  731.9 2.3 collective-permute-start.20
  735.0 2.3 collective-permute-done.21
  737.4 2.5 collective-permute-start.22
  739.9 6.1 collective-permute-start.23
  746.0 1.4 collective-permute-done.22
  747.4 0.9 collective-permute-done.23
  749.3 102.6 %psum.63 = f32[]{:T(128)} all-reduce(f32[]{:T(128)} %fusion.73), channel_id=1, replica_groups=mesh['gx'=32,'gy'=16] {'gx','gy'}, use_global_device_ids=true, to_apply=%region_18.19 | all-reduce | flops 1 | bytes 8 | tf_op jit(solution)/shard_map/psum | solution.py:163
  854.3 2.7 collective-permute-start.24
  857.0 0.8 collective-permute-done.24
  857.8 2.3 collective-permute-done.25
  860.3 1.9 collective-permute-start.26
  862.2 6.7 collective-permute-start.27
  868.9 5.4 collective-permute-done.26
  874.3 1.0 collective-permute-done.27
  875.8 1.0 fusion.35
  (175 shorter events, 31.4 us)
Async XLA Ops:
  0.6 0.7 copy-start.11
  1.3 1.3 copy-start
  1.3 1.3 copy-start.2
  2.7 0.8 copy-start.6
  4.1 0.7 copy-start.15
  4.9 0.7 copy-start.12
  6.4 0.7 copy-start.13
  7.1 0.7 copy-start.14
  7.7 0.8 copy-start.10
  9.0 7.6 collective-permute-start
  12.1 3.9 copy-start.16
  12.1 4.7 collective-permute-start.1
  17.0 10.8 %collective-permute-start.2 = (f32[3,8,18,1]{3,2,1,0:T(8,128)S(1)}, f32[3,8,18,1]{3,2,1,0:T(8,128)S(1)}, u32[]{:S(2)}, u32[]{:S(2)}) collective-permute-start(f32[3,8,18,1]{3,2,1,0:T(8,128)S(1)} %get-tuple-element.15), channel_id=1, source_target_pairs={{0,1},{1,2},{2,3},{3,4},{4,5},{5,6},{6,7},{7,8},{8,9},{9,10},{10,1... | collective-permute-start | bytes 5192 | tf_op jit(solution)/shard_map/ppermute | solution.py:46
  18.9 10.3 %collective-permute-start.3 = (f32[3,8,18,1]{3,2,1,0:T(8,128)S(1)}, f32[3,8,18,1]{3,2,1,0:T(8,128)S(1)}, u32[]{:S(2)}, u32[]{:S(2)}) collective-permute-start(f32[3,8,18,1]{3,2,1,0:T(8,128)S(1)} %get-tuple-element.16), channel_id=1, source_target_pairs={{1,0},{2,1},{3,2},{4,3},{5,4},{6,5},{7,6},{8,7},{9,8},{10,9},{11,1... | collective-permute-start | bytes 5192 | tf_op jit(solution)/shard_map/ppermute | solution.py:47
  30.0 0.8 copy-start.1
  30.8 0.7 copy-start.7
  31.5 0.7 copy-start.5
  32.4 5.9 collective-permute-start.4
  34.3 4.3 collective-permute-start.5
  38.7 9.4 %collective-permute-start.6 = (f32[1,8,18,1]{3,2,1,0:T(8,128)S(1)}, f32[1,8,18,1]{3,2,1,0:T(8,128)S(1)}, u32[]{:S(2)}, u32[]{:S(2)}) collective-permute-start(f32[1,8,18,1]{3,2,1,0:T(8,128)S(1)} %get-tuple-element.32), channel_id=1, source_target_pairs={{0,1},{1,2},{2,3},{3,4},{4,5},{5,6},{6,7},{7,8},{8,9},{9,10},{10,1... | collective-permute-start | bytes 1736 | tf_op jit(solution)/shard_map/ppermute | solution.py:46
  40.6 9.1 %collective-permute-start.7 = (f32[1,8,18,1]{3,2,1,0:T(8,128)S(1)}, f32[1,8,18,1]{3,2,1,0:T(8,128)S(1)}, u32[]{:S(2)}, u32[]{:S(2)}) collective-permute-start(f32[1,8,18,1]{3,2,1,0:T(8,128)S(1)} %get-tuple-element.33), channel_id=1, source_target_pairs={{1,0},{2,1},{3,2},{4,3},{5,4},{6,5},{7,6},{8,7},{9,8},{10,9},{11,1... | collective-permute-start | bytes 1736 | tf_op jit(solution)/shard_map/ppermute | solution.py:47
  50.8 0.8 copy-start.3
  51.6 0.7 copy-start.9
  52.3 0.7 copy-start.8
  53.3 7.1 collective-permute-start.8
  53.3 7.3 collective-permute-start.9
  60.6 9.4 %collective-permute-start.10 = (f32[1,8,18,1]{3,2,1,0:T(8,128)S(1)}, f32[1,8,18,1]{3,2,1,0:T(8,128)S(1)}, u32[]{:S(2)}, u32[]{:S(2)}) collective-permute-start(f32[1,8,18,1]{3,2,1,0:T(8,128)S(1)} %get-tuple-element.30), channel_id=1, source_target_pairs={{0,1},{1,2},{2,3},{3,4},{4,5},{5,6},{6,7},{7,8},{8,9},{9,10},{10,1... | collective-permute-start | bytes 1736 | tf_op jit(solution)/shard_map/ppermute | solution.py:46
  62.6 9.0 %collective-permute-start.11 = (f32[1,8,18,1]{3,2,1,0:T(8,128)S(1)}, f32[1,8,18,1]{3,2,1,0:T(8,128)S(1)}, u32[]{:S(2)}, u32[]{:S(2)}) collective-permute-start(f32[1,8,18,1]{3,2,1,0:T(8,128)S(1)} %get-tuple-element.31), channel_id=1, source_target_pairs={{1,0},{2,1},{3,2},{4,3},{5,4},{6,5},{7,6},{8,7},{9,8},{10,9},{11,1... | collective-permute-start | bytes 1736 | tf_op jit(solution)/shard_map/ppermute | solution.py:47
  284.5 3.1 collective-permute-start.12
  286.8 3.0 collective-permute-start.13
  289.9 10.0 %collective-permute-start.14 = (f32[1,8,18,1]{3,2,1,0:T(8,128)S(1)}, f32[1,8,18,1]{3,2,1,0:T(8,128)S(1)}, u32[]{:S(2)}, u32[]{:S(2)}) collective-permute-start(f32[1,8,18,1]{3,2,1,0:T(8,128)S(1)} %get-tuple-element.28), channel_id=1, source_target_pairs={{0,1},{1,2},{2,3},{3,4},{4,5},{5,6},{6,7},{7,8},{8,9},{9,10},{10,1... | collective-permute-start | bytes 1736 | tf_op jit(solution)/shard_map/ppermute | solution.py:46
  292.2 8.7 collective-permute-start.15
  508.6 2.2 collective-permute-start.16
  510.1 3.1 collective-permute-start.17
  513.3 9.1 %collective-permute-start.18 = (f32[1,8,18,1]{3,2,1,0:T(8,128)S(1)}, f32[1,8,18,1]{3,2,1,0:T(8,128)S(1)}, u32[]{:S(2)}, u32[]{:S(2)}) collective-permute-start(f32[1,8,18,1]{3,2,1,0:T(8,128)S(1)} %get-tuple-element.26), channel_id=1, source_target_pairs={{0,1},{1,2},{2,3},{3,4},{4,5},{5,6},{6,7},{7,8},{8,9},{9,10},{10,1... | collective-permute-start | bytes 1736 | tf_op jit(solution)/shard_map/ppermute | solution.py:46
  515.6 7.9 collective-permute-start.19
  731.9 3.1 collective-permute-start.20
  734.3 3.0 collective-permute-start.21
  737.4 10.0 %collective-permute-start.22 = (f32[1,8,18,1]{3,2,1,0:T(8,128)S(1)}, f32[1,8,18,1]{3,2,1,0:T(8,128)S(1)}, u32[]{:S(2)}, u32[]{:S(2)}) collective-permute-start(f32[1,8,18,1]{3,2,1,0:T(8,128)S(1)} %get-tuple-element.24), channel_id=1, source_target_pairs={{0,1},{1,2},{2,3},{3,4},{4,5},{5,6},{6,7},{7,8},{8,9},{9,10},{10,1... | collective-permute-start | bytes 1736 | tf_op jit(solution)/shard_map/ppermute | solution.py:46
  739.9 8.4 collective-permute-start.23
  853.4 0.6 copy-start.4
  854.3 3.5 collective-permute-start.24
  857.0 3.1 collective-permute-start.25
  860.3 14.0 %collective-permute-start.26 = (f32[3,8,18,1]{3,2,1,0:T(8,128)S(1)}, f32[3,8,18,1]{3,2,1,0:T(8,128)S(1)}, u32[]{:S(2)}, u32[]{:S(2)}) collective-permute-start(f32[3,8,18,1]{3,2,1,0:T(8,128)S(1)} %get-tuple-element.13), channel_id=1, source_target_pairs={{0,1},{1,2},{2,3},{3,4},{4,5},{5,6},{6,7},{7,8},{8,9},{9,10},{10,1... | collective-permute-start | bytes 5192 | tf_op jit(solution)/shard_map/ppermute | solution.py:46
  862.2 13.1 %collective-permute-start.27 = (f32[3,8,18,1]{3,2,1,0:T(8,128)S(1)}, f32[3,8,18,1]{3,2,1,0:T(8,128)S(1)}, u32[]{:S(2)}, u32[]{:S(2)}) collective-permute-start(f32[3,8,18,1]{3,2,1,0:T(8,128)S(1)} %get-tuple-element.14), channel_id=1, source_target_pairs={{1,0},{2,1},{3,2},{4,3},{5,4},{6,5},{7,6},{8,7},{9,8},{10,9},{11,1... | collective-permute-start | bytes 5192 | tf_op jit(solution)/shard_map/ppermute | solution.py:47
where the time goes:
time: 879 us; the launch traced here: 877 us
  blocking collectives  714 us (81%)
  starting transfers between devices  89.1 us (10%)
  waiting for transfers between devices  33.5 us (4%)
  between operations  10.9 us (1%)
  other arithmetic  10 us (1%)
  matrix products  9.55 us (1%)
  local copies, waits for them, and re-layouts  9.23 us (1%)
    psum x3, blocking collectives, solve_pressure(): curve = lax.psum(inner(direction, image, inverse_share), ('gx', 'gy'))  310 us
    psum x3, blocking collectives, solve_pressure(): norm_next = lax.psum(inner(resid, resid, inverse_share), ('gx', 'gy'))  296 us
    psum x1, blocking collectives, solve_pressure(): lax.psum((inner(resid, resid, inverse_share), inner(direction, image, inv...  109 us
    ppermute x14, starting transfers between devices, with_halo(): after = lax.ppermute(initial, axis, down)  60.8 us
    ppermute x14, starting transfers between devices, with_halo(): before = lax.ppermute(last, axis, up)  28.4 us
    ppermute x14, waiting for transfers between devices, with_halo(): after = lax.ppermute(initial, axis, down)  18.2 us
  transfers between devices with their start and end apart: 28, of which 27 were waited for; matrix products, arithmetic and copies ran while one was open for 0% of the time, Pallas kernels for 0%

commit v1 on v0

v1 whole, which is shorter than its diff:
```python
import jax
import jax.numpy as jnp
import numpy as np
from jax import lax
from jax.experimental import pallas as pl
from jax.experimental.pallas import tpu as pltpu
from jax.sharding import PartitionSpec as P

f32 = jnp.float32
bf16 = jnp.bfloat16

node_points = np.array(
    [
        -1.0,
        -0.8717401485096066,
        -0.5917001814331423,
        -0.2092992179024789,
        0.2092992179024789,
        0.5917001814331423,
        0.8717401485096066,
        1.0,
    ]
)
node_weights = np.array(
    [
        0.03571428571428571,
        0.2107042271435061,
        0.3411226924835044,
        0.4124587946587038,
        0.4124587946587038,
        0.3411226924835044,
        0.2107042271435061,
        0.03571428571428571,
    ]
)
time_step = 0.05
viscosity = 0.02
span = 8.0
ROUNDS = 4


def derivative_table(points):
    identity = np.eye(points.shape[0])
    spacing = points[:, None] - points[None, :] + identity
    barycentric = 1.0 / np.prod(spacing, axis=1)
    matrix = barycentric[None, :] / barycentric[:, None] / spacing
    matrix = matrix * (1.0 - identity)
    return matrix - identity * np.sum(matrix, axis=1)[:, None]


deriv = derivative_table(node_points)
stiff = deriv.T @ np.diag(node_weights) @ deriv
copies = np.array([2.0, 1, 1, 1, 1, 1, 1, 2.0])
inverse_mass = 1.0 / (copies * node_weights)


def lane_matrix(matrix):
    full = np.kron(np.eye(16), matrix).T.astype(np.float32)
    high = full.astype(jnp.bfloat16)
    low = (full - high.astype(np.float32)).astype(jnp.bfloat16)
    pair = np.concatenate([high, low], axis=1)
    return np.concatenate([pair, pair], axis=0)


lane_deriv = lane_matrix(deriv)
lane_stiff = lane_matrix(stiff)


def iota(lanes, dim):
    return lax.broadcasted_iota(jnp.int32, (8, lanes), dim)


def pick(place, values):
    out = jnp.full(place.shape, float(values[0]), f32)
    for k in range(1, 8):
        out = jnp.where(place == k, float(values[k]), out)
    return out


def node_x(lanes, values):
    return pick(iota(lanes, 0), values)


def node_y(lanes, values):
    return pick(iota(lanes, 1) & 7, values)


def rim_mask(lanes):
    a = iota(lanes, 0)
    b = iota(lanes, 1) & 7
    return (a == 0) | (a == 7) | (b == 0) | (b == 7)


def row_coefs(lanes, matrix):
    return [node_x(lanes, [matrix[a, (a - r) % 8] for a in range(8)]) for r in range(8)]


def row_turns(value):
    return [value] + [pltpu.roll(value, r, axis=1) for r in range(1, 8)]


def weigh(turns, coefs):
    out = turns[0] * coefs[0]
    for r in range(1, 8):
        out = out + turns[r] * coefs[r]
    return out


def depth(planes, matrix):
    out = []
    for c in range(8):
        total = planes[0] * float(matrix[c, 0])
        for k in range(1, 8):
            total = total + planes[k] * float(matrix[c, k])
        out.append(total)
    return out


def lanes_times(value, table):
    n, _, lanes = value.shape
    blocks = [value[:, :, k * 128 : (k + 1) * 128].reshape(n * 8, 128) for k in range(lanes // 128)]
    rows = blocks[0] if len(blocks) == 1 else jnp.concatenate(blocks, axis=0)
    high = rows.astype(bf16)
    low = (rows - high.astype(f32)).astype(bf16)
    both = jnp.concatenate([high, low], axis=1)
    got = jnp.dot(both, table, preferred_element_type=f32)
    got = got[:, :128] + got[:, 128:]
    parts = [got[k * n * 8 : (k + 1) * n * 8].reshape(n, 8, 128) for k in range(lanes // 128)]
    return parts[0] if len(parts) == 1 else jnp.concatenate(parts, axis=2)


def sum_lanes(value, first, last):
    lanes = value.shape[2]
    return (
        value
        + last * pltpu.roll(value, lanes - 1, axis=2)
        + first * pltpu.roll(value, 1, axis=2)
    )


def sum_rows(before, here, after, first, last):
    return here + last * pltpu.roll(after, 7, axis=1) + first * pltpu.roll(before, 1, axis=1)


def own_lanes(value):
    n = value.shape[0]
    lane = lax.broadcasted_iota(jnp.int32, (n, 8, 128), 2)
    mixed = jnp.where(lane >= 64, value[:, :, :128], value[:, :, 128:])
    return pltpu.roll(mixed, 64, axis=2)


def expand_walls(faces_ref):
    spread = (
        lax.broadcasted_iota(jnp.int32, (16, 128), 1) // 8
        == lax.broadcasted_iota(jnp.int32, (16, 128), 0)
    ).astype(f32)
    out = []
    for face in range(2):
        rows = faces_ref[face].astype(f32)
        wide = jnp.dot(rows, spread, preferred_element_type=f32)
        out.append(wide)
    return out


def rhs_kernel(adj_ref, flow_ref, faces_ref, dy_ref, ky_ref, r_ref, up_ref, down_ref, wall_ref):
    lanes = 128
    for face, wide in enumerate(expand_walls(faces_ref)):
        for e in range(2):
            wall_ref[face, e] = jnp.broadcast_to(wide[e : e + 1], (8, lanes))
    dcoef = row_coefs(lanes, deriv)
    kcoef = row_coefs(lanes, stiff)
    wx = node_x(lanes, node_weights)
    wy = node_y(lanes, node_weights)
    wxy = wx * wy
    rim = rim_mask(lanes)
    half = iota(lanes, 1) < 64

    def body(e, carry):
        v = [adj_ref[c, :, e] for c in range(3)]
        u = [flow_ref[c, :, e].astype(f32) for c in range(3)]
        vall = jnp.concatenate(v, axis=0)
        uall = jnp.concatenate(u, axis=0)
        vdy = lanes_times(vall, dy_ref[...])
        vky = lanes_times(vall, ky_ref[...])
        udy = lanes_times(uall, dy_ref[...])
        stretch_x = jnp.zeros((8, 8, lanes), f32)
        stretch_y = jnp.zeros((8, 8, lanes), f32)
        stretch_z = jnp.zeros((8, 8, lanes), f32)
        for j in range(3):
            stretch_x = stretch_x + v[j] * weigh(row_turns(u[j]), dcoef)
            stretch_y = stretch_y + v[j] * udy[8 * j : 8 * j + 8]
            stretch_z = stretch_z + v[j] * jnp.stack(depth([u[j][z] for z in range(8)], deriv))
        stretch = [stretch_x, stretch_y, stretch_z]
        for i in range(3):
            turns = row_turns(v[i])
            planes = [v[i][z] for z in range(8)]
            zd = depth(planes, deriv)
            zk = depth(planes, stiff)
            xd = weigh(turns, dcoef)
            xk = weigh(turns, kcoef)
            made = []
            for z in range(8):
                wz = float(node_weights[z])
                adv = (
                    u[0][z] * xd[z]
                    + u[1][z] * vdy[8 * i + z]
                    + u[2][z] * zd[z]
                    - stretch[i][z]
                )
                bend = wy * (wz * xk[z]) + wx * (wz * vky[8 * i + z]) + wxy * zk[z]
                out = (wxy * wz) * (v[i][z] + time_step * adv) - (time_step * viscosity) * bend
                if i == 0 and z in (0, 7):
                    out = jnp.where(rim, wall_ref[z // 7, e], out)
                r_ref[i, z, e] = out
                made.append(out)
            for z in range(4):
                up_ref[i, z, e] = jnp.where(half, pltpu.roll(made[z], 64, axis=1), made[z + 4])
                down_ref[i, z, e] = jnp.where(half, made[z], pltpu.roll(made[z + 4], 64, axis=1))
        return carry

    lax.fori_loop(0, 2, body, 0)


def join_kernel(r_ref, left_ref, right_ref, e_ref):
    half = iota(128, 1) < 64

    def body(e, carry):
        for c in range(3):
            for z in range(8):
                turned = pltpu.roll(r_ref[c, z, e], 64, axis=1)
                left = left_ref[c, z % 4, e]
                right = right_ref[c, z % 4, e]
                if z >= 4:
                    left = pltpu.roll(left, 64, axis=1)
                else:
                    right = pltpu.roll(right, 64, axis=1)
                e_ref[c, z, e, :, 0:128] = jnp.where(half, left, turned)
                e_ref[c, z, e, :, 128:256] = jnp.where(half, turned, right)
        return carry

    lax.fori_loop(0, 2, body, 0)


def source_kernel(left_ref, mid_ref, right_ref, dy_ref, b_ref, w_ref, all_ref, s_ref):
    lanes = 256
    for part, ref in enumerate((left_ref, mid_ref, right_ref)):
        for k in range(2):
            all_ref[:, :, 2 * part + k] = ref[:, :, k]
    dcoef = row_coefs(lanes, deriv)
    wxy = node_x(lanes, node_weights) * node_y(lanes, node_weights)
    inv = node_x(lanes, inverse_mass) * node_y(lanes, inverse_mass)
    first_x = (iota(lanes, 0) == 0).astype(f32)
    last_x = (iota(lanes, 0) == 7).astype(f32)
    first_y = ((iota(lanes, 1) & 7) == 0).astype(f32)
    last_y = ((iota(lanes, 1) & 7) == 7).astype(f32)
    inside = 1.0 - rim_mask(lanes).astype(f32)

    def wall(z, e):
        return jnp.broadcast_to(all_ref[0, z, e, 0:1, :], (8, lanes))

    def body(e, carry):
        w = []
        for c in range(3):
            rows = sum_rows(all_ref[c, :, e], all_ref[c, :, e + 1], all_ref[c, :, e + 2], first_x, last_x)
            total = sum_lanes(rows, first_y, last_y)
            planes = []
            for z in range(8):
                got = total[z] * (inv / float(node_weights[z]))
                if z in (0, 7):
                    got = got * (inside * (1.0 - wall(z, e + 1)))
                planes.append(got)
            w.append(jnp.stack(planes))
        div = (
            weigh(row_turns(w[0]), dcoef)
            + lanes_times(w[1], dy_ref[...])
            + jnp.stack(depth([w[2][z] for z in range(8)], deriv))
        )
        for z in range(8):
            s_ref[z, e] = (wxy * float(node_weights[z])) * div[z]

        @pl.when((e == 1) | (e == 2))
        def _():
            for c in range(3):
                w_ref[c, :, e - 1] = own_lanes(w[c])

        return carry

    lax.fori_loop(0, 4, body, 0)

    def body2(e, carry):
        rows = sum_rows(s_ref[:, e], s_ref[:, e + 1], s_ref[:, e + 2], first_x, last_x)
        total = sum_lanes(rows, first_y, last_y)
        for z in range(8):
            if z in (0, 7):
                face = wall(z, e + 2)
                b_ref[z, e] = jnp.where(inside > 0.5, -total[z] * face, face)
            else:
                b_ref[z, e] = -total[z]
        return carry

    lax.fori_loop(0, 2, body2, 0)


def krylov_kernel(mine_ref, other_ref, ky_ref, v_out, m_out, v_ref, k_ref, p_ref, acc_ref):
    lanes = 256
    core = lax.axis_index("gx") % 2
    rim = rim_mask(lanes)
    for k in range(3):
        for ref, shift in ((mine_ref, core), (other_ref, 1 - core)):
            for e in range(2):
                at = 4 * k + 2 * shift + e
                for z in range(8):
                    got = ref[k, z, e]
                    if z in (0, 7):
                        face = jnp.broadcast_to(got[0:1, :], (8, lanes))
                        p_ref[z // 7, at] = jnp.where(rim, 0.0, face)
                        got = jnp.where(rim, 0.0, got)
                    v_ref[0, z, at] = got
    kcoef = row_coefs(lanes, stiff)
    wx = node_x(lanes, node_weights)
    wy = node_y(lanes, node_weights)
    wxy = wx * wy
    first_x = (iota(lanes, 0) == 0).astype(f32)
    last_x = (iota(lanes, 0) == 7).astype(f32)
    first_y = ((iota(lanes, 1) & 7) == 0).astype(f32)
    last_y = ((iota(lanes, 1) & 7) == 7).astype(f32)
    lane = iota(lanes, 1)
    own = ((lane >= 64) & (lane < 192)).astype(f32)
    share = own * node_x(lanes, 1.0 / copies) * node_y(lanes, 1.0 / copies)
    acc_ref[...] = jnp.zeros(acc_ref.shape, f32)

    def fold(value):
        total = value[0]
        for z in range(1, 8):
            total = total + value[z]
        return total[:, :128] + total[:, 128:]

    def apply(j, e):
        v = v_ref[j, :, e]
        xk = weigh(row_turns(v), kcoef)
        yk = lanes_times(v, ky_ref[...])
        zk = depth([v[z] for z in range(8)], stiff)
        for z in range(8):
            wz = float(node_weights[z])
            k_ref[z, e] = wy * (wz * xk[z]) + wx * (wz * yk[z]) + wxy * zk[z]

    slot = 0
    for j in range(ROUNDS):
        low, high = (j, 12 - j) if j < 3 else (4, 8)
        lax.fori_loop(low, high, lambda e, c, j=j: (apply(j, e), c)[1], 0)

        def gram(e, carry, j=j, slot=slot):
            image = k_ref[:, e] * own
            for i in range(j + 1):
                acc_ref[slot + i] += fold(v_ref[i, :, e] * image)
            acc_ref[10 + j] += fold(v_ref[j, :, e] * (v_ref[0, :, e] * share))
            return carry

        lax.fori_loop(4, 8, gram, 0)
        slot += j + 1
        if j < 3:

            def step(e, carry, j=j):
                rows = sum_rows(k_ref[:, e - 1], k_ref[:, e], k_ref[:, e + 1], first_x, last_x)
                total = sum_lanes(rows, first_y, last_y)
                for z in range(8):
                    image = total[z] * (1.0 / span)
                    if z in (0, 7):
                        image = image * p_ref[z // 7, e]
                    v_ref[j + 1, z, e] = image - 0.5 * v_ref[j, z, e]
                return carry

            lax.fori_loop(low + 1, high - 1, step, 0)
    at = 3 + 2 * core
    for j in range(ROUNDS):
        for e in range(4):
            v_out[j, :, e] = v_ref[j, :, at + e]
    lane = iota(128, 1)
    packed = jnp.zeros((8, 128), f32)
    for k in range(14):
        total = jnp.sum(jnp.sum(acc_ref[k], axis=0, keepdims=True), axis=1, keepdims=True)
        packed = jnp.where(lane == k, total, packed)
    for k in range(m_out.shape[0]):
        m_out[k] = packed


def final_kernel(m_ref, v_ref, w_ref, faces_ref, dy_ref, out_ref, q_ref, f_ref):
    lanes = 256
    sums = m_ref[0]
    for k in range(1, m_ref.shape[0]):
        sums = sums + m_ref[k]
    lane = iota(128, 1)

    def moment(k):
        return jnp.sum(jnp.where(lane == k, sums, 0.0), axis=1, keepdims=True)

    e = {}
    slot = 0
    for j in range(ROUNDS):
        for i in range(j + 1):
            e[j, i] = moment(slot)
            slot += 1
    g = [moment(10 + j) for j in range(ROUNDS)]
    low, diag, scaled = {}, [], {}
    for j in range(ROUNDS):
        d = e[j, j]
        for k in range(j):
            d = d - low[j, k] * scaled[j, k]
        diag.append(d)
        for i in range(j + 1, ROUNDS):
            t = e[i, j]
            for k in range(j):
                t = t - scaled[i, k] * low[j, k]
            scaled[i, j] = t
            low[i, j] = t / d
    y = []
    for j in range(ROUNDS):
        t = g[j]
        for k in range(j):
            t = t - low[j, k] * y[k]
        y.append(t)
    c = [None] * ROUNDS
    for j in reversed(range(ROUNDS)):
        t = y[j] / diag[j]
        for k in range(j + 1, ROUNDS):
            t = t - low[k, j] * c[k]
        c[j] = t
    coef = [jnp.broadcast_to(t, (8, lanes)) for t in c]

    dcoef = row_coefs(lanes, deriv)
    wxy = node_x(lanes, node_weights) * node_y(lanes, node_weights)
    inv = node_x(lanes, inverse_mass) * node_y(lanes, inverse_mass)
    first_x = (iota(lanes, 0) == 0).astype(f32)
    last_x = (iota(lanes, 0) == 7).astype(f32)
    first_y = ((iota(lanes, 1) & 7) == 0).astype(f32)
    last_y = ((iota(lanes, 1) & 7) == 7).astype(f32)

    def body(e, carry):
        q = v_ref[0, :, e] * coef[0]
        for j in range(1, ROUNDS):
            q = q + v_ref[j, :, e] * coef[j]

        @pl.when((e == 1) | (e == 2))
        def _():
            q_ref[:, e - 1] = own_lanes(q)

        slopes = [
            weigh(row_turns(q), dcoef),
            lanes_times(q, dy_ref[...]),
            jnp.stack(depth([q[z] for z in range(8)], deriv)),
        ]
        for i in range(3):
            for z in range(8):
                f_ref[i, z, e] = (wxy * float(node_weights[z])) * slopes[i][z]
        return carry

    lax.fori_loop(0, 4, body, 0)
    inside = 1.0 - rim_mask(128).astype(f32)
    walls = expand_walls(faces_ref)
    for e in range(2):
        for i in range(3):
            rows = sum_rows(f_ref[i, :, e], f_ref[i, :, e + 1], f_ref[i, :, e + 2], first_x, last_x)
            total = own_lanes(sum_lanes(rows, first_y, last_y) * inv)
            for z in range(8):
                got = w_ref[i, z, e] - total[z] * float(1.0 / node_weights[z])
                if z in (0, 7):
                    face = jnp.broadcast_to(walls[z // 7][e : e + 1], (8, 128))
                    got = got * (inside * (1.0 - face))
                out_ref[i, z, e] = got


def shape(*dims):
    return jax.ShapeDtypeStruct(dims, f32)


def call(kernel, out_shape, scratch, *args):
    return pl.pallas_call(
        kernel,
        out_shape=out_shape,
        in_specs=[pl.BlockSpec(memory_space=pltpu.VMEM)] * len(args),
        out_specs=jax.tree.map(lambda s: pl.BlockSpec(memory_space=pltpu.VMEM), out_shape),
        scratch_shapes=scratch,
        compiler_params=pltpu.CompilerParams(vmem_limit_bytes=48 * 2**20),
    )(*args)


def shift(value, axis, by):
    size = lax.axis_size(axis)
    return lax.ppermute(value, axis, [(i, (i + by) % size) for i in range(size)])


def spread_sum(value, axis, groups):
    return lax.all_to_all(value, axis, 0, 0, axis_index_groups=groups, tiled=True)


def local(adjoint, checkpoints, wall_faces):
    nx, ny = lax.axis_size("gx"), lax.axis_size("gy")
    dy = jnp.asarray(lane_deriv)
    ky = jnp.asarray(lane_stiff)
    adj = adjoint.reshape(3, 8, 2, 8, 128)
    flow = checkpoints.reshape(3, 8, 2, 8, 128)
    vm = pltpu.VMEM
    rhs, up, down = call(
        rhs_kernel,
        (shape(3, 8, 2, 8, 128), shape(3, 4, 2, 8, 128), shape(3, 4, 2, 8, 128)),
        [vm((2, 2, 8, 128), f32)],
        adj, flow, wall_faces, dy, ky,
    )
    left = shift(up, "gy", 1)
    right = shift(down, "gy", -1)
    wide = call(join_kernel, shape(3, 8, 2, 8, 256), [], rhs, left, right)
    before = shift(wide, "gx", 1)
    after = shift(wide, "gx", -1)
    source, moved = call(
        source_kernel,
        (shape(8, 2, 8, 256), shape(3, 8, 2, 8, 128)),
        [vm((3, 8, 6, 8, 256), f32), vm((8, 4, 8, 256), f32)],
        before, wide, after, dy,
    )
    lower = shift(source, "gx", 2)
    upper = shift(source, "gx", -2)
    mine = jnp.stack([lower, source, upper])
    other = lax.ppermute(mine, "gx", [(i, i ^ 1) for i in range(nx)])
    basis, sums = call(
        krylov_kernel,
        (shape(4, 8, 4, 8, 256), shape(nx // 2, 8, 128)),
        [
            vm((4, 8, 12, 8, 256), f32),
            vm((8, 12, 8, 256), f32),
            vm((2, 12, 8, 256), f32),
            vm((14, 8, 128), f32),
        ],
        mine, other, ky,
    )
    along = [[2 * z + c for z in range(nx // 2)] for c in range(2)]
    sums = jnp.sum(spread_sum(sums, "gx", along), axis=0, keepdims=True)
    sums = spread_sum(jnp.broadcast_to(sums, (ny, 8, 128)), "gy", None)
    velocity, pressure = call(
        final_kernel,
        (shape(3, 8, 2, 8, 128), shape(8, 2, 8, 128)),
        [vm((3, 8, 4, 8, 256), f32)],
        sums, basis, moved, wall_faces, dy,
    )
    return velocity.reshape(3, 8, 16, 128), pressure.reshape(8, 16, 128)


def solution(mesh):
    return jax.shard_map(
        local,
        mesh=mesh,
        in_specs=(P(None, None, "gx", "gy"), P(None, None, None, "gx", "gy"), P(None, "gx", "gy")),
        out_specs=(P(None, None, "gx", "gy"), P(None, "gx", "gy")),
        check_vma=False,
    )
```

time: 879 us -> 96.4 us (0.11)
  blocking collectives: 714 us -> 31.6 us
  starting transfers between devices: 89.1 us -> 30 us
  waiting for transfers between devices: 33.5 us -> 13.1 us
  Pallas kernels: 0 us -> 15.1 us
  between operations: 10.9 us -> 0.73 us
  other arithmetic: 10 us -> 0.04 us
  matrix products: 9.55 us -> 0 us
    psum x7 -> x0, blocking collectives: 714 us -> none  [the longest x3 310 us: solve_pressure(): curve = lax.psum(inner(direction, image, inverse_share), ('gx', 'gy'))]
    ppermute x28 -> x7, starting transfers between devices: 89.1 us -> 30 us  [the longest x6 26.3 us: shift(): lax.ppermute(value, axis, [(i, (i + by) % size) for i in range(size)])]
    all_to_all x0 -> x2, blocking collectives: none -> 31.6 us  [spread_sum(): lax.all_to_all(value, axis, 0, 0, axis_index_groups=groups, tiled=True)]
    ppermute x28 -> x7, waiting for transfers between devices: 33.5 us -> 13.1 us  [the longest x6 11.8 us: shift(): lax.ppermute(value, axis, [(i, (i + by) % size) for i in range(size)])]
    pallas_call x0 -> x5, Pallas kernels: none -> 15.1 us  [call(): pl.pallas_call(kernel, out_shape=out_shape, in_specs=[pl.BlockSpec(memory...]
    dot_general x39 -> x0, matrix products: 9.55 us -> none  [the longest x13 3.76 us: along_rows(): return jnp.einsum('xk,czky->czxy', blocked, nodal, precision=highest)]
  transfers between devices with their start and end apart: 28 -> 7, of which waited for: 27 -> 7; matrix products, arithmetic and copies ran while one was open for 0% -> 0% of each run, Pallas kernels for 0% -> 0%
where the time goes in v1:
time: 96.4 us; the launch traced here: 95 us
  blocking collectives  31.6 us (33%)
  starting transfers between devices  30 us (31%)
  Pallas kernels  15.1 us (16%)
  waiting for transfers between devices  13.1 us (14%)
  local copies, waits for them, and re-layouts  4.32 us (4%)
    all_to_all x2, blocking collectives, spread_sum(): lax.all_to_all(value, axis, 0, 0, axis_index_groups=groups, tiled=True)  31.6 us
    ppermute x6, starting transfers between devices, shift(): lax.ppermute(value, axis, [(i, (i + by) % size) for i in range(size)])  26.3 us
    pallas_call x5, Pallas kernels, call(): pl.pallas_call(kernel, out_shape=out_shape, in_specs=[pl.BlockSpec(memory...  15.1 us
    ppermute x6, waiting for transfers between devices, shift(): lax.ppermute(value, axis, [(i, (i + by) % size) for i in range(size)])  11.8 us
    unnamed x14, local copies, waits for them, and re-layouts  4.31 us
    ppermute x1, starting transfers between devices, local(): other = lax.ppermute(mine, 'gx', [(i, i ^ 1) for i in range(nx)])  3.67 us
  transfers between devices with their start and end apart: 7, of which 7 were waited for; matrix products, arithmetic and copies ran while one was open for 0% of the time, Pallas kernels for 0%

profile of v1, /device:TPU:1, one launch (start us, length us, event | category | flops | bytes accessed | tf_op | source)
XLA Modules:
  0.0 95.0 jit_solution(6561981792096057753)
XLA Ops:
  0.6 0.0 copy-start.6
  0.6 0.7 copy-done.6
  1.3 0.0 copy-start
  1.3 0.9 copy-done
  2.2 0.0 copy-start.2
  2.2 0.9 copy-done.2
  3.1 0.0 copy-start.4
  3.1 0.9 copy-done.4
  4.0 0.0 copy-start.5
  4.1 0.9 copy-done.5
  4.9 1.4 %shard_map.68 = (f32[3,8,2,8,128]{4,3,2,1,0:T(8,128)S(1)}, f32[3,4,2,8,128]{4,3,2,1,0:T(8,128)S(1)}, f32[3,4,2,8,128]{4,3,2,1,0:T(8,128)S(1)}) custom-call(f32[3,8,2,8,128]{4,3,2,1,0:T(8,128)S(1)} %bitcast.7, bf16[3,8,2,8,128]{4,3,2,1,0:T(8,128)(2,1)S(1)} %bitcast.9, s32[2,2,16]{2,1,0:T(2,128)S(1)} %copy-done.6, bf16[256,256]{1,0:T(8,128)(2,1)S(1)} %copy-done, ...), custom_call_target="tpu_custom_call" | custom-call | tf_op jit(solution)/shard_map/pallas_call | solution.py:477
  6.3 4.0 %collective-permute-start = (f32[3,4,2,8,128]{4,3,2,1,0:T(8,128)S(1)}, f32[3,4,2,8,128]{4,3,2,1,0:T(8,128)S(1)}, u32[]{:S(2)}, u32[]{:S(2)}) collective-permute-start(f32[3,4,2,8,128]{4,3,2,1,0:T(8,128)S(1)} %get-tuple-element.12), channel_id=1, source_target_pairs={{0,1},{1,2},{2,3},{3,4},{4,5},{5,6},{6,7},{7,8},{8,9},{9,10},{10,1... | collective-permute-start | bytes 294920 | tf_op jit(solution)/shard_map/ppermute | solution.py:489
  10.4 5.5 %collective-permute-start.1 = (f32[3,4,2,8,128]{4,3,2,1,0:T(8,128)S(1)}, f32[3,4,2,8,128]{4,3,2,1,0:T(8,128)S(1)}, u32[]{:S(2)}, u32[]{:S(2)}) collective-permute-start(f32[3,4,2,8,128]{4,3,2,1,0:T(8,128)S(1)} %get-tuple-element.13), channel_id=1, source_target_pairs={{0,15},{1,0},{2,1},{3,2},{4,3},{5,4},{6,5},{7,6},{8,7},{9,8},{10,9... | collective-permute-start | bytes 294920 | tf_op jit(solution)/shard_map/ppermute | solution.py:489
  15.9 0.1 collective-permute-done.left_ref
  16.0 1.6 %collective-permute-done.1.right_ref = f32[3,4,2,8,128]{4,3,2,1,0:T(8,128)S(1)} collective-permute-done((f32[3,4,2,8,128]{4,3,2,1,0:T(8,128)S(1)}, f32[3,4,2,8,128]{4,3,2,1,0:T(8,128)S(1)}, u32[]{:S(2)}, u32[]{:S(2)}) %collective-permute-start.1) | collective-permute-done | bytes 98336 | tf_op jit(solution)/shard_map/ppermute | solution.py:489
  17.5 0.0 copy-start.1
  17.5 0.2 shard_map.69.mid_ref
  17.8 7.0 %collective-permute-start.3 = (f32[3,8,2,8,256]{4,3,2,1,0:T(8,128)S(1)}, f32[3,8,2,8,256]{4,3,2,1,0:T(8,128)S(1)}, u32[]{:S(2)}, u32[]{:S(2)}) collective-permute-start(f32[3,8,2,8,256]{4,3,2,1,0:T(8,128)S(1)} %shard_map.69.mid_ref), channel_id=1, source_target_pairs={{0,496},{16,0},{32,16},{48,32},{64,48},{80,64},{96,80},{112,96},{1... | collective-permute-start | bytes 1179656 | tf_op jit(solution)/shard_map/ppermute | solution.py:489
  24.8 0.0 collective-permute-start.2
  24.8 1.6 %collective-permute-done.3.right_ref = f32[3,8,2,8,256]{4,3,2,1,0:T(8,128)S(1)} collective-permute-done((f32[3,8,2,8,256]{4,3,2,1,0:T(8,128)S(1)}, f32[3,8,2,8,256]{4,3,2,1,0:T(8,128)S(1)}, u32[]{:S(2)}, u32[]{:S(2)}) %collective-permute-start.3) | collective-permute-done | bytes 393248 | tf_op jit(solution)/shard_map/ppermute | solution.py:489
  26.4 3.1 %collective-permute-done.2.left_ref = f32[3,8,2,8,256]{4,3,2,1,0:T(8,128)S(1)} collective-permute-done((f32[3,8,2,8,256]{4,3,2,1,0:T(8,128)S(1)}, f32[3,8,2,8,256]{4,3,2,1,0:T(8,128)S(1)}, u32[]{:S(2)}, u32[]{:S(2)}) %collective-permute-start.2) | collective-permute-done | bytes 393248 | tf_op jit(solution)/shard_map/ppermute | solution.py:489
  29.5 0.0 copy-done.1
  29.5 1.6 %shard_map.70 = (f32[8,2,8,256]{3,2,1,0:T(8,128)S(1)}, f32[3,8,2,8,128]{4,3,2,1,0:T(8,128)S(1)}) custom-call(f32[3,8,2,8,256]{4,3,2,1,0:T(8,128)S(1)} %collective-permute-done.2.left_ref, f32[3,8,2,8,256]{4,3,2,1,0:T(8,128)S(1)} %shard_map.69.mid_ref, f32[3,8,2,8,256]{4,3,2,1,0:T(8,128)S(1)} %collective-permute-done.3.right_ref, bf16[256,256]{1,0:T(8,128)(2,1)S(1)} %copy-done.1), custom_call_target="tpu_custom_call" | custom-call | tf_op jit(solution)/shard_map/pallas_call | solution.py:477
  31.1 7.8 %collective-permute-start.5 = (f32[8,2,8,256]{3,2,1,0:T(8,128)S(1)}, f32[8,2,8,256]{3,2,1,0:T(8,128)S(1)}, u32[]{:S(2)}, u32[]{:S(2)}) collective-permute-start(f32[8,2,8,256]{3,2,1,0:T(8,128)S(1)} %get-tuple-element.14), channel_id=1, source_target_pairs={{0,480},{16,496},{32,0},{48,16},{64,32},{80,48},{96,64},{112,80},{... | collective-permute-start | bytes 393224 | tf_op jit(solution)/shard_map/ppermute | solution.py:489
  38.9 1.9 %collective-permute-start.4 = (f32[8,2,8,256]{3,2,1,0:T(8,128)S(1)}, f32[8,2,8,256]{3,2,1,0:T(8,128)S(1)}, u32[]{:S(2)}, u32[]{:S(2)}) collective-permute-start(f32[8,2,8,256]{3,2,1,0:T(8,128)S(1)} %get-tuple-element.14), channel_id=1, source_target_pairs={{0,32},{16,48},{32,64},{48,80},{64,96},{80,112},{96,128},{112,144}... | collective-permute-start | bytes 393224 | tf_op jit(solution)/shard_map/ppermute | solution.py:489
  40.8 0.5 collective-permute-done.5
  41.3 5.0 %collective-permute-done.4 = f32[8,2,8,256]{3,2,1,0:T(8,128)S(1)} collective-permute-done((f32[8,2,8,256]{3,2,1,0:T(8,128)S(1)}, f32[8,2,8,256]{3,2,1,0:T(8,128)S(1)}, u32[]{:S(2)}, u32[]{:S(2)}) %collective-permute-start.4) | collective-permute-done | bytes 131104 | tf_op jit(solution)/shard_map/ppermute | solution.py:489
  46.3 0.0 copy-start.3
  46.3 3.7 %collective-permute-start.6 = (f32[3,8,2,8,256]{4,3,2,1,0:T(8,128)S(1)}, f32[3,8,2,8,256]{4,3,2,1,0:T(8,128)S(1)}, u32[]{:S(2)}, u32[]{:S(2)}) collective-permute-start(f32[3,8,2,8,256]{4,3,2,1,0:T(8,128)S(1)} %pad_maximum_fusion.mine_ref), channel_id=1, source_target_pairs={{0,16},{16,0},{32,48},{48,32},{64,80},{80,64},{96,112},{112,96},{1... | collective-permute-start | bytes 1179656 | tf_op jit(solution)/shard_map/ppermute | solution.py:523
  50.0 1.3 %collective-permute-done.6.other_ref = f32[3,8,2,8,256]{4,3,2,1,0:T(8,128)S(1)} collective-permute-done((f32[3,8,2,8,256]{4,3,2,1,0:T(8,128)S(1)}, f32[3,8,2,8,256]{4,3,2,1,0:T(8,128)S(1)}, u32[]{:S(2)}, u32[]{:S(2)}) %collective-permute-start.6) | collective-permute-done | bytes 393248 | tf_op jit(solution)/shard_map/ppermute | solution.py:523
  51.3 0.0 copy-done.3
  51.3 9.6 %shard_map.71 = (f32[4,8,4,8,256]{4,3,2,1,0:T(8,128)S(1)}, f32[16,8,128]{2,1,0:T(8,128)S(1)}) custom-call(f32[3,8,2,8,256]{4,3,2,1,0:T(8,128)S(1)} %pad_maximum_fusion.mine_ref, f32[3,8,2,8,256]{4,3,2,1,0:T(8,128)S(1)} %collective-permute-done.6.other_ref, bf16[256,256]{1,0:T(8,128)(2,1)S(1)} %copy-done.3), custom_call_target="tpu_custom_call" | custom-call | tf_op jit(solution)/shard_map/pallas_call | solution.py:477
  61.0 18.5 %all_to_all.10 = f32[16,8,128]{2,1,0:T(8,128)S(1)} all-to-all(f32[16,8,128]{2,1,0:T(8,128)S(1)} %get-tuple-element.15), channel_id=1, replica_groups={{0,32,64,96,128,160,192,224,256,288,320,352,384,416,448,480},{16,48,80,..., dimensions={0} | all-to-all | bytes 131072 | tf_op jit(solution)/shard_map/all_to_all | solution.py:493
  79.5 13.2 %all_to_all.11.m_ref = f32[16,8,128]{2,1,0:T(8,128)S(1)} all-to-all(f32[16,8,128]{2,1,0:T(8,128)S(1)} %broadcast_in_dim.2), channel_id=1, replica_groups=mesh['gx'=32,'gy'=16] {'gy'}, dimensions={0} | all-to-all | bytes 131072 | tf_op jit(solution)/shard_map/all_to_all | solution.py:493
  92.6 2.3 %shard_map.72 = (f32[3,8,2,8,128]{4,3,2,1,0:T(8,128)}, f32[8,2,8,128]{3,2,1,0:T(8,128)}) custom-call(f32[16,8,128]{2,1,0:T(8,128)S(1)} %all_to_all.11.m_ref, f32[4,8,4,8,256]{4,3,2,1,0:T(8,128)S(1)} %get-tuple-element.16.v_ref, f32[3,8,2,8,128]{4,3,2,1,0:T(8,128)S(1)} %get-tuple-element.17.w_ref, s32[2,2,16]{2,1,0:T(2,128)S(1)} %copy-done.6, ...), custom_call_target="tpu_custom_call" | custom-call | tf_op jit(solution)/shard_map/pallas_call | solution.py:477
  (3 shorter events, 0.1 us)
Async XLA Ops:
  0.6 0.7 copy-start.6
  1.3 0.9 copy-start
  2.2 0.9 copy-start.2
  3.1 0.9 copy-start.4
  4.0 0.9 copy-start.5
  6.3 9.7 %collective-permute-start = (f32[3,4,2,8,128]{4,3,2,1,0:T(8,128)S(1)}, f32[3,4,2,8,128]{4,3,2,1,0:T(8,128)S(1)}, u32[]{:S(2)}, u32[]{:S(2)}) collective-permute-start(f32[3,4,2,8,128]{4,3,2,1,0:T(8,128)S(1)} %get-tuple-element.12), channel_id=1, source_target_pairs={{0,1},{1,2},{2,3},{3,4},{4,5},{5,6},{6,7},{7,8},{8,9},{9,10},{10,1... | collective-permute-start | bytes 294920 | tf_op jit(solution)/shard_map/ppermute | solution.py:489
  10.4 7.2 %collective-permute-start.1 = (f32[3,4,2,8,128]{4,3,2,1,0:T(8,128)S(1)}, f32[3,4,2,8,128]{4,3,2,1,0:T(8,128)S(1)}, u32[]{:S(2)}, u32[]{:S(2)}) collective-permute-start(f32[3,4,2,8,128]{4,3,2,1,0:T(8,128)S(1)} %get-tuple-element.13), channel_id=1, source_target_pairs={{0,15},{1,0},{2,1},{3,2},{4,3},{5,4},{6,5},{7,6},{8,7},{9,8},{10,9... | collective-permute-start | bytes 294920 | tf_op jit(solution)/shard_map/ppermute | solution.py:489
  17.5 12.0 %copy-start.1 = (bf16[256,256]{1,0:T(8,128)(2,1)S(1)}, bf16[256,256]{1,0:T(8,128)(2,1)}, u32[]{:S(2)}) copy-start(bf16[256,256]{1,0:T(8,128)(2,1)} %constant.6.clone.dy_ref) | copy-start | bytes 393220
  17.8 8.7 %collective-permute-start.3 = (f32[3,8,2,8,256]{4,3,2,1,0:T(8,128)S(1)}, f32[3,8,2,8,256]{4,3,2,1,0:T(8,128)S(1)}, u32[]{:S(2)}, u32[]{:S(2)}) collective-permute-start(f32[3,8,2,8,256]{4,3,2,1,0:T(8,128)S(1)} %shard_map.69.mid_ref), channel_id=1, source_target_pairs={{0,496},{16,0},{32,16},{48,32},{64,48},{80,64},{96,80},{112,96},{1... | collective-permute-start | bytes 1179656 | tf_op jit(solution)/shard_map/ppermute | solution.py:489
  24.8 4.7 %collective-permute-start.2 = (f32[3,8,2,8,256]{4,3,2,1,0:T(8,128)S(1)}, f32[3,8,2,8,256]{4,3,2,1,0:T(8,128)S(1)}, u32[]{:S(2)}, u32[]{:S(2)}) collective-permute-start(f32[3,8,2,8,256]{4,3,2,1,0:T(8,128)S(1)} %shard_map.69.mid_ref), channel_id=1, source_target_pairs={{0,16},{16,32},{32,48},{48,64},{64,80},{80,96},{96,112},{112,128},... | collective-permute-start | bytes 1179656 | tf_op jit(solution)/shard_map/ppermute | solution.py:489
  31.1 10.2 %collective-permute-start.5 = (f32[8,2,8,256]{3,2,1,0:T(8,128)S(1)}, f32[8,2,8,256]{3,2,1,0:T(8,128)S(1)}, u32[]{:S(2)}, u32[]{:S(2)}) collective-permute-start(f32[8,2,8,256]{3,2,1,0:T(8,128)S(1)} %get-tuple-element.14), channel_id=1, source_target_pairs={{0,480},{16,496},{32,0},{48,16},{64,32},{80,48},{96,64},{112,80},{... | collective-permute-start | bytes 393224 | tf_op jit(solution)/shard_map/ppermute | solution.py:489
  38.9 7.4 %collective-permute-start.4 = (f32[8,2,8,256]{3,2,1,0:T(8,128)S(1)}, f32[8,2,8,256]{3,2,1,0:T(8,128)S(1)}, u32[]{:S(2)}, u32[]{:S(2)}) collective-permute-start(f32[8,2,8,256]{3,2,1,0:T(8,128)S(1)} %get-tuple-element.14), channel_id=1, source_target_pairs={{0,32},{16,48},{32,64},{48,80},{64,96},{80,112},{96,128},{112,144}... | collective-permute-start | bytes 393224 | tf_op jit(solution)/shard_map/ppermute | solution.py:489
  46.3 5.0 %copy-start.3 = (bf16[256,256]{1,0:T(8,128)(2,1)S(1)}, bf16[256,256]{1,0:T(8,128)(2,1)}, u32[]{:S(2)}) copy-start(bf16[256,256]{1,0:T(8,128)(2,1)} %constant.7.clone.ky_ref) | copy-start | bytes 393220
  46.3 5.0 %collective-permute-start.6 = (f32[3,8,2,8,256]{4,3,2,1,0:T(8,128)S(1)}, f32[3,8,2,8,256]{4,3,2,1,0:T(8,128)S(1)}, u32[]{:S(2)}, u32[]{:S(2)}) collective-permute-start(f32[3,8,2,8,256]{4,3,2,1,0:T(8,128)S(1)} %pad_maximum_fusion.mine_ref), channel_id=1, source_target_pairs={{0,16},{16,0},{32,48},{48,32},{64,80},{80,64},{96,112},{112,96},{1... | collective-permute-start | bytes 1179656 | tf_op jit(solution)/shard_map/ppermute | solution.py:523

commit v2 on v1

v2 whole, which is shorter than its diff:
```python
import jax
import jax.numpy as jnp
import numpy as np
from jax import lax
from jax.experimental import pallas as pl
from jax.experimental.pallas import tpu as pltpu
from jax.sharding import PartitionSpec as P

f32 = jnp.float32
bf16 = jnp.bfloat16

node_points = np.array(
    [
        -1.0,
        -0.8717401485096066,
        -0.5917001814331423,
        -0.2092992179024789,
        0.2092992179024789,
        0.5917001814331423,
        0.8717401485096066,
        1.0,
    ]
)
node_weights = np.array(
    [
        0.03571428571428571,
        0.2107042271435061,
        0.3411226924835044,
        0.4124587946587038,
        0.4124587946587038,
        0.3411226924835044,
        0.2107042271435061,
        0.03571428571428571,
    ]
)
time_step = 0.05
viscosity = 0.02
span = 8.0
ROUNDS = 4


def derivative_table(points):
    identity = np.eye(points.shape[0])
    spacing = points[:, None] - points[None, :] + identity
    barycentric = 1.0 / np.prod(spacing, axis=1)
    matrix = barycentric[None, :] / barycentric[:, None] / spacing
    matrix = matrix * (1.0 - identity)
    return matrix - identity * np.sum(matrix, axis=1)[:, None]


deriv = derivative_table(node_points)
stiff = deriv.T @ np.diag(node_weights) @ deriv
copies = np.array([2.0, 1, 1, 1, 1, 1, 1, 2.0])
inverse_mass = 1.0 / (copies * node_weights)


scaled_stiff = stiff / node_weights[:, None]


def iota(lanes, dim):
    return lax.broadcasted_iota(jnp.int32, (8, lanes), dim)


def pick(place, values):
    out = jnp.full(place.shape, float(values[0]), f32)
    for k in range(1, 8):
        out = jnp.where(place == k, float(values[k]), out)
    return out


def node_x(lanes, values):
    return pick(iota(lanes, 0), values)


def node_y(lanes, values):
    return pick(iota(lanes, 1) & 7, values)


def rim_mask(lanes):
    a = iota(lanes, 0)
    b = iota(lanes, 1) & 7
    return (a == 0) | (a == 7) | (b == 0) | (b == 7)


def row_coefs(lanes, matrix):
    return [node_x(lanes, [matrix[a, (a - r) % 8] for a in range(8)]) for r in range(8)]


def row_turns(value):
    return [value] + [pltpu.roll(value, r, axis=1) for r in range(1, 8)]


def weigh(turns, coefs):
    out = turns[0] * coefs[0]
    for r in range(1, 8):
        out = out + turns[r] * coefs[r]
    return out


def depth(planes, matrix, sign):
    plus = [planes[k] + planes[7 - k] for k in range(4)]
    minus = [planes[k] - planes[7 - k] for k in range(4)]
    out = [None] * 8
    for a in range(4):
        even = plus[0] * float(0.5 * (matrix[a, 0] + matrix[a, 7]))
        odd = minus[0] * float(0.5 * (matrix[a, 0] - matrix[a, 7]))
        for k in range(1, 4):
            even = even + plus[k] * float(0.5 * (matrix[a, k] + matrix[a, 7 - k]))
            odd = odd + minus[k] * float(0.5 * (matrix[a, k] - matrix[a, 7 - k]))
        out[a] = even + odd
        out[7 - a] = even - odd if sign > 0 else odd - even
    return out


def z_slope(value):
    return jnp.stack(depth([value[z] for z in range(8)], deriv, -1))


def lane_table(matrix):
    lane = iota(128, 1)
    pattern = jnp.zeros((8, 128), f32)
    for b in range(8):
        pattern = jnp.where((lane & 7) == b, node_x(128, matrix[b]), pattern)
    full = jnp.concatenate([jnp.where(lane // 8 == k, pattern, 0.0) for k in range(16)], axis=0)
    high = full.astype(bf16)
    low = (full - high.astype(f32)).astype(bf16)
    pair = jnp.concatenate([high, low], axis=1)
    return jnp.concatenate([pair, pair], axis=0)


def lanes_times(value, table):
    n, _, lanes = value.shape
    blocks = [value[:, :, k * 128 : (k + 1) * 128].reshape(n * 8, 128) for k in range(lanes // 128)]
    rows = blocks[0] if len(blocks) == 1 else jnp.concatenate(blocks, axis=0)
    high = rows.astype(bf16)
    low = (rows - high.astype(f32)).astype(bf16)
    both = jnp.concatenate([high, low], axis=1)
    got = jnp.dot(both, table, preferred_element_type=f32)
    got = got[:, :128] + got[:, 128:]
    parts = [got[k * n * 8 : (k + 1) * n * 8].reshape(n, 8, 128) for k in range(lanes // 128)]
    return parts[0] if len(parts) == 1 else jnp.concatenate(parts, axis=2)


def sum_lanes(value, first, last):
    lanes = value.shape[2]
    return (
        value
        + last * pltpu.roll(value, lanes - 1, axis=2)
        + first * pltpu.roll(value, 1, axis=2)
    )


def sum_rows(before, here, after, first, last):
    return here + last * pltpu.roll(after, 7, axis=1) + first * pltpu.roll(before, 1, axis=1)


def own_lanes(value):
    n = value.shape[0]
    lane = lax.broadcasted_iota(jnp.int32, (n, 8, 128), 2)
    mixed = jnp.where(lane >= 64, value[:, :, :128], value[:, :, 128:])
    return pltpu.roll(mixed, 64, axis=2)


def expand_walls(faces_ref):
    spread = (
        lax.broadcasted_iota(jnp.int32, (16, 128), 1) // 8
        == lax.broadcasted_iota(jnp.int32, (16, 128), 0)
    ).astype(f32)
    out = []
    for face in range(2):
        rows = faces_ref[face].astype(f32)
        wide = jnp.dot(rows, spread, preferred_element_type=f32)
        out.append(wide)
    return out


def rhs_kernel(
    adj_hbm, flow_hbm, faces_hbm,
    r_ref, up_ref, down_ref, dy_ref, ky_ref,
    adj_ref, flow_ref, faces_ref, u_ref, wall_ref, sems,
):
    moves = [
        pltpu.make_async_copy(src, dst, sems.at[k])
        for k, (src, dst) in enumerate(
            ((adj_hbm, adj_ref), (flow_hbm, flow_ref), (faces_hbm, faces_ref))
        )
    ]
    for move in moves:
        move.start()
    lanes = 128
    dy_ref[...] = lane_table(deriv)
    ky_ref[...] = lane_table(scaled_stiff)
    dcoef = row_coefs(lanes, deriv)
    kcoef = row_coefs(lanes, scaled_stiff)
    wxy = node_x(lanes, node_weights) * node_y(lanes, node_weights)
    rim = rim_mask(lanes)
    half = iota(lanes, 1) < 64
    for move in moves:
        move.wait()
    for face, wide in enumerate(expand_walls(faces_ref)):
        for e in range(2):
            wall_ref[face, e] = jnp.broadcast_to(wide[e : e + 1], (8, lanes))
    for c in range(3):
        for z in range(8):
            rows = flow_ref[c, z].astype(f32)
            u_ref[c, z, 0] = rows[:8]
            u_ref[c, z, 1] = rows[8:]

    def body(e, carry):
        v = [adj_ref[c, :, e] for c in range(3)]
        u = [u_ref[c, :, e] for c in range(3)]
        vall = jnp.concatenate(v, axis=0)
        uall = jnp.concatenate(u, axis=0)
        vdy = lanes_times(vall, dy_ref[...])
        vky = lanes_times(vall, ky_ref[...])
        udy = lanes_times(uall, dy_ref[...])
        stretch = [jnp.zeros((8, 8, lanes), f32)] * 3
        for j in range(3):
            stretch[0] = stretch[0] + v[j] * weigh(row_turns(u[j]), dcoef)
            stretch[1] = stretch[1] + v[j] * udy[8 * j : 8 * j + 8]
            stretch[2] = stretch[2] + v[j] * z_slope(u[j])
        for i in range(3):
            turns = row_turns(v[i])
            planes = [v[i][z] for z in range(8)]
            zd = depth(planes, deriv, -1)
            zk = depth(planes, scaled_stiff, 1)
            xd = weigh(turns, dcoef)
            xk = weigh(turns, kcoef)
            made = []
            for z in range(8):
                wz = float(node_weights[z])
                adv = (
                    u[0][z] * xd[z]
                    + u[1][z] * vdy[8 * i + z]
                    + u[2][z] * zd[z]
                    - stretch[i][z]
                )
                bend = xk[z] + vky[8 * i + z] + zk[z]
                out = (wxy * wz) * (v[i][z] + time_step * adv - (time_step * viscosity) * bend)
                if i == 0 and z in (0, 7):
                    out = jnp.where(rim, wall_ref[z // 7, e], out)
                r_ref[i, z, e] = out
                made.append(out)
            for z in range(4):
                up_ref[i, z, e] = jnp.where(half, pltpu.roll(made[z], 64, axis=1), made[z + 4])
                down_ref[i, z, e] = jnp.where(half, made[z], pltpu.roll(made[z + 4], 64, axis=1))
        return carry

    lax.fori_loop(0, 2, body, 0)


def join_kernel(r_ref, left_ref, right_ref, e_ref, up_ref, down_ref):
    half = iota(128, 1) < 64
    place = iota(256, 0)
    first = place == 0
    last = place == 7
    for c in range(3):
        faces_up = jnp.zeros((8, 256), f32)
        faces_down = jnp.zeros((8, 256), f32)
        for z in range(8):
            tiles = []
            for e in range(2):
                turned = pltpu.roll(r_ref[c, z, e], 64, axis=1)
                left = left_ref[c, z % 4, e]
                right = right_ref[c, z % 4, e]
                if z >= 4:
                    left = pltpu.roll(left, 64, axis=1)
                else:
                    right = pltpu.roll(right, 64, axis=1)
                tile = jnp.concatenate(
                    [jnp.where(half, left, turned), jnp.where(half, turned, right)], axis=1
                )
                e_ref[c, z, e] = tile
                tiles.append(tile)
            if c == 0:
                go_up, go_down = tiles[1], tiles[0]
                if 0 < z < 7:
                    go_up = go_up + jnp.where(first, pltpu.roll(tiles[0], 1, axis=0), 0.0)
                    go_down = go_down + jnp.where(last, pltpu.roll(tiles[1], 7, axis=0), 0.0)
                up_ref[z] = go_up
                down_ref[z] = go_down
            else:
                turned = pltpu.roll(tiles[1], (z + 1) % 8, axis=0) if z < 7 else tiles[1]
                faces_up = jnp.where(place == z, turned, faces_up)
                turned = pltpu.roll(tiles[0], z, axis=0) if z else tiles[0]
                faces_down = jnp.where(place == z, turned, faces_down)
        if c:
            up_ref[7 + c] = faces_up
            down_ref[7 + c] = faces_down


def flags(lanes):
    first_x = (iota(lanes, 0) == 0).astype(f32)
    last_x = (iota(lanes, 0) == 7).astype(f32)
    first_y = ((iota(lanes, 1) & 7) == 0).astype(f32)
    last_y = ((iota(lanes, 1) & 7) == 7).astype(f32)
    return first_x, last_x, first_y, last_y


def source_kernel(left_ref, mid_ref, right_ref, dy_ref, b_ref, w_ref, t_ref):
    lanes = 256
    dcoef = row_coefs(lanes, deriv)
    wx = node_x(lanes, node_weights)
    wy = node_y(lanes, node_weights)
    mx = node_x(lanes, copies)
    my = node_y(lanes, copies)
    inv = node_x(lanes, inverse_mass) * node_y(lanes, inverse_mass)
    first_x, last_x, first_y, last_y = flags(lanes)
    inside = 1.0 - rim_mask(lanes).astype(f32)

    def wall(tile):
        return jnp.broadcast_to(tile[0:1, :], (8, lanes))

    def finish(rows, faces):
        total = sum_lanes(rows, first_y, last_y)
        planes = []
        for z in range(8):
            got = total[z] * (inv * float(1.0 / node_weights[z]))
            if z in (0, 7):
                got = got * (inside * (1.0 - wall(faces[z])))
            planes.append(got)
        return jnp.stack(planes)

    def turn(tile, by):
        by = by % 8
        return pltpu.roll(tile, by, axis=0) if by else tile

    slope = {}
    left = left_ref[0:8]
    right = right_ref[0:8]
    near = finish(left + last_x * pltpu.roll(mid_ref[0, :, 0], 7, axis=1), left)
    slope[-1] = weigh(row_turns(near), dcoef)
    near = finish(right + first_x * pltpu.roll(mid_ref[0, :, 1], 1, axis=1), right)
    slope[2] = weigh(row_turns(near), dcoef)
    for e in range(2):
        faces = mid_ref[0, :, e]
        w = []
        for c in range(3):
            if c == 0:
                before, after = left, right
            else:
                before = jnp.stack([turn(left_ref[7 + c], 7 - z) for z in range(8)])
                after = jnp.stack([turn(right_ref[7 + c], 8 - z) for z in range(8)])
            if e == 0:
                rows = sum_rows(before, mid_ref[c, :, 0], mid_ref[c, :, 1], first_x, last_x)
            else:
                rows = sum_rows(mid_ref[c, :, 0], mid_ref[c, :, 1], after, first_x, last_x)
            got = finish(rows, faces)
            w.append(got)
            w_ref[c, :, e] = own_lanes(got)
        slope[e] = weigh(row_turns(w[0]), dcoef)
        along = sum_lanes(lanes_times(w[1], dy_ref[...]) * wy, first_y, last_y) * (mx * wx)
        t_ref[:, e] = along + z_slope(w[2]) * (mx * wx * my * wy)
    for e in range(2):
        faces = mid_ref[0, :, e]
        rows = sum_rows(slope[e - 1], slope[e], slope[e + 1], first_x, last_x)
        total = rows * (wx * my * wy) + t_ref[:, e]
        for z in range(8):
            got = total[z] * float(-node_weights[z])
            if z in (0, 7):
                face = wall(faces[z])
                got = jnp.where(inside > 0.5, got * face, face)
            b_ref[z, e] = got


def krylov_kernel(*refs):
    blocks = refs[:5]
    ky_ref, v_out, m_out, v_ref, k_ref, p_ref, acc_ref = refs[5:]
    lanes = 256
    rim = rim_mask(lanes)
    for k, ref in enumerate(blocks):
        for e in range(2):
            at = 2 * k + e
            for z in range(8):
                got = ref[z, e]
                if z in (0, 7):
                    face = jnp.broadcast_to(got[0:1, :], (8, lanes))
                    p_ref[z // 7, at] = jnp.where(rim, 0.0, face)
                    got = jnp.where(rim, 0.0, got)
                v_ref[0, z, at] = got
    kcoef = row_coefs(lanes, scaled_stiff)
    wxy = node_x(lanes, node_weights) * node_y(lanes, node_weights)
    first_x, last_x, first_y, last_y = flags(lanes)
    acc_ref[...] = jnp.zeros(acc_ref.shape, f32)

    def fold(value):
        total = value[0]
        for z in range(1, 8):
            total = total + value[z]
        return total

    def apply(j, e):
        v = v_ref[j, :, e]
        yk = lanes_times(v, ky_ref[...])
        xk = weigh(row_turns(v), kcoef)
        zk = depth([v[z] for z in range(8)], scaled_stiff, 1)
        for z in range(8):
            k_ref[z, e] = (xk[z] + zk[z] + yk[z]) * (wxy * float(node_weights[z] / span))

    slot = 0
    for j in range(ROUNDS):
        low, high = (j, 10 - j) if j < 3 else (4, 6)
        lax.fori_loop(low, high, lambda e, c, j=j: (apply(j, e), c)[1], 0, unroll=2)

        def gram(e, carry, j=j, slot=slot):
            image = k_ref[:, e]
            for i in range(j + 1):
                acc_ref[slot + i] += fold(v_ref[i, :, e] * image)
            acc_ref[10 + j] += fold(v_ref[j, :, e] * v_ref[0, :, e])
            return carry

        lax.fori_loop(4, 6, gram, 0, unroll=2)
        slot += j + 1
        if j < 3:

            def step(e, carry, j=j):
                rows = sum_rows(k_ref[:, e - 1], k_ref[:, e], k_ref[:, e + 1], first_x, last_x)
                total = sum_lanes(rows, first_y, last_y)
                for z in range(8):
                    image = total[z]
                    if z in (0, 7):
                        image = image * p_ref[z // 7, e]
                    v_ref[j + 1, z, e] = image - 0.5 * v_ref[j, z, e]
                return carry

            lax.fori_loop(low + 1, high - 1, step, 0, unroll=2)
    for j in range(ROUNDS):
        for e in range(4):
            v_out[j, :, e] = v_ref[j, :, 3 + e]
    lane = iota(lanes, 1)
    own = (lane >= 64) & (lane < 192)
    share = node_x(lanes, 1.0 / copies) * node_y(lanes, 1.0 / copies)
    lane = iota(128, 1)
    packed = jnp.zeros((8, 128), f32)
    for k in range(14):
        part = jnp.where(own, acc_ref[k], 0.0)
        if k >= 10:
            part = part * share
        part = part[:, :128] + part[:, 128:]
        total = jnp.sum(jnp.sum(part, axis=0, keepdims=True), axis=1, keepdims=True)
        packed = jnp.where(lane == k, total, packed)
    m_out[...] = packed


def final_kernel(m_ref, v_ref, w_ref, faces_ref, dy_ref, out_ref, q_ref):
    lanes = 256
    count = m_ref.shape[0] // 8
    parts = [m_ref[8 * k : 8 * k + 8] for k in range(count)]
    while len(parts) > 1:
        odd = parts[len(parts) // 2 * 2 :]
        parts = [parts[k] + parts[k + 1] for k in range(0, len(parts) - 1, 2)] + odd
    sums = jnp.broadcast_to(jnp.sum(parts[0], axis=0, keepdims=True), (8, 128))
    lane = iota(128, 1)

    def moment(k):
        return jnp.sum(jnp.where(lane == k, sums, 0.0), axis=1, keepdims=True)

    e = {}
    slot = 0
    for j in range(ROUNDS):
        for i in range(j + 1):
            e[j, i] = moment(slot)
            slot += 1
    g = [moment(10 + j) for j in range(ROUNDS)]
    low, diag, scaled = {}, [], {}
    for j in range(ROUNDS):
        d = e[j, j]
        for k in range(j):
            d = d - low[j, k] * scaled[j, k]
        diag.append(d)
        for i in range(j + 1, ROUNDS):
            t = e[i, j]
            for k in range(j):
                t = t - scaled[i, k] * low[j, k]
            scaled[i, j] = t
            low[i, j] = t / d
    y = []
    for j in range(ROUNDS):
        t = g[j]
        for k in range(j):
            t = t - low[j, k] * y[k]
        y.append(t)
    c = [None] * ROUNDS
    for j in reversed(range(ROUNDS)):
        t = y[j] / diag[j]
        for k in range(j + 1, ROUNDS):
            t = t - low[k, j] * c[k]
        c[j] = t
    coef = [jnp.broadcast_to(t * (1.0 / span), (8, lanes)) for t in c]

    dcoef = row_coefs(lanes, deriv)
    first_x, last_x, first_y, last_y = flags(lanes)
    mean_x = node_x(lanes, 1.0 / copies)
    mean_y = node_y(lanes, 1.0 / copies)
    inside = 1.0 - rim_mask(128).astype(f32)
    walls = expand_walls(faces_ref)
    q, slope = [], []
    for e in range(4):
        got = v_ref[0, :, e] * coef[0]
        for j in range(1, ROUNDS):
            got = got + v_ref[j, :, e] * coef[j]
        q.append(got)
        slope.append(weigh(row_turns(got), dcoef))
    for e in range(2):
        here = q[e + 1]
        q_own = own_lanes(here)
        q_ref[:, e] = q_own
        along_x = sum_rows(slope[e], slope[e + 1], slope[e + 2], first_x, last_x) * mean_x
        along_y = sum_lanes(lanes_times(here, dy_ref[...]), first_y, last_y) * mean_y
        parts = [own_lanes(along_x), own_lanes(along_y), z_slope(q_own)]
        for i in range(3):
            for z in range(8):
                got = w_ref[i, z, e] - parts[i][z]
                if z in (0, 7):
                    face = jnp.broadcast_to(walls[z // 7][e : e + 1], (8, 128))
                    got = got * (inside * (1.0 - face))
                out_ref[i, z, e] = got


def shape(*dims):
    return jax.ShapeDtypeStruct(dims, f32)


def call(kernel, out_shape, scratch, *args, space=pltpu.VMEM, vmem=48):
    return pl.pallas_call(
        kernel,
        out_shape=out_shape,
        in_specs=[pl.BlockSpec(memory_space=space)] * len(args),
        out_specs=jax.tree.map(lambda s: pl.BlockSpec(memory_space=pltpu.VMEM), out_shape),
        scratch_shapes=scratch,
        compiler_params=pltpu.CompilerParams(vmem_limit_bytes=vmem * 2**20),
    )(*args)


def shift(value, axis, by):
    size = lax.axis_size(axis)
    return lax.ppermute(value, axis, [(i, (i + by) % size) for i in range(size)])


def total_rows(packed):
    nx, ny = lax.axis_size("gx"), lax.axis_size("gy")
    pairs = [[i, i + 1] for i in range(0, nx, 2)]
    both = lax.all_gather(packed, "gx", axis_index_groups=pairs)
    rows = jnp.broadcast_to(both[0, :1] + both[1, :1], (nx // 2 * ny, 128))
    chips = [[(2 * z + c) * ny + y for z in range(nx // 2) for y in range(ny)] for c in range(2)]
    return lax.all_to_all(rows, ("gx", "gy"), 0, 0, axis_index_groups=chips, tiled=True)


def local(adjoint, checkpoints, wall_faces):
    adj = adjoint.reshape(3, 8, 2, 8, 128)
    flow = checkpoints.reshape(3, 8, 16, 128)
    vm = pltpu.VMEM
    table = jax.ShapeDtypeStruct((256, 256), bf16)
    strip = shape(3, 4, 2, 8, 128)
    rhs, up, down, dy, ky = call(
        rhs_kernel,
        (shape(3, 8, 2, 8, 128), strip, strip, table, table),
        [
            vm((3, 8, 2, 8, 128), f32),
            vm((3, 8, 16, 128), bf16),
            vm((2, 2, 16), jnp.int32),
            vm((3, 8, 2, 8, 128), f32),
            vm((2, 2, 8, 128), f32),
            pltpu.SemaphoreType.DMA((3,)),
        ],
        adj, flow, wall_faces,
        space=pl.ANY,
        vmem=62,
    )
    left = shift(up, "gy", 1)
    right = shift(down, "gy", -1)
    packet = shape(10, 8, 256)
    wide, up, down = call(
        join_kernel, (shape(3, 8, 2, 8, 256), packet, packet), [], rhs, left, right
    )
    before = shift(up, "gx", 1)
    after = shift(down, "gx", -1)
    source, moved = call(
        source_kernel,
        (shape(8, 2, 8, 256), shape(3, 8, 2, 8, 128)),
        [vm((8, 2, 8, 256), f32)],
        before, wide, after, dy,
    )
    left = shift(source, "gx", 1)
    right = shift(source, "gx", -1)
    left2 = shift(left, "gx", 1)
    right2 = shift(right, "gx", -1)
    basis, packed = call(
        krylov_kernel,
        (shape(4, 8, 4, 8, 256), shape(8, 128)),
        [
            vm((4, 8, 10, 8, 256), f32),
            vm((8, 10, 8, 256), f32),
            vm((2, 10, 8, 256), f32),
            vm((14, 8, 256), f32),
        ],
        left2, left, source, right, right2, ky,
    )
    velocity, pressure = call(
        final_kernel,
        (shape(3, 8, 2, 8, 128), shape(8, 2, 8, 128)),
        [],
        total_rows(packed), basis, moved, wall_faces, dy,
    )
    return velocity.reshape(3, 8, 16, 128), pressure.reshape(8, 16, 128)


def solution(mesh):
    return jax.shard_map(
        local,
        mesh=mesh,
        in_specs=(P(None, None, "gx", "gy"), P(None, None, None, "gx", "gy"), P(None, "gx", "gy")),
        out_specs=(P(None, None, "gx", "gy"), P(None, "gx", "gy")),
        check_vma=False,
    )
```

time: 96.4 us -> 87 us (0.902)
  blocking collectives: 31.6 us -> 40.5 us
  waiting for transfers between devices: 13.1 us -> 7.76 us
  Pallas kernels: 15.1 us -> 9.95 us
  starting transfers between devices: 30 us -> 25.3 us
  local copies, waits for them, and re-layouts: 4.32 us -> 1.69 us
    all_gather x0 -> x1, blocking collectives: none -> 6.25 us  [total_rows(): both = lax.all_gather(packed, 'gx', axis_index_groups=pairs)]
    pallas_call x5, Pallas kernels: 15.1 us -> 9.95 us  [call(): pl.pallas_call(kernel, out_shape=out_shape, in_specs=[pl.BlockSpec(memory...]
    ppermute x6 -> x8, waiting for transfers between devices: 11.8 us -> 7.76 us  [shift(): lax.ppermute(value, axis, [(i, (i + by) % size) for i in range(size)])]
    ppermute x1 -> x0, starting transfers between devices: 3.67 us -> none  [local(): other = lax.ppermute(mine, 'gx', [(i, i ^ 1) for i in range(nx)])]
    unnamed x14 -> x8, local copies, waits for them, and re-layouts: 4.31 us -> 1.62 us
    all_to_all x2 -> x1, blocking collectives: 31.6 us -> 34.3 us  [total_rows(): lax.all_to_all(rows, ('gx', 'gy'), 0, 0, axis_index_groups=chips, tiled=T...]
    ppermute x1 -> x0, waiting for transfers between devices: 1.33 us -> none  [local(): other = lax.ppermute(mine, 'gx', [(i, i ^ 1) for i in range(nx)])]
    ppermute x6 -> x8, starting transfers between devices: 26.3 us -> 25.3 us  [shift(): lax.ppermute(value, axis, [(i, (i + by) % size) for i in range(size)])]
  transfers between devices with their start and end apart: 7 -> 8, of which waited for: 7 -> 7; matrix products, arithmetic and copies ran while one was open for 0% -> 0% of each run, Pallas kernels for 0% -> 0%
where the time goes in v2:
time: 87 us; the launch traced here: 85.9 us
  blocking collectives  40.5 us (47%)
  starting transfers between devices  25.3 us (29%)
  Pallas kernels  9.95 us (11%)
  waiting for transfers between devices  7.76 us (9%)
  local copies, waits for them, and re-layouts  1.69 us (2%)
    all_to_all x1, blocking collectives, total_rows(): lax.all_to_all(rows, ('gx', 'gy'), 0, 0, axis_index_groups=chips, tiled=T...  34.3 us
    ppermute x8, starting transfers between devices, shift(): lax.ppermute(value, axis, [(i, (i + by) % size) for i in range(size)])  25.3 us
    pallas_call x5, Pallas kernels, call(): pl.pallas_call(kernel, out_shape=out_shape, in_specs=[pl.BlockSpec(memory...  9.95 us
    ppermute x8, waiting for transfers between devices, shift(): lax.ppermute(value, axis, [(i, (i + by) % size) for i in range(size)])  7.76 us
    all_gather x1, blocking collectives, total_rows(): both = lax.all_gather(packed, 'gx', axis_index_groups=pairs)  6.25 us
  transfers between devices with their start and end apart: 8, of which 7 were waited for; matrix products, arithmetic and copies ran while one was open for 0% of the time, Pallas kernels for 0%

profile of v2, /device:TPU:1, one launch (start us, length us, event | category | flops | bytes accessed | tf_op | source)
XLA Modules:
  0.0 85.9 jit_solution(13286701077347858322)
XLA Ops:
  0.6 2.9 %shard_map.50 = (f32[3,8,2,8,128]{4,3,2,1,0:T(8,128)}, f32[3,4,2,8,128]{4,3,2,1,0:T(8,128)}, f32[3,4,2,8,128]{4,3,2,1,0:T(8,128)}, bf16[256,256]{1,0:T(8,128)(2,1)}, bf16[256,256]{1,0:T(8,128)(2,1)}) custom-call(f32[3,8,2,8,128]{4,3,2,1,0:T(8,128)} %bitcast.9, bf16[3,8,16,128]{3,2,1,0:T(8,128)(2,1)} %bitcast.10, s32[2,2,16]{2,1,0:T(2,128)} %faces_ref.1), custom_call_target="tpu_custom_call" | custom-call | tf_op jit(solution)/shard_map/pallas_call | solution.py:525
  3.6 4.0 %collective-permute-start = (f32[3,4,2,8,128]{4,3,2,1,0:T(8,128)}, f32[3,4,2,8,128]{4,3,2,1,0:T(8,128)S(1)}, u32[]{:S(2)}, u32[]{:S(2)}) collective-permute-start(f32[3,4,2,8,128]{4,3,2,1,0:T(8,128)} %get-tuple-element.17), channel_id=1, source_target_pairs={{0,1},{1,2},{2,3},{3,4},{4,5},{5,6},{6,7},{7,8},{8,9},{9,10},{10,1... | collective-permute-start | bytes 294920 | tf_op jit(solution)/shard_map/ppermute | solution.py:537
  7.6 5.6 %collective-permute-start.1 = (f32[3,4,2,8,128]{4,3,2,1,0:T(8,128)}, f32[3,4,2,8,128]{4,3,2,1,0:T(8,128)S(1)}, u32[]{:S(2)}, u32[]{:S(2)}) collective-permute-start(f32[3,4,2,8,128]{4,3,2,1,0:T(8,128)} %get-tuple-element.18), channel_id=1, source_target_pairs={{0,15},{1,0},{2,1},{3,2},{4,3},{5,4},{6,5},{7,6},{8,7},{9,8},{10,9... | collective-permute-start | bytes 294920 | tf_op jit(solution)/shard_map/ppermute | solution.py:537
  13.2 0.3 collective-permute-done.left_ref
  13.4 1.7 %collective-permute-done.1.right_ref = f32[3,4,2,8,128]{4,3,2,1,0:T(8,128)S(1)} collective-permute-done((f32[3,4,2,8,128]{4,3,2,1,0:T(8,128)}, f32[3,4,2,8,128]{4,3,2,1,0:T(8,128)S(1)}, u32[]{:S(2)}, u32[]{:S(2)}) %collective-permute-start.1) | collective-permute-done | bytes 98336 | tf_op jit(solution)/shard_map/ppermute | solution.py:537
  15.1 0.0 copy-start.1
  15.1 0.9 %copy-done.1 = f32[3,8,2,8,128]{4,3,2,1,0:T(8,128)S(1)} copy-done((f32[3,8,2,8,128]{4,3,2,1,0:T(8,128)S(1)}, f32[3,8,2,8,128]{4,3,2,1,0:T(8,128)}, u32[]{:S(2)}) %copy-start.1) | copy-done | bytes 196632
  16.0 0.0 copy-start
  16.0 0.2 shard_map.51
  16.2 3.2 %collective-permute-start.2 = (f32[10,8,256]{2,1,0:T(8,128)S(1)}, f32[10,8,256]{2,1,0:T(8,128)S(1)}, u32[]{:S(2)}, u32[]{:S(2)}) collective-permute-start(f32[10,8,256]{2,1,0:T(8,128)S(1)} %get-tuple-element.19), channel_id=1, source_target_pairs={{0,16},{16,32},{32,48},{48,64},{64,80},{80,96},{96,112},{112,128},... | collective-permute-start | bytes 245768 | tf_op jit(solution)/shard_map/ppermute | solution.py:537
  19.4 3.9 %collective-permute-start.3 = (f32[10,8,256]{2,1,0:T(8,128)S(1)}, f32[10,8,256]{2,1,0:T(8,128)S(1)}, u32[]{:S(2)}, u32[]{:S(2)}) collective-permute-start(f32[10,8,256]{2,1,0:T(8,128)S(1)} %get-tuple-element.21), channel_id=1, source_target_pairs={{0,496},{16,0},{32,16},{48,32},{64,48},{80,64},{96,80},{112,96},{1... | collective-permute-start | bytes 245768 | tf_op jit(solution)/shard_map/ppermute | solution.py:537
  23.3 0.7 collective-permute-done.2.left_ref
  24.0 0.2 collective-permute-done.3.right_ref
  24.2 0.0 copy-done
  24.2 0.0 copy-start.2
  24.2 0.8 shard_map.52
  25.0 4.1 %collective-permute-start.6 = (f32[8,2,8,256]{3,2,1,0:T(8,128)S(1)}, f32[8,2,8,256]{3,2,1,0:T(8,128)S(1)}, u32[]{:S(2)}, u32[]{:S(2)}) collective-permute-start(f32[8,2,8,256]{3,2,1,0:T(8,128)S(1)} %get-tuple-element.23.refs_2_), channel_id=1, source_target_pairs={{0,496},{16,0},{32,16},{48,32},{64,48},{80,64},{96,80},{112,96},{1... | collective-permute-start | bytes 393224 | tf_op jit(solution)/shard_map/ppermute | solution.py:537
  29.1 0.0 collective-permute-start.4
  29.1 1.0 %collective-permute-done.6.refs_3_ = f32[8,2,8,256]{3,2,1,0:T(8,128)S(1)} collective-permute-done((f32[8,2,8,256]{3,2,1,0:T(8,128)S(1)}, f32[8,2,8,256]{3,2,1,0:T(8,128)S(1)}, u32[]{:S(2)}, u32[]{:S(2)}) %collective-permute-start.6) | collective-permute-done | bytes 131104 | tf_op jit(solution)/shard_map/ppermute | solution.py:537
  30.1 4.5 %collective-permute-start.7 = (f32[8,2,8,256]{3,2,1,0:T(8,128)S(1)}, f32[8,2,8,256]{3,2,1,0:T(8,128)S(1)}, u32[]{:S(2)}, u32[]{:S(2)}) collective-permute-start(f32[8,2,8,256]{3,2,1,0:T(8,128)S(1)} %collective-permute-done.6.refs_3_), channel_id=1, source_target_pairs={{0,496},{16,0},{32,16},{48,32},{64,48},{80,64},{96,80},{112,96},{1... | collective-permute-start | bytes 393224 | tf_op jit(solution)/shard_map/ppermute | solution.py:537
  34.6 0.0 collective-permute-done.4.refs_1_
  34.6 0.0 collective-permute-start.5
  34.6 1.0 %collective-permute-done.7.refs_4_ = f32[8,2,8,256]{3,2,1,0:T(8,128)S(1)} collective-permute-done((f32[8,2,8,256]{3,2,1,0:T(8,128)S(1)}, f32[8,2,8,256]{3,2,1,0:T(8,128)S(1)}, u32[]{:S(2)}, u32[]{:S(2)}) %collective-permute-start.7) | collective-permute-done | bytes 131104 | tf_op jit(solution)/shard_map/ppermute | solution.py:537
  35.6 2.9 %collective-permute-done.5.refs_0_ = f32[8,2,8,256]{3,2,1,0:T(8,128)S(1)} collective-permute-done((f32[8,2,8,256]{3,2,1,0:T(8,128)S(1)}, f32[8,2,8,256]{3,2,1,0:T(8,128)S(1)}, u32[]{:S(2)}, u32[]{:S(2)}) %collective-permute-start.5) | collective-permute-done | bytes 131104 | tf_op jit(solution)/shard_map/ppermute | solution.py:537
  38.5 0.0 copy-done.2
  38.5 4.8 %shard_map.53 = (f32[4,8,4,8,256]{4,3,2,1,0:T(8,128)S(1)}, f32[8,128]{1,0:T(8,128)S(1)}) custom-call(f32[8,2,8,256]{3,2,1,0:T(8,128)S(1)} %collective-permute-done.5.refs_0_, f32[8,2,8,256]{3,2,1,0:T(8,128)S(1)} %collective-permute-done.4.refs_1_, f32[8,2,8,256]{3,2,1,0:T(8,128)S(1)} %get-tuple-element.23.refs_2_, ...), custom_call_target="tpu_custom_call" | custom-call | tf_op jit(solution)/shard_map/pallas_call | solution.py:525
  43.3 6.3 %all-gather = f32[16,128]{1,0:T(8,128)S(1)} all-gather(f32[8,128]{1,0:T(8,128)S(1)} %get-tuple-element.25), channel_id=2, replica_groups={{0,16},{32,48},{64,80},{96,112},{128,144},{160,176},{192,208},{224,240}..., dimensions={0}, use_global_device_ids=true | all-gather | bytes 12288 | tf_op jit(solution)/shard_map/all_gather | solution.py:543
  49.6 0.1 broadcast_in_dim.2
  49.7 34.3 %all_to_all.8 = f32[256,1,128]{2,1,0:T(1,128)S(1)} all-to-all(f32[256,1,128]{2,1,0:T(1,128)S(1)} %broadcast_in_dim.2), channel_id=1, replica_groups={{0,1,2,3,4,5,6,7,8,9,10,11,12,13,14,15,32,33,34,35,36,37,38,39,40,41,42..., dimensions={0} | all-to-all | bytes 262144 | tf_op jit(solution)/shard_map/all_to_all | solution.py:546
  83.9 0.0 copy-start.3
  83.9 0.7 copy-done.3
  84.6 1.3 %shard_map.54 = (f32[3,8,2,8,128]{4,3,2,1,0:T(8,128)}, f32[8,2,8,128]{3,2,1,0:T(8,128)}) custom-call(f32[256,128]{1,0:T(8,128)S(1)} %bitcast.8, f32[4,8,4,8,256]{4,3,2,1,0:T(8,128)S(1)} %get-tuple-element.26.v_ref, f32[3,8,2,8,128]{4,3,2,1,0:T(8,128)S(1)} %get-tuple-element.27.w_ref, s32[2,2,16]{2,1,0:T(2,128)S(1)} %copy-done.3, bf16[256,256]{1,0:T(8,128)(2,1)S(1)} %copy-done), custom_call_target="tpu_custom_call" | custom-call | tf_op jit(solution)/shard_map/pallas_call | solution.py:525
  (1 shorter events, 0.0 us)
Async XLA Ops:
  3.6 9.9 %collective-permute-start = (f32[3,4,2,8,128]{4,3,2,1,0:T(8,128)}, f32[3,4,2,8,128]{4,3,2,1,0:T(8,128)S(1)}, u32[]{:S(2)}, u32[]{:S(2)}) collective-permute-start(f32[3,4,2,8,128]{4,3,2,1,0:T(8,128)} %get-tuple-element.17), channel_id=1, source_target_pairs={{0,1},{1,2},{2,3},{3,4},{4,5},{5,6},{6,7},{7,8},{8,9},{9,10},{10,1... | collective-permute-start | bytes 294920 | tf_op jit(solution)/shard_map/ppermute | solution.py:537
  7.6 7.5 %collective-permute-start.1 = (f32[3,4,2,8,128]{4,3,2,1,0:T(8,128)}, f32[3,4,2,8,128]{4,3,2,1,0:T(8,128)S(1)}, u32[]{:S(2)}, u32[]{:S(2)}) collective-permute-start(f32[3,4,2,8,128]{4,3,2,1,0:T(8,128)} %get-tuple-element.18), channel_id=1, source_target_pairs={{0,15},{1,0},{2,1},{3,2},{4,3},{5,4},{6,5},{7,6},{8,7},{9,8},{10,9... | collective-permute-start | bytes 294920 | tf_op jit(solution)/shard_map/ppermute | solution.py:537
  15.1 0.9 %copy-start.1 = (f32[3,8,2,8,128]{4,3,2,1,0:T(8,128)S(1)}, f32[3,8,2,8,128]{4,3,2,1,0:T(8,128)}, u32[]{:S(2)}) copy-start(f32[3,8,2,8,128]{4,3,2,1,0:T(8,128)} %get-tuple-element.16.r_ref) | copy-start | bytes 589828
  16.0 8.2 %copy-start = (bf16[256,256]{1,0:T(8,128)(2,1)S(1)}, bf16[256,256]{1,0:T(8,128)(2,1)}, u32[]{:S(2)}) copy-start(bf16[256,256]{1,0:T(8,128)(2,1)} %get-tuple-element.22.dy_ref) | copy-start | bytes 393220
  16.2 7.8 %collective-permute-start.2 = (f32[10,8,256]{2,1,0:T(8,128)S(1)}, f32[10,8,256]{2,1,0:T(8,128)S(1)}, u32[]{:S(2)}, u32[]{:S(2)}) collective-permute-start(f32[10,8,256]{2,1,0:T(8,128)S(1)} %get-tuple-element.19), channel_id=1, source_target_pairs={{0,16},{16,32},{32,48},{48,64},{64,80},{80,96},{96,112},{112,128},... | collective-permute-start | bytes 245768 | tf_op jit(solution)/shard_map/ppermute | solution.py:537
  19.4 4.8 %collective-permute-start.3 = (f32[10,8,256]{2,1,0:T(8,128)S(1)}, f32[10,8,256]{2,1,0:T(8,128)S(1)}, u32[]{:S(2)}, u32[]{:S(2)}) collective-permute-start(f32[10,8,256]{2,1,0:T(8,128)S(1)} %get-tuple-element.21), channel_id=1, source_target_pairs={{0,496},{16,0},{32,16},{48,32},{64,48},{80,64},{96,80},{112,96},{1... | collective-permute-start | bytes 245768 | tf_op jit(solution)/shard_map/ppermute | solution.py:537
  24.2 14.3 %copy-start.2 = (bf16[256,256]{1,0:T(8,128)(2,1)S(1)}, bf16[256,256]{1,0:T(8,128)(2,1)}, u32[]{:S(2)}) copy-start(bf16[256,256]{1,0:T(8,128)(2,1)} %get-tuple-element.24.refs_5_) | copy-start | bytes 393220
  25.0 5.1 %collective-permute-start.6 = (f32[8,2,8,256]{3,2,1,0:T(8,128)S(1)}, f32[8,2,8,256]{3,2,1,0:T(8,128)S(1)}, u32[]{:S(2)}, u32[]{:S(2)}) collective-permute-start(f32[8,2,8,256]{3,2,1,0:T(8,128)S(1)} %get-tuple-element.23.refs_2_), channel_id=1, source_target_pairs={{0,496},{16,0},{32,16},{48,32},{64,48},{80,64},{96,80},{112,96},{1... | collective-permute-start | bytes 393224 | tf_op jit(solution)/shard_map/ppermute | solution.py:537
  29.1 5.5 %collective-permute-start.4 = (f32[8,2,8,256]{3,2,1,0:T(8,128)S(1)}, f32[8,2,8,256]{3,2,1,0:T(8,128)S(1)}, u32[]{:S(2)}, u32[]{:S(2)}) collective-permute-start(f32[8,2,8,256]{3,2,1,0:T(8,128)S(1)} %get-tuple-element.23.refs_2_), channel_id=1, source_target_pairs={{0,16},{16,32},{32,48},{48,64},{64,80},{80,96},{96,112},{112,128},... | collective-permute-start | bytes 393224 | tf_op jit(solution)/shard_map/ppermute | solution.py:537
  30.1 5.5 %collective-permute-start.7 = (f32[8,2,8,256]{3,2,1,0:T(8,128)S(1)}, f32[8,2,8,256]{3,2,1,0:T(8,128)S(1)}, u32[]{:S(2)}, u32[]{:S(2)}) collective-permute-start(f32[8,2,8,256]{3,2,1,0:T(8,128)S(1)} %collective-permute-done.6.refs_3_), channel_id=1, source_target_pairs={{0,496},{16,0},{32,16},{48,32},{64,48},{80,64},{96,80},{112,96},{1... | collective-permute-start | bytes 393224 | tf_op jit(solution)/shard_map/ppermute | solution.py:537
  34.6 3.9 %collective-permute-start.5 = (f32[8,2,8,256]{3,2,1,0:T(8,128)S(1)}, f32[8,2,8,256]{3,2,1,0:T(8,128)S(1)}, u32[]{:S(2)}, u32[]{:S(2)}) collective-permute-start(f32[8,2,8,256]{3,2,1,0:T(8,128)S(1)} %collective-permute-done.4.refs_1_), channel_id=1, source_target_pairs={{0,16},{16,32},{32,48},{48,64},{64,80},{80,96},{96,112},{112,128},... | collective-permute-start | bytes 393224 | tf_op jit(solution)/shard_map/ppermute | solution.py:537
  83.9 0.7 copy-start.3

commit v3 on v2

--- a/solution.py
+++ b/solution.py
@@ -249,6 +249,13 @@
     lax.fori_loop(0, 2, body, 0)
 
 
+def hold_kernel(r_ref, turned_ref):
+    for c in range(3):
+        for z in range(8):
+            for e in range(2):
+                turned_ref[c, z, e] = pltpu.roll(r_ref[c, z, e], 64, axis=1)
+
+
 def join_kernel(r_ref, left_ref, right_ref, e_ref, up_ref, down_ref):
     half = iota(128, 1) < 64
     place = iota(256, 0)
@@ -260,7 +267,7 @@
         for z in range(8):
             tiles = []
             for e in range(2):
-                turned = pltpu.roll(r_ref[c, z, e], 64, axis=1)
+                turned = r_ref[c, z, e]
                 left = left_ref[c, z % 4, e]
                 right = right_ref[c, z % 4, e]
                 if z >= 4:
@@ -297,7 +304,7 @@
     return first_x, last_x, first_y, last_y
 
 
-def source_kernel(left_ref, mid_ref, right_ref, dy_ref, b_ref, w_ref, t_ref):
+def source_kernel(left_ref, mid_ref, right_ref, dy_ref, b_ref, w_ref, open_ref, t_ref):
     lanes = 256
     dcoef = row_coefs(lanes, deriv)
     wx = node_x(lanes, node_weights)
@@ -334,6 +341,9 @@
     slope[2] = weigh(row_turns(near), dcoef)
     for e in range(2):
         faces = mid_ref[0, :, e]
+        for face in range(2):
+            open_face = inside * (1.0 - wall(faces[7 * face]))
+            open_ref[face, e] = own_lanes(open_face[None])[0]
         w = []
         for c in range(3):
             if c == 0:
@@ -439,17 +449,17 @@
         part = part[:, :128] + part[:, 128:]
         total = jnp.sum(jnp.sum(part, axis=0, keepdims=True), axis=1, keepdims=True)
         packed = jnp.where(lane == k, total, packed)
-    m_out[...] = packed
-
-
-def final_kernel(m_ref, v_ref, w_ref, faces_ref, dy_ref, out_ref, q_ref):
+    for k in range(m_out.shape[0]):
+        m_out[k] = packed
+
+
+def final_kernel(m_ref, v_ref, w_ref, open_ref, dy_ref, out_ref, q_ref):
     lanes = 256
-    count = m_ref.shape[0] // 8
-    parts = [m_ref[8 * k : 8 * k + 8] for k in range(count)]
+    parts = [m_ref[k] for k in range(m_ref.shape[0])]
     while len(parts) > 1:
         odd = parts[len(parts) // 2 * 2 :]
         parts = [parts[k] + parts[k + 1] for k in range(0, len(parts) - 1, 2)] + odd
-    sums = jnp.broadcast_to(jnp.sum(parts[0], axis=0, keepdims=True), (8, 128))
+    sums = parts[0]
     lane = iota(128, 1)
 
     def moment(k):
@@ -492,8 +502,6 @@
     first_x, last_x, first_y, last_y = flags(lanes)
     mean_x = node_x(lanes, 1.0 / copies)
     mean_y = node_y(lanes, 1.0 / copies)
-    inside = 1.0 - rim_mask(128).astype(f32)
-    walls = expand_walls(faces_ref)
     q, slope = [], []
     for e in range(4):
         got = v_ref[0, :, e] * coef[0]
@@ -512,8 +520,7 @@
             for z in range(8):
                 got = w_ref[i, z, e] - parts[i][z]
                 if z in (0, 7):
-                    face = jnp.broadcast_to(walls[z // 7][e : e + 1], (8, 128))
-                    got = got * (inside * (1.0 - face))
+                    got = got * open_ref[z // 7, e]
                 out_ref[i, z, e] = got
 
 
@@ -521,13 +528,14 @@
     return jax.ShapeDtypeStruct(dims, f32)
 
 
-def call(kernel, out_shape, scratch, *args, space=pltpu.VMEM, vmem=48):
+def call(kernel, out_shape, scratch, *args, space=pltpu.VMEM, vmem=48, cost=None):
     return pl.pallas_call(
         kernel,
         out_shape=out_shape,
         in_specs=[pl.BlockSpec(memory_space=space)] * len(args),
         out_specs=jax.tree.map(lambda s: pl.BlockSpec(memory_space=pltpu.VMEM), out_shape),
         scratch_shapes=scratch,
+        cost_estimate=cost,
         compiler_params=pltpu.CompilerParams(vmem_limit_bytes=vmem * 2**20),
     )(*args)
 
@@ -539,11 +547,11 @@
 
 def total_rows(packed):
     nx, ny = lax.axis_size("gx"), lax.axis_size("gy")
-    pairs = [[i, i + 1] for i in range(0, nx, 2)]
-    both = lax.all_gather(packed, "gx", axis_index_groups=pairs)
-    rows = jnp.broadcast_to(both[0, :1] + both[1, :1], (nx // 2 * ny, 128))
-    chips = [[(2 * z + c) * ny + y for z in range(nx // 2) for y in range(ny)] for c in range(2)]
-    return lax.all_to_all(rows, ("gx", "gy"), 0, 0, axis_index_groups=chips, tiled=True)
+    along = [[2 * z + c for z in range(nx // 2)] for c in range(2)]
+    part = lax.all_to_all(packed, "gx", 0, 0, axis_index_groups=along, tiled=True)
+    part = jnp.broadcast_to(jnp.sum(part, axis=0, keepdims=True), (2 * ny, 8, 128))
+    planes = [[(2 * z + c) * ny + y for y in range(ny) for c in range(2)] for z in range(nx // 2)]
+    return lax.all_to_all(part, ("gx", "gy"), 0, 0, axis_index_groups=planes, tiled=True)
 
 
 def local(adjoint, checkpoints, wall_faces):
@@ -570,14 +578,16 @@
     left = shift(up, "gy", 1)
     right = shift(down, "gy", -1)
     packet = shape(10, 8, 256)
+    cost = pl.CostEstimate(flops=10**6, bytes_accessed=4 * 10**5, transcendentals=0)
+    turned = call(hold_kernel, shape(3, 8, 2, 8, 128), [], rhs, cost=cost)
     wide, up, down = call(
-        join_kernel, (shape(3, 8, 2, 8, 256), packet, packet), [], rhs, left, right
+        join_kernel, (shape(3, 8, 2, 8, 256), packet, packet), [], turned, left, right
     )
     before = shift(up, "gx", 1)
     after = shift(down, "gx", -1)
-    source, moved = call(
+    source, moved, opened = call(
         source_kernel,
-        (shape(8, 2, 8, 256), shape(3, 8, 2, 8, 128)),
+        (shape(8, 2, 8, 256), shape(3, 8, 2, 8, 128), shape(2, 2, 8, 128)),
         [vm((8, 2, 8, 256), f32)],
         before, wide, after, dy,
     )
@@ -587,7 +597,7 @@
     right2 = shift(right, "gx", -1)
     basis, packed = call(
         krylov_kernel,
-        (shape(4, 8, 4, 8, 256), shape(8, 128)),
+        (shape(4, 8, 4, 8, 256), shape(lax.axis_size("gx") // 2, 8, 128)),
         [
             vm((4, 8, 10, 8, 256), f32),
             vm((8, 10, 8, 256), f32),
@@ -600,7 +610,7 @@
         final_kernel,
         (shape(3, 8, 2, 8, 128), shape(8, 2, 8, 128)),
         [],
-        total_rows(packed), basis, moved, wall_faces, dy,
+        total_rows(packed), basis, moved, opened, dy,
     )
     return velocity.reshape(3, 8, 16, 128), pressure.reshape(8, 16, 128)
 

time: 87 us -> 85.6 us (0.984)
  blocking collectives: 40.5 us -> 41.7 us
  waiting for transfers between devices: 7.76 us -> 6.7 us
    all_to_all x1 -> x2, blocking collectives: 34.3 us -> 41.7 us  [the longest x1 22.9 us: total_rows(): lax.all_to_all(packed, 'gx', 0, 0, axis_index_groups=along, tiled=True)]
    all_gather x1 -> x0, blocking collectives: 6.25 us -> none  [total_rows(): both = lax.all_gather(packed, 'gx', axis_index_groups=pairs)]
    ppermute x8, waiting for transfers between devices: 7.76 us -> 6.7 us  [shift(): lax.ppermute(value, axis, [(i, (i + by) % size) for i in range(size)])]
    pallas_call x5 -> x6, Pallas kernels: 9.95 us -> 10 us  [call(): pl.pallas_call(kernel, out_shape=out_shape, in_specs=[pl.BlockSpec(memory...]
  transfers between devices with their start and end apart: 8 -> 8, of which waited for: 7 -> 6; matrix products, arithmetic and copies ran while one was open for 0% -> 0% of each run, Pallas kernels for 0% -> 0%
where the time goes in v3:
time: 85.6 us; the launch traced here: 85.3 us
  blocking collectives  41.7 us (49%)
  starting transfers between devices  25.3 us (30%)
  Pallas kernels  10 us (12%)
  waiting for transfers between devices  6.7 us (8%)
  local copies, waits for them, and re-layouts  0.94 us (1%)
    ppermute x8, starting transfers between devices, shift(): lax.ppermute(value, axis, [(i, (i + by) % size) for i in range(size)])  25.3 us
    all_to_all x1, blocking collectives, total_rows(): lax.all_to_all(packed, 'gx', 0, 0, axis_index_groups=along, tiled=True)  22.9 us
    all_to_all x1, blocking collectives, total_rows(): lax.all_to_all(part, ('gx', 'gy'), 0, 0, axis_index_groups=planes, tiled=...  18.8 us
    pallas_call x6, Pallas kernels, call(): pl.pallas_call(kernel, out_shape=out_shape, in_specs=[pl.BlockSpec(memory...  10 us
    ppermute x8, waiting for transfers between devices, shift(): lax.ppermute(value, axis, [(i, (i + by) % size) for i in range(size)])  6.7 us
  transfers between devices with their start and end apart: 8, of which 6 were waited for; matrix products, arithmetic and copies ran while one was open for 0% of the time, Pallas kernels for 0%

profile of v3, /device:TPU:1, one launch (start us, length us, event | category | flops | bytes accessed | tf_op | source)
XLA Modules:
  0.0 85.3 jit_solution(6536037619128139939)
XLA Ops:
  0.6 2.9 %shard_map.50 = (f32[3,8,2,8,128]{4,3,2,1,0:T(8,128)}, f32[3,4,2,8,128]{4,3,2,1,0:T(8,128)}, f32[3,4,2,8,128]{4,3,2,1,0:T(8,128)}, bf16[256,256]{1,0:T(8,128)(2,1)}, bf16[256,256]{1,0:T(8,128)(2,1)}) custom-call(f32[3,8,2,8,128]{4,3,2,1,0:T(8,128)} %bitcast.4, bf16[3,8,16,128]{3,2,1,0:T(8,128)(2,1)} %bitcast.5, s32[2,2,16]{2,1,0:T(2,128)} %faces_hbm.1), custom_call_target="tpu_custom_call" | custom-call | tf_op jit(solution)/shard_map/pallas_call | solution.py:532
  3.6 4.0 %collective-permute-start = (f32[3,4,2,8,128]{4,3,2,1,0:T(8,128)}, f32[3,4,2,8,128]{4,3,2,1,0:T(8,128)S(1)}, u32[]{:S(2)}, u32[]{:S(2)}) collective-permute-start(f32[3,4,2,8,128]{4,3,2,1,0:T(8,128)} %get-tuple-element.18), channel_id=1, source_target_pairs={{0,1},{1,2},{2,3},{3,4},{4,5},{5,6},{6,7},{7,8},{8,9},{9,10},{10,1... | collective-permute-start | bytes 294920 | tf_op jit(solution)/shard_map/ppermute | solution.py:545
  7.6 5.6 %collective-permute-start.1 = (f32[3,4,2,8,128]{4,3,2,1,0:T(8,128)}, f32[3,4,2,8,128]{4,3,2,1,0:T(8,128)S(1)}, u32[]{:S(2)}, u32[]{:S(2)}) collective-permute-start(f32[3,4,2,8,128]{4,3,2,1,0:T(8,128)} %get-tuple-element.19), channel_id=1, source_target_pairs={{0,15},{1,0},{2,1},{3,2},{4,3},{5,4},{6,5},{7,6},{8,7},{9,8},{10,9... | collective-permute-start | bytes 294920 | tf_op jit(solution)/shard_map/ppermute | solution.py:545
  13.2 0.0 copy-start.1
  13.2 0.9 %copy-done.1 = f32[3,8,2,8,128]{4,3,2,1,0:T(8,128)S(1)} copy-done((f32[3,8,2,8,128]{4,3,2,1,0:T(8,128)S(1)}, f32[3,8,2,8,128]{4,3,2,1,0:T(8,128)}, u32[]{:S(2)}) %copy-start.1) | copy-done | bytes 196632
  14.1 0.1 shard_map.51.r_ref
  14.2 0.0 copy-start
  14.2 0.0 collective-permute-done.left_ref
  14.2 0.9 %collective-permute-done.1.right_ref = f32[3,4,2,8,128]{4,3,2,1,0:T(8,128)S(1)} collective-permute-done((f32[3,4,2,8,128]{4,3,2,1,0:T(8,128)}, f32[3,4,2,8,128]{4,3,2,1,0:T(8,128)S(1)}, u32[]{:S(2)}, u32[]{:S(2)}) %collective-permute-start.1) | collective-permute-done | bytes 98336 | tf_op jit(solution)/shard_map/ppermute | solution.py:545
  15.1 0.1 shard_map.52
  15.2 3.2 %collective-permute-start.2 = (f32[10,8,256]{2,1,0:T(8,128)S(1)}, f32[10,8,256]{2,1,0:T(8,128)S(1)}, u32[]{:S(2)}, u32[]{:S(2)}) collective-permute-start(f32[10,8,256]{2,1,0:T(8,128)S(1)} %get-tuple-element.20), channel_id=1, source_target_pairs={{0,16},{16,32},{32,48},{48,64},{64,80},{80,96},{96,112},{112,128},... | collective-permute-start | bytes 245768 | tf_op jit(solution)/shard_map/ppermute | solution.py:545
  18.4 3.9 %collective-permute-start.3 = (f32[10,8,256]{2,1,0:T(8,128)S(1)}, f32[10,8,256]{2,1,0:T(8,128)S(1)}, u32[]{:S(2)}, u32[]{:S(2)}) collective-permute-start(f32[10,8,256]{2,1,0:T(8,128)S(1)} %get-tuple-element.22), channel_id=1, source_target_pairs={{0,496},{16,0},{32,16},{48,32},{64,48},{80,64},{96,80},{112,96},{1... | collective-permute-start | bytes 245768 | tf_op jit(solution)/shard_map/ppermute | solution.py:545
  22.3 0.7 collective-permute-done.2.left_ref
  23.0 0.2 collective-permute-done.3.right_ref
  23.2 0.0 copy-done
  23.2 0.0 copy-start.2
  23.2 0.8 shard_map.53
  24.0 4.1 %collective-permute-start.6 = (f32[8,2,8,256]{3,2,1,0:T(8,128)S(1)}, f32[8,2,8,256]{3,2,1,0:T(8,128)S(1)}, u32[]{:S(2)}, u32[]{:S(2)}) collective-permute-start(f32[8,2,8,256]{3,2,1,0:T(8,128)S(1)} %get-tuple-element.24.refs_2_), channel_id=1, source_target_pairs={{0,496},{16,0},{32,16},{48,32},{64,48},{80,64},{96,80},{112,96},{1... | collective-permute-start | bytes 393224 | tf_op jit(solution)/shard_map/ppermute | solution.py:545
  28.2 0.0 collective-permute-start.4
  28.2 1.0 %collective-permute-done.6.refs_3_ = f32[8,2,8,256]{3,2,1,0:T(8,128)S(1)} collective-permute-done((f32[8,2,8,256]{3,2,1,0:T(8,128)S(1)}, f32[8,2,8,256]{3,2,1,0:T(8,128)S(1)}, u32[]{:S(2)}, u32[]{:S(2)}) %collective-permute-start.6) | collective-permute-done | bytes 131104 | tf_op jit(solution)/shard_map/ppermute | solution.py:545
  29.1 4.5 %collective-permute-start.7 = (f32[8,2,8,256]{3,2,1,0:T(8,128)S(1)}, f32[8,2,8,256]{3,2,1,0:T(8,128)S(1)}, u32[]{:S(2)}, u32[]{:S(2)}) collective-permute-start(f32[8,2,8,256]{3,2,1,0:T(8,128)S(1)} %collective-permute-done.6.refs_3_), channel_id=1, source_target_pairs={{0,496},{16,0},{32,16},{48,32},{64,48},{80,64},{96,80},{112,96},{1... | collective-permute-start | bytes 393224 | tf_op jit(solution)/shard_map/ppermute | solution.py:545
  33.6 0.0 collective-permute-done.4.refs_1_
  33.6 0.0 collective-permute-start.5
  33.6 1.0 %collective-permute-done.7.refs_4_ = f32[8,2,8,256]{3,2,1,0:T(8,128)S(1)} collective-permute-done((f32[8,2,8,256]{3,2,1,0:T(8,128)S(1)}, f32[8,2,8,256]{3,2,1,0:T(8,128)S(1)}, u32[]{:S(2)}, u32[]{:S(2)}) %collective-permute-start.7) | collective-permute-done | bytes 131104 | tf_op jit(solution)/shard_map/ppermute | solution.py:545
  34.6 2.9 %collective-permute-done.5.refs_0_ = f32[8,2,8,256]{3,2,1,0:T(8,128)S(1)} collective-permute-done((f32[8,2,8,256]{3,2,1,0:T(8,128)S(1)}, f32[8,2,8,256]{3,2,1,0:T(8,128)S(1)}, u32[]{:S(2)}, u32[]{:S(2)}) %collective-permute-start.5) | collective-permute-done | bytes 131104 | tf_op jit(solution)/shard_map/ppermute | solution.py:545
  37.6 0.0 copy-done.2
  37.6 4.8 %shard_map.54 = (f32[4,8,4,8,256]{4,3,2,1,0:T(8,128)S(1)}, f32[16,8,128]{2,1,0:T(8,128)S(1)}) custom-call(f32[8,2,8,256]{3,2,1,0:T(8,128)S(1)} %collective-permute-done.5.refs_0_, f32[8,2,8,256]{3,2,1,0:T(8,128)S(1)} %collective-permute-done.4.refs_1_, f32[8,2,8,256]{3,2,1,0:T(8,128)S(1)} %get-tuple-element.24.refs_2_, ...), custom_call_target="tpu_custom_call" | custom-call | tf_op jit(solution)/shard_map/pallas_call | solution.py:532
  42.4 22.9 %all_to_all.10 = f32[16,8,128]{2,1,0:T(8,128)S(1)} all-to-all(f32[16,8,128]{2,1,0:T(8,128)S(1)} %get-tuple-element.26), channel_id=1, replica_groups={{0,32,64,96,128,160,192,224,256,288,320,352,384,416,448,480},{16,48,80,..., dimensions={0} | all-to-all | bytes 131072 | tf_op jit(solution)/shard_map/all_to_all | solution.py:551
  65.3 18.8 %all_to_all.11.m_ref = f32[32,8,128]{2,1,0:T(8,128)S(1)} all-to-all(f32[32,8,128]{2,1,0:T(8,128)S(1)} %broadcast_in_dim.2), channel_id=1, replica_groups={{0,16,1,17,2,18,3,19,4,20,5,21,6,22,7,23,8,24,9,25,10,26,11,27,12,28,13..., dimensions={0} | all-to-all | bytes 262144 | tf_op jit(solution)/shard_map/all_to_all | solution.py:554
  84.1 1.3 %shard_map.55 = (f32[3,8,2,8,128]{4,3,2,1,0:T(8,128)}, f32[8,2,8,128]{3,2,1,0:T(8,128)}) custom-call(f32[32,8,128]{2,1,0:T(8,128)S(1)} %all_to_all.11.m_ref, f32[4,8,4,8,256]{4,3,2,1,0:T(8,128)S(1)} %get-tuple-element.27.v_ref, f32[3,8,2,8,128]{4,3,2,1,0:T(8,128)S(1)} %get-tuple-element.28.w_ref, f32[2,2,8,128]{3,2,1,0:T(8,128)S(1)} %get-tuple-element.29.open_ref, ...), custom_call_target="tpu_custom_call" | custom-call | tf_op jit(solution)/shard_map/pallas_call | solution.py:532
  (2 shorter events, 0.0 us)
Async XLA Ops:
  3.6 10.7 %collective-permute-start = (f32[3,4,2,8,128]{4,3,2,1,0:T(8,128)}, f32[3,4,2,8,128]{4,3,2,1,0:T(8,128)S(1)}, u32[]{:S(2)}, u32[]{:S(2)}) collective-permute-start(f32[3,4,2,8,128]{4,3,2,1,0:T(8,128)} %get-tuple-element.18), channel_id=1, source_target_pairs={{0,1},{1,2},{2,3},{3,4},{4,5},{5,6},{6,7},{7,8},{8,9},{9,10},{10,1... | collective-permute-start | bytes 294920 | tf_op jit(solution)/shard_map/ppermute | solution.py:545
  7.6 7.5 %collective-permute-start.1 = (f32[3,4,2,8,128]{4,3,2,1,0:T(8,128)}, f32[3,4,2,8,128]{4,3,2,1,0:T(8,128)S(1)}, u32[]{:S(2)}, u32[]{:S(2)}) collective-permute-start(f32[3,4,2,8,128]{4,3,2,1,0:T(8,128)} %get-tuple-element.19), channel_id=1, source_target_pairs={{0,15},{1,0},{2,1},{3,2},{4,3},{5,4},{6,5},{7,6},{8,7},{9,8},{10,9... | collective-permute-start | bytes 294920 | tf_op jit(solution)/shard_map/ppermute | solution.py:545
  13.2 0.9 %copy-start.1 = (f32[3,8,2,8,128]{4,3,2,1,0:T(8,128)S(1)}, f32[3,8,2,8,128]{4,3,2,1,0:T(8,128)}, u32[]{:S(2)}) copy-start(f32[3,8,2,8,128]{4,3,2,1,0:T(8,128)} %get-tuple-element.17.r_ref) | copy-start | bytes 589828
  14.2 9.0 %copy-start = (bf16[256,256]{1,0:T(8,128)(2,1)S(1)}, bf16[256,256]{1,0:T(8,128)(2,1)}, u32[]{:S(2)}) copy-start(bf16[256,256]{1,0:T(8,128)(2,1)} %get-tuple-element.23.dy_ref) | copy-start | bytes 393220
  15.2 7.8 %collective-permute-start.2 = (f32[10,8,256]{2,1,0:T(8,128)S(1)}, f32[10,8,256]{2,1,0:T(8,128)S(1)}, u32[]{:S(2)}, u32[]{:S(2)}) collective-permute-start(f32[10,8,256]{2,1,0:T(8,128)S(1)} %get-tuple-element.20), channel_id=1, source_target_pairs={{0,16},{16,32},{32,48},{48,64},{64,80},{80,96},{96,112},{112,128},... | collective-permute-start | bytes 245768 | tf_op jit(solution)/shard_map/ppermute | solution.py:545
  18.4 4.8 %collective-permute-start.3 = (f32[10,8,256]{2,1,0:T(8,128)S(1)}, f32[10,8,256]{2,1,0:T(8,128)S(1)}, u32[]{:S(2)}, u32[]{:S(2)}) collective-permute-start(f32[10,8,256]{2,1,0:T(8,128)S(1)} %get-tuple-element.22), channel_id=1, source_target_pairs={{0,496},{16,0},{32,16},{48,32},{64,48},{80,64},{96,80},{112,96},{1... | collective-permute-start | bytes 245768 | tf_op jit(solution)/shard_map/ppermute | solution.py:545
  23.2 14.3 %copy-start.2 = (bf16[256,256]{1,0:T(8,128)(2,1)S(1)}, bf16[256,256]{1,0:T(8,128)(2,1)}, u32[]{:S(2)}) copy-start(bf16[256,256]{1,0:T(8,128)(2,1)} %get-tuple-element.25.refs_5_) | copy-start | bytes 393220
  24.0 5.1 %collective-permute-start.6 = (f32[8,2,8,256]{3,2,1,0:T(8,128)S(1)}, f32[8,2,8,256]{3,2,1,0:T(8,128)S(1)}, u32[]{:S(2)}, u32[]{:S(2)}) collective-permute-start(f32[8,2,8,256]{3,2,1,0:T(8,128)S(1)} %get-tuple-element.24.refs_2_), channel_id=1, source_target_pairs={{0,496},{16,0},{32,16},{48,32},{64,48},{80,64},{96,80},{112,96},{1... | collective-permute-start | bytes 393224 | tf_op jit(solution)/shard_map/ppermute | solution.py:545
  28.2 5.5 %collective-permute-start.4 = (f32[8,2,8,256]{3,2,1,0:T(8,128)S(1)}, f32[8,2,8,256]{3,2,1,0:T(8,128)S(1)}, u32[]{:S(2)}, u32[]{:S(2)}) collective-permute-start(f32[8,2,8,256]{3,2,1,0:T(8,128)S(1)} %get-tuple-element.24.refs_2_), channel_id=1, source_target_pairs={{0,16},{16,32},{32,48},{48,64},{64,80},{80,96},{96,112},{112,128},... | collective-permute-start | bytes 393224 | tf_op jit(solution)/shard_map/ppermute | solution.py:545
  29.1 5.5 %collective-permute-start.7 = (f32[8,2,8,256]{3,2,1,0:T(8,128)S(1)}, f32[8,2,8,256]{3,2,1,0:T(8,128)S(1)}, u32[]{:S(2)}, u32[]{:S(2)}) collective-permute-start(f32[8,2,8,256]{3,2,1,0:T(8,128)S(1)} %collective-permute-done.6.refs_3_), channel_id=1, source_target_pairs={{0,496},{16,0},{32,16},{48,32},{64,48},{80,64},{96,80},{112,96},{1... | collective-permute-start | bytes 393224 | tf_op jit(solution)/shard_map/ppermute | solution.py:545
  33.6 3.9 %collective-permute-start.5 = (f32[8,2,8,256]{3,2,1,0:T(8,128)S(1)}, f32[8,2,8,256]{3,2,1,0:T(8,128)S(1)}, u32[]{:S(2)}, u32[]{:S(2)}) collective-permute-start(f32[8,2,8,256]{3,2,1,0:T(8,128)S(1)} %collective-permute-done.4.refs_1_), channel_id=1, source_target_pairs={{0,16},{16,32},{32,48},{48,64},{64,80},{80,96},{96,112},{112,128},... | collective-permute-start | bytes 393224 | tf_op jit(solution)/shard_map/ppermute | solution.py:545

commit v4 on v3

--- a/solution.py
+++ b/solution.py
@@ -176,8 +176,8 @@
 
 def rhs_kernel(
     adj_hbm, flow_hbm, faces_hbm,
-    r_ref, up_ref, down_ref, dy_ref, ky_ref,
-    adj_ref, flow_ref, faces_ref, u_ref, wall_ref, sems,
+    r_ref, up_ref, down_ref,
+    adj_ref, flow_ref, faces_ref, u_ref, wall_ref, dy_ref, ky_ref, sems,
 ):
     moves = [
         pltpu.make_async_copy(src, dst, sems.at[k])
@@ -249,7 +249,9 @@
     lax.fori_loop(0, 2, body, 0)
 
 
-def hold_kernel(r_ref, turned_ref):
+def hold_kernel(r_ref, turned_ref, dy_ref, ky_ref):
+    dy_ref[...] = lane_table(deriv)
+    ky_ref[...] = lane_table(scaled_stiff)
     for c in range(3):
         for z in range(8):
             for e in range(2):
@@ -373,31 +375,30 @@
             b_ref[z, e] = got
 
 
-def krylov_kernel(*refs):
-    blocks = refs[:5]
-    ky_ref, v_out, m_out, v_ref, k_ref, p_ref, acc_ref = refs[5:]
+def fold(value):
+    total = value[0]
+    for z in range(1, 8):
+        total = total + value[z]
+    return total
+
+
+def load_block(ref, at, v_ref, p_ref, rim, fill):
+    for e in range(2):
+        for z in range(8):
+            got = ref[z, e]
+            if z in (0, 7):
+                face = jnp.broadcast_to(got[0:1, :], got.shape)
+                p_ref[z // 7, at + e] = jnp.where(rim, 0.0, face)
+                got = jnp.where(rim, 0.0, got)
+            if fill:
+                v_ref[0, z, at + e] = got
+
+
+def krylov_tools(ky_ref, v_ref, k_ref, p_ref):
     lanes = 256
-    rim = rim_mask(lanes)
-    for k, ref in enumerate(blocks):
-        for e in range(2):
-            at = 2 * k + e
-            for z in range(8):
-                got = ref[z, e]
-                if z in (0, 7):
-                    face = jnp.broadcast_to(got[0:1, :], (8, lanes))
-                    p_ref[z // 7, at] = jnp.where(rim, 0.0, face)
-                    got = jnp.where(rim, 0.0, got)
-                v_ref[0, z, at] = got
     kcoef = row_coefs(lanes, scaled_stiff)
     wxy = node_x(lanes, node_weights) * node_y(lanes, node_weights)
     first_x, last_x, first_y, last_y = flags(lanes)
-    acc_ref[...] = jnp.zeros(acc_ref.shape, f32)
-
-    def fold(value):
-        total = value[0]
-        for z in range(1, 8):
-            total = total + value[z]
-        return total
 
     def apply(j, e):
         v = v_ref[j, :, e]
@@ -405,45 +406,89 @@
         xk = weigh(row_turns(v), kcoef)
         zk = depth([v[z] for z in range(8)], scaled_stiff, 1)
         for z in range(8):
-            k_ref[z, e] = (xk[z] + zk[z] + yk[z]) * (wxy * float(node_weights[z] / span))
-
+            k_ref[j, z, e] = (xk[z] + zk[z] + yk[z]) * (wxy * float(node_weights[z] / span))
+
+    def step(j, e):
+        rows = sum_rows(
+            k_ref[j, :, e - 1], k_ref[j, :, e], k_ref[j, :, e + 1], first_x, last_x
+        )
+        total = sum_lanes(rows, first_y, last_y)
+        for z in range(8):
+            image = total[z]
+            if z in (0, 7):
+                image = image * p_ref[z // 7, e]
+            v_ref[j + 1, z, e] = image - 0.5 * v_ref[j, z, e]
+
+    return apply, step
+
+
+def over(low, high, body):
+    lax.fori_loop(low, high, lambda e, c: (body(e), c)[1], 0, unroll=2)
+
+
+def sides(low, body):
+    over(0, 4, lambda t: body(low + t + (t // 2) * (6 - 2 * low)))
+
+
+def inner_kernel(left_ref, mid_ref, right_ref, ky_ref, v_ref, k_ref, acc_ref, p_ref):
+    rim = rim_mask(256)
+    for at, ref in ((2, left_ref), (4, mid_ref), (6, right_ref)):
+        load_block(ref, at, v_ref, p_ref, rim, True)
+    apply, step = krylov_tools(ky_ref, v_ref, k_ref, p_ref)
     slot = 0
-    for j in range(ROUNDS):
-        low, high = (j, 10 - j) if j < 3 else (4, 6)
-        lax.fori_loop(low, high, lambda e, c, j=j: (apply(j, e), c)[1], 0, unroll=2)
-
-        def gram(e, carry, j=j, slot=slot):
-            image = k_ref[:, e]
-            for i in range(j + 1):
-                acc_ref[slot + i] += fold(v_ref[i, :, e] * image)
-            acc_ref[10 + j] += fold(v_ref[j, :, e] * v_ref[0, :, e])
-            return carry
-
-        lax.fori_loop(4, 6, gram, 0, unroll=2)
+    for j in range(3):
+        over(2 + j, 8 - j, lambda e, j=j: apply(j, e))
+        for i in range(j + 1):
+            acc_ref[slot + i] = fold(v_ref[i, :, 4] * k_ref[j, :, 4]) + fold(
+                v_ref[i, :, 5] * k_ref[j, :, 5]
+            )
+        acc_ref[6 + j] = fold(v_ref[j, :, 4] * v_ref[0, :, 4]) + fold(
+            v_ref[j, :, 5] * v_ref[0, :, 5]
+        )
         slot += j + 1
-        if j < 3:
-
-            def step(e, carry, j=j):
-                rows = sum_rows(k_ref[:, e - 1], k_ref[:, e], k_ref[:, e + 1], first_x, last_x)
-                total = sum_lanes(rows, first_y, last_y)
-                for z in range(8):
-                    image = total[z]
-                    if z in (0, 7):
-                        image = image * p_ref[z // 7, e]
-                    v_ref[j + 1, z, e] = image - 0.5 * v_ref[j, z, e]
-                return carry
-
-            lax.fori_loop(low + 1, high - 1, step, 0, unroll=2)
-    for j in range(ROUNDS):
-        for e in range(4):
-            v_out[j, :, e] = v_ref[j, :, 3 + e]
+        if j < 2:
+            over(3 + j, 7 - j, lambda e, j=j: step(j, e))
+
+
+def outer_kernel(*refs):
+    blocks = refs[:5]
+    v_in, k_in, acc_ref, ky_ref, v_out, m_out, v_ref, k_ref, p_ref = refs[5:]
+    lanes = 256
+    rim = rim_mask(lanes)
+    for k, ref in enumerate(blocks):
+        load_block(ref, 2 * k, v_ref, p_ref, rim, k in (0, 4))
+    for j, els in ((0, (2, 3, 4, 5, 6, 7)), (1, (3, 4, 5, 6)), (2, (4, 5))):
+        for e in els:
+            v_ref[j, :, e] = v_in[j, :, e]
+            if j or e not in (4, 5):
+                k_ref[j, :, e] = k_in[j, :, e]
+    apply, step = krylov_tools(ky_ref, v_ref, k_ref, p_ref)
+    for j in range(3):
+        sides(j, lambda e, j=j: apply(j, e))
+        if j < 2:
+            sides(j + 1, lambda e, j=j: step(j, e))
+        else:
+            over(3, 7, lambda e: step(2, e))
+    over(4, 6, lambda e: apply(3, e))
+    for e in range(4):
+        v_out[0, :, e] = v_ref[2, :, 3 + e]
+        v_out[1, :, e] = v_ref[3, :, 3 + e]
+    energy = [acc_ref[k] for k in range(6)]
+    for i in range(ROUNDS):
+        energy.append(
+            fold(v_ref[i, :, 4] * k_ref[3, :, 4]) + fold(v_ref[i, :, 5] * k_ref[3, :, 5])
+        )
+    load = [acc_ref[6 + k] for k in range(3)]
+    load.append(
+        fold(v_ref[3, :, 4] * v_ref[0, :, 4]) + fold(v_ref[3, :, 5] * v_ref[0, :, 5])
+    )
     lane = iota(lanes, 1)
     own = (lane >= 64) & (lane < 192)
     share = node_x(lanes, 1.0 / copies) * node_y(lanes, 1.0 / copies)
     lane = iota(128, 1)
     packed = jnp.zeros((8, 128), f32)
-    for k in range(14):
-        part = jnp.where(own, acc_ref[k], 0.0)
+    for k, part in enumerate(energy + load):
+        part = jnp.where(own, part, 0.0)
         if k >= 10:
             part = part * share
         part = part[:, :128] + part[:, 128:]
@@ -453,7 +498,7 @@
         m_out[k] = packed
 
 
-def final_kernel(m_ref, v_ref, w_ref, open_ref, dy_ref, out_ref, q_ref):
+def final_kernel(m_ref, low_ref, high_ref, w_ref, open_ref, dy_ref, out_ref, q_ref):
     lanes = 256
     parts = [m_ref[k] for k in range(m_ref.shape[0])]
     while len(parts) > 1:
@@ -504,9 +549,8 @@
     mean_y = node_y(lanes, 1.0 / copies)
     q, slope = [], []
     for e in range(4):
-        got = v_ref[0, :, e] * coef[0]
-        for j in range(1, ROUNDS):
-            got = got + v_ref[j, :, e] * coef[j]
+        got = low_ref[0, :, 3 + e] * coef[0] + low_ref[1, :, 3 + e] * coef[1]
+        got = got + high_ref[0, :, e] * coef[2] + high_ref[1, :, e] * coef[3]
         q.append(got)
         slope.append(weigh(row_turns(got), dcoef))
     for e in range(2):
@@ -549,9 +593,10 @@
     nx, ny = lax.axis_size("gx"), lax.axis_size("gy")
     along = [[2 * z + c for z in range(nx // 2)] for c in range(2)]
     part = lax.all_to_all(packed, "gx", 0, 0, axis_index_groups=along, tiled=True)
-    part = jnp.broadcast_to(jnp.sum(part, axis=0, keepdims=True), (2 * ny, 8, 128))
-    planes = [[(2 * z + c) * ny + y for y in range(ny) for c in range(2)] for z in range(nx // 2)]
-    return lax.all_to_all(part, ("gx", "gy"), 0, 0, axis_index_groups=planes, tiled=True)
+    part = jnp.broadcast_to(jnp.sum(part, axis=0, keepdims=True), (ny, 8, 128))
+    part = lax.all_to_all(part, "gy", 0, 0, tiled=True)
+    pairs = [[i, i + 1] for i in range(0, nx, 2)]
+    return lax.all_gather(part, "gx", axis_index_groups=pairs, tiled=True)
 
 
 def local(adjoint, checkpoints, wall_faces):
@@ -560,15 +605,17 @@
     vm = pltpu.VMEM
     table = jax.ShapeDtypeStruct((256, 256), bf16)
     strip = shape(3, 4, 2, 8, 128)
-    rhs, up, down, dy, ky = call(
+    rhs, up, down = call(
         rhs_kernel,
-        (shape(3, 8, 2, 8, 128), strip, strip, table, table),
+        (shape(3, 8, 2, 8, 128), strip, strip),
         [
             vm((3, 8, 2, 8, 128), f32),
             vm((3, 8, 16, 128), bf16),
             vm((2, 2, 16), jnp.int32),
             vm((3, 8, 2, 8, 128), f32),
             vm((2, 2, 8, 128), f32),
+            vm((256, 256), bf16),
+            vm((256, 256), bf16),
             pltpu.SemaphoreType.DMA((3,)),
         ],
         adj, flow, wall_faces,
@@ -579,7 +626,9 @@
     right = shift(down, "gy", -1)
     packet = shape(10, 8, 256)
     cost = pl.CostEstimate(flops=10**6, bytes_accessed=4 * 10**5, transcendentals=0)
-    turned = call(hold_kernel, shape(3, 8, 2, 8, 128), [], rhs, cost=cost)
+    turned, dy, ky = call(
+        hold_kernel, (shape(3, 8, 2, 8, 128), table, table), [], rhs, cost=cost
+    )
     wide, up, down = call(
         join_kernel, (shape(3, 8, 2, 8, 256), packet, packet), [], turned, left, right
     )
@@ -595,22 +644,29 @@
     right = shift(source, "gx", -1)
     left2 = shift(left, "gx", 1)
     right2 = shift(right, "gx", -1)
-    basis, packed = call(
-        krylov_kernel,
-        (shape(4, 8, 4, 8, 256), shape(lax.axis_size("gx") // 2, 8, 128)),
+    cost = pl.CostEstimate(flops=5 * 10**6, bytes_accessed=4 * 10**6, transcendentals=0)
+    low, images, acc = call(
+        inner_kernel,
+        (shape(3, 8, 10, 8, 256), shape(3, 8, 10, 8, 256), shape(9, 8, 256)),
+        [vm((2, 10, 8, 256), f32)],
+        left, source, right, ky,
+        cost=cost,
+    )
+    high, packed = call(
+        outer_kernel,
+        (shape(2, 8, 4, 8, 256), shape(lax.axis_size("gx") // 2, 8, 128)),
         [
             vm((4, 8, 10, 8, 256), f32),
-            vm((8, 10, 8, 256), f32),
+            vm((4, 8, 10, 8, 256), f32),
             vm((2, 10, 8, 256), f32),
-            vm((14, 8, 256), f32),
         ],
-        left2, left, source, right, right2, ky,
+        left2, left, source, right, right2, low, images, acc, ky,
     )
     velocity, pressure = call(
         final_kernel,
         (shape(3, 8, 2, 8, 128), shape(8, 2, 8, 128)),
         [],
-        total_rows(packed), basis, moved, opened, dy,
+        total_rows(packed), low, high, moved, opened, dy,
     )
     return velocity.reshape(3, 8, 16, 128), pressure.reshape(8, 16, 128)
 

time: 85.6 us -> 85.1 us (level)
  waiting for transfers between devices: 6.7 us -> 4.78 us
  blocking collectives: 41.7 us -> 43.1 us
    all_gather x0 -> x1, blocking collectives: none -> 7.19 us  [total_rows(): return lax.all_gather(part, 'gx', axis_index_groups=pairs, tiled=True)]
    all_to_all x1, blocking collectives: 18.8 us -> 13 us  [total_rows(): part = lax.all_to_all(part, 'gy', 0, 0, tiled=True)]
    ppermute x8, waiting for transfers between devices: 6.7 us -> 4.78 us  [shift(): lax.ppermute(value, axis, [(i, (i + by) % size) for i in range(size)])]
    pallas_call x6 -> x7, Pallas kernels: 10 us -> 9.96 us  [call(): pl.pallas_call(kernel, out_shape=out_shape, in_specs=[pl.BlockSpec(memory...]
  transfers between devices with their start and end apart: 8 -> 8, of which waited for: 6 -> 5; matrix products, arithmetic and copies ran while one was open for 0% -> 0% of each run, Pallas kernels for 0% -> 2%
where the time goes in v4:
time: 85.1 us; the launch traced here: 84.8 us
  blocking collectives  43.1 us (51%)
  starting transfers between devices  25.3 us (30%)
  Pallas kernels  9.96 us (12%)
  waiting for transfers between devices  4.78 us (6%)
  local copies, waits for them, and re-layouts  0.93 us (1%)
    ppermute x8, starting transfers between devices, shift(): lax.ppermute(value, axis, [(i, (i + by) % size) for i in range(size)])  25.3 us
    all_to_all x1, blocking collectives, total_rows(): lax.all_to_all(packed, 'gx', 0, 0, axis_index_groups=along, tiled=True)  22.9 us
    all_to_all x1, blocking collectives, total_rows(): part = lax.all_to_all(part, 'gy', 0, 0, tiled=True)  13 us
    pallas_call x7, Pallas kernels, call(): pl.pallas_call(kernel, out_shape=out_shape, in_specs=[pl.BlockSpec(memory...  9.96 us
    all_gather x1, blocking collectives, total_rows(): return lax.all_gather(part, 'gx', axis_index_groups=pairs, tiled=True)  7.19 us
    ppermute x8, waiting for transfers between devices, shift(): lax.ppermute(value, axis, [(i, (i + by) % size) for i in range(size)])  4.78 us
  transfers between devices with their start and end apart: 8, of which 5 were waited for; matrix products, arithmetic and copies ran while one was open for 0% of the time, Pallas kernels for 2%

profile of v4, /device:TPU:1, one launch (start us, length us, event | category | flops | bytes accessed | tf_op | source)
XLA Modules:
  0.0 84.8 jit_solution(17723362935081837855)
XLA Ops:
  0.6 2.9 %shard_map.50 = (f32[3,8,2,8,128]{4,3,2,1,0:T(8,128)}, f32[3,4,2,8,128]{4,3,2,1,0:T(8,128)}, f32[3,4,2,8,128]{4,3,2,1,0:T(8,128)}) custom-call(f32[3,8,2,8,128]{4,3,2,1,0:T(8,128)} %bitcast.4, bf16[3,8,16,128]{3,2,1,0:T(8,128)(2,1)} %bitcast.5, s32[2,2,16]{2,1,0:T(2,128)} %faces_hbm.1), custom_call_target="tpu_custom_call" | custom-call | tf_op jit(solution)/shard_map/pallas_call | solution.py:576
  3.5 4.0 %collective-permute-start = (f32[3,4,2,8,128]{4,3,2,1,0:T(8,128)}, f32[3,4,2,8,128]{4,3,2,1,0:T(8,128)S(1)}, u32[]{:S(2)}, u32[]{:S(2)}) collective-permute-start(f32[3,4,2,8,128]{4,3,2,1,0:T(8,128)} %get-tuple-element.23), channel_id=1, source_target_pairs={{0,1},{1,2},{2,3},{3,4},{4,5},{5,6},{6,7},{7,8},{8,9},{9,10},{10,1... | collective-permute-start | bytes 294920 | tf_op jit(solution)/shard_map/ppermute | solution.py:589
  7.6 5.6 %collective-permute-start.1 = (f32[3,4,2,8,128]{4,3,2,1,0:T(8,128)}, f32[3,4,2,8,128]{4,3,2,1,0:T(8,128)S(1)}, u32[]{:S(2)}, u32[]{:S(2)}) collective-permute-start(f32[3,4,2,8,128]{4,3,2,1,0:T(8,128)} %get-tuple-element.24), channel_id=1, source_target_pairs={{0,15},{1,0},{2,1},{3,2},{4,3},{5,4},{6,5},{7,6},{8,7},{9,8},{10,9... | collective-permute-start | bytes 294920 | tf_op jit(solution)/shard_map/ppermute | solution.py:589
  13.1 0.0 copy-start
  13.1 0.9 %copy-done = f32[3,8,2,8,128]{4,3,2,1,0:T(8,128)S(1)} copy-done((f32[3,8,2,8,128]{4,3,2,1,0:T(8,128)S(1)}, f32[3,8,2,8,128]{4,3,2,1,0:T(8,128)}, u32[]{:S(2)}) %copy-start) | copy-done | bytes 196632
  14.1 0.1 shard_map.51
  14.2 0.0 collective-permute-done.left_ref
  14.2 0.9 %collective-permute-done.1.right_ref = f32[3,4,2,8,128]{4,3,2,1,0:T(8,128)S(1)} collective-permute-done((f32[3,4,2,8,128]{4,3,2,1,0:T(8,128)}, f32[3,4,2,8,128]{4,3,2,1,0:T(8,128)S(1)}, u32[]{:S(2)}, u32[]{:S(2)}) %collective-permute-start.1) | collective-permute-done | bytes 98336 | tf_op jit(solution)/shard_map/ppermute | solution.py:589
  15.1 0.1 shard_map.52
  15.2 3.2 %collective-permute-start.2 = (f32[10,8,256]{2,1,0:T(8,128)S(1)}, f32[10,8,256]{2,1,0:T(8,128)S(1)}, u32[]{:S(2)}, u32[]{:S(2)}) collective-permute-start(f32[10,8,256]{2,1,0:T(8,128)S(1)} %get-tuple-element.25), channel_id=1, source_target_pairs={{0,16},{16,32},{32,48},{48,64},{64,80},{80,96},{96,112},{112,128},... | collective-permute-start | bytes 245768 | tf_op jit(solution)/shard_map/ppermute | solution.py:589
  18.4 3.9 %collective-permute-start.3 = (f32[10,8,256]{2,1,0:T(8,128)S(1)}, f32[10,8,256]{2,1,0:T(8,128)S(1)}, u32[]{:S(2)}, u32[]{:S(2)}) collective-permute-start(f32[10,8,256]{2,1,0:T(8,128)S(1)} %get-tuple-element.27), channel_id=1, source_target_pairs={{0,496},{16,0},{32,16},{48,32},{64,48},{80,64},{96,80},{112,96},{1... | collective-permute-start | bytes 245768 | tf_op jit(solution)/shard_map/ppermute | solution.py:589
  22.3 0.7 collective-permute-done.2.left_ref
  23.0 0.2 collective-permute-done.3.right_ref
  23.2 0.8 shard_map.53
  24.0 4.1 %collective-permute-start.6 = (f32[8,2,8,256]{3,2,1,0:T(8,128)S(1)}, f32[8,2,8,256]{3,2,1,0:T(8,128)S(1)}, u32[]{:S(2)}, u32[]{:S(2)}) collective-permute-start(f32[8,2,8,256]{3,2,1,0:T(8,128)S(1)} %get-tuple-element.29.mid_ref.refs_2_), channel_id=1, source_target_pairs={{0,496},{16,0},{32,16},{48,32},{64,48},{80,64},{96,80},{112,96},{1... | collective-permute-start | bytes 393224 | tf_op jit(solution)/shard_map/ppermute | solution.py:589
  28.1 0.0 collective-permute-start.4
  28.1 1.0 %collective-permute-done.6.right_ref.refs_3_ = f32[8,2,8,256]{3,2,1,0:T(8,128)S(1)} collective-permute-done((f32[8,2,8,256]{3,2,1,0:T(8,128)S(1)}, f32[8,2,8,256]{3,2,1,0:T(8,128)S(1)}, u32[]{:S(2)}, u32[]{:S(2)}) %collective-permute-start.6) | collective-permute-done | bytes 131104 | tf_op jit(solution)/shard_map/ppermute | solution.py:589
  29.1 4.5 %collective-permute-start.7 = (f32[8,2,8,256]{3,2,1,0:T(8,128)S(1)}, f32[8,2,8,256]{3,2,1,0:T(8,128)S(1)}, u32[]{:S(2)}, u32[]{:S(2)}) collective-permute-start(f32[8,2,8,256]{3,2,1,0:T(8,128)S(1)} %collective-permute-done.6.right_ref.refs_3_), channel_id=1, source_target_pairs={{0,496},{16,0},{32,16},{48,32},{64,48},{80,64},{96,80},{112,96},{1... | collective-permute-start | bytes 393224 | tf_op jit(solution)/shard_map/ppermute | solution.py:589
  33.6 0.0 collective-permute-done.4.left_ref.refs_1_
  33.6 0.0 collective-permute-start.5
  33.6 1.9 %shard_map.54 = (f32[3,8,10,8,256]{4,3,2,1,0:T(8,128)S(1)}, f32[3,8,10,8,256]{4,3,2,1,0:T(8,128)S(1)}, f32[9,8,256]{2,1,0:T(8,128)S(1)}) custom-call(f32[8,2,8,256]{3,2,1,0:T(8,128)S(1)} %collective-permute-done.4.left_ref.refs_1_, f32[8,2,8,256]{3,2,1,0:T(8,128)S(1)} %get-tuple-element.29.mid_ref.refs_2_, ...), custom_call_target="tpu_custom_call" | custom-call | flops 5000000 | bytes 4000000 | tf_op jit(solution)/shard_map/pallas_call | solution.py:576
  35.5 0.0 collective-permute-done.7.refs_4_
  35.5 2.0 %collective-permute-done.5.refs_0_ = f32[8,2,8,256]{3,2,1,0:T(8,128)S(1)} collective-permute-done((f32[8,2,8,256]{3,2,1,0:T(8,128)S(1)}, f32[8,2,8,256]{3,2,1,0:T(8,128)S(1)}, u32[]{:S(2)}, u32[]{:S(2)}) %collective-permute-start.5) | collective-permute-done | bytes 131104 | tf_op jit(solution)/shard_map/ppermute | solution.py:589
  37.5 2.9 %shard_map.55 = (f32[2,8,4,8,256]{4,3,2,1,0:T(8,128)S(1)}, f32[16,8,128]{2,1,0:T(8,128)S(1)}) custom-call(f32[8,2,8,256]{3,2,1,0:T(8,128)S(1)} %collective-permute-done.5.refs_0_, f32[8,2,8,256]{3,2,1,0:T(8,128)S(1)} %collective-permute-done.4.left_ref.refs_1_, f32[8,2,8,256]{3,2,1,0:T(8,128)S(1)} %get-tuple-element.29.mid_ref.refs_2_, ...), custom_call_target="tpu_custom_call" | custom-call | tf_op jit(solution)/shard_map/pallas_call | solution.py:576
  40.4 22.9 %all_to_all.10 = f32[16,8,128]{2,1,0:T(8,128)S(1)} all-to-all(f32[16,8,128]{2,1,0:T(8,128)S(1)} %get-tuple-element.34), channel_id=1, replica_groups={{0,32,64,96,128,160,192,224,256,288,320,352,384,416,448,480},{16,48,80,..., dimensions={0} | all-to-all | bytes 131072 | tf_op jit(solution)/shard_map/all_to_all | solution.py:595
  63.3 13.0 %all_to_all.11 = f32[16,8,128]{2,1,0:T(8,128)S(1)} all-to-all(f32[16,8,128]{2,1,0:T(8,128)S(1)} %broadcast_in_dim.2), channel_id=1, replica_groups=mesh['gx'=32,'gy'=16] {'gy'}, dimensions={0} | all-to-all | bytes 131072 | tf_op jit(solution)/shard_map/all_to_all | solution.py:597
  76.4 7.2 %all_gather.3.m_ref = f32[32,8,128]{2,1,0:T(8,128)S(1)} all-gather(f32[16,8,128]{2,1,0:T(8,128)S(1)} %all_to_all.11), channel_id=1, replica_groups={{0,16},{32,48},{64,80},{96,112},{128,144},{160,176},{192,208},{224,240}..., dimensions={0}, use_global_device_ids=true | all-gather | bytes 196608 | tf_op jit(solution)/shard_map/all_gather | solution.py:599
  83.5 1.3 %shard_map.56 = (f32[3,8,2,8,128]{4,3,2,1,0:T(8,128)}, f32[8,2,8,128]{3,2,1,0:T(8,128)}) custom-call(f32[32,8,128]{2,1,0:T(8,128)S(1)} %all_gather.3.m_ref, f32[3,8,10,8,256]{4,3,2,1,0:T(8,128)S(1)} %get-tuple-element.31.refs_5_.low_ref, f32[2,8,4,8,256]{4,3,2,1,0:T(8,128)S(1)} %get-tuple-element.35.high_ref, ...), custom_call_target="tpu_custom_call" | custom-call | tf_op jit(solution)/shard_map/pallas_call | solution.py:576
  (2 shorter events, 0.0 us)
Async XLA Ops:
  3.5 10.6 %collective-permute-start = (f32[3,4,2,8,128]{4,3,2,1,0:T(8,128)}, f32[3,4,2,8,128]{4,3,2,1,0:T(8,128)S(1)}, u32[]{:S(2)}, u32[]{:S(2)}) collective-permute-start(f32[3,4,2,8,128]{4,3,2,1,0:T(8,128)} %get-tuple-element.23), channel_id=1, source_target_pairs={{0,1},{1,2},{2,3},{3,4},{4,5},{5,6},{6,7},{7,8},{8,9},{9,10},{10,1... | collective-permute-start | bytes 294920 | tf_op jit(solution)/shard_map/ppermute | solution.py:589
  7.6 7.5 %collective-permute-start.1 = (f32[3,4,2,8,128]{4,3,2,1,0:T(8,128)}, f32[3,4,2,8,128]{4,3,2,1,0:T(8,128)S(1)}, u32[]{:S(2)}, u32[]{:S(2)}) collective-permute-start(f32[3,4,2,8,128]{4,3,2,1,0:T(8,128)} %get-tuple-element.24), channel_id=1, source_target_pairs={{0,15},{1,0},{2,1},{3,2},{4,3},{5,4},{6,5},{7,6},{8,7},{9,8},{10,9... | collective-permute-start | bytes 294920 | tf_op jit(solution)/shard_map/ppermute | solution.py:589
  13.1 0.9 %copy-start = (f32[3,8,2,8,128]{4,3,2,1,0:T(8,128)S(1)}, f32[3,8,2,8,128]{4,3,2,1,0:T(8,128)}, u32[]{:S(2)}) copy-start(f32[3,8,2,8,128]{4,3,2,1,0:T(8,128)} %get-tuple-element.21.r_ref) | copy-start | bytes 589828
  15.2 7.8 %collective-permute-start.2 = (f32[10,8,256]{2,1,0:T(8,128)S(1)}, f32[10,8,256]{2,1,0:T(8,128)S(1)}, u32[]{:S(2)}, u32[]{:S(2)}) collective-permute-start(f32[10,8,256]{2,1,0:T(8,128)S(1)} %get-tuple-element.25), channel_id=1, source_target_pairs={{0,16},{16,32},{32,48},{48,64},{64,80},{80,96},{96,112},{112,128},... | collective-permute-start | bytes 245768 | tf_op jit(solution)/shard_map/ppermute | solution.py:589
  18.4 4.8 %collective-permute-start.3 = (f32[10,8,256]{2,1,0:T(8,128)S(1)}, f32[10,8,256]{2,1,0:T(8,128)S(1)}, u32[]{:S(2)}, u32[]{:S(2)}) collective-permute-start(f32[10,8,256]{2,1,0:T(8,128)S(1)} %get-tuple-element.27), channel_id=1, source_target_pairs={{0,496},{16,0},{32,16},{48,32},{64,48},{80,64},{96,80},{112,96},{1... | collective-permute-start | bytes 245768 | tf_op jit(solution)/shard_map/ppermute | solution.py:589
  24.0 5.1 %collective-permute-start.6 = (f32[8,2,8,256]{3,2,1,0:T(8,128)S(1)}, f32[8,2,8,256]{3,2,1,0:T(8,128)S(1)}, u32[]{:S(2)}, u32[]{:S(2)}) collective-permute-start(f32[8,2,8,256]{3,2,1,0:T(8,128)S(1)} %get-tuple-element.29.mid_ref.refs_2_), channel_id=1, source_target_pairs={{0,496},{16,0},{32,16},{48,32},{64,48},{80,64},{96,80},{112,96},{1... | collective-permute-start | bytes 393224 | tf_op jit(solution)/shard_map/ppermute | solution.py:589
  28.1 5.5 %collective-permute-start.4 = (f32[8,2,8,256]{3,2,1,0:T(8,128)S(1)}, f32[8,2,8,256]{3,2,1,0:T(8,128)S(1)}, u32[]{:S(2)}, u32[]{:S(2)}) collective-permute-start(f32[8,2,8,256]{3,2,1,0:T(8,128)S(1)} %get-tuple-element.29.mid_ref.refs_2_), channel_id=1, source_target_pairs={{0,16},{16,32},{32,48},{48,64},{64,80},{80,96},{96,112},{112,128},... | collective-permute-start | bytes 393224 | tf_op jit(solution)/shard_map/ppermute | solution.py:589
  29.1 6.4 %collective-permute-start.7 = (f32[8,2,8,256]{3,2,1,0:T(8,128)S(1)}, f32[8,2,8,256]{3,2,1,0:T(8,128)S(1)}, u32[]{:S(2)}, u32[]{:S(2)}) collective-permute-start(f32[8,2,8,256]{3,2,1,0:T(8,128)S(1)} %collective-permute-done.6.right_ref.refs_3_), channel_id=1, source_target_pairs={{0,496},{16,0},{32,16},{48,32},{64,48},{80,64},{96,80},{112,96},{1... | collective-permute-start | bytes 393224 | tf_op jit(solution)/shard_map/ppermute | solution.py:589
  33.6 3.9 %collective-permute-start.5 = (f32[8,2,8,256]{3,2,1,0:T(8,128)S(1)}, f32[8,2,8,256]{3,2,1,0:T(8,128)S(1)}, u32[]{:S(2)}, u32[]{:S(2)}) collective-permute-start(f32[8,2,8,256]{3,2,1,0:T(8,128)S(1)} %collective-permute-done.4.left_ref.refs_1_), channel_id=1, source_target_pairs={{0,16},{16,32},{32,48},{48,64},{64,80},{80,96},{96,112},{112,128},... | collective-permute-start | bytes 393224 | tf_op jit(solution)/shard_map/ppermute | solution.py:589

commit v5 on v4

--- a/solution.py
+++ b/solution.py
@@ -580,7 +580,7 @@
         out_specs=jax.tree.map(lambda s: pl.BlockSpec(memory_space=pltpu.VMEM), out_shape),
         scratch_shapes=scratch,
         cost_estimate=cost,
-        compiler_params=pltpu.CompilerParams(vmem_limit_bytes=vmem * 2**20),
+        compiler_params=pltpu.CompilerParams(vmem_limit_bytes=int(vmem * 2**20)),
     )(*args)
 
 
@@ -591,12 +591,11 @@
 
 def total_rows(packed):
     nx, ny = lax.axis_size("gx"), lax.axis_size("gy")
+    planes = [[(2 * z + c) * ny + y for y in range(ny) for c in range(2)] for z in range(nx // 2)]
+    part = lax.all_to_all(packed, ("gx", "gy"), 0, 0, axis_index_groups=planes, tiled=True)
+    part = jnp.broadcast_to(jnp.sum(part, axis=0, keepdims=True), (nx // 2, 8, 128))
     along = [[2 * z + c for z in range(nx // 2)] for c in range(2)]
-    part = lax.all_to_all(packed, "gx", 0, 0, axis_index_groups=along, tiled=True)
-    part = jnp.broadcast_to(jnp.sum(part, axis=0, keepdims=True), (ny, 8, 128))
-    part = lax.all_to_all(part, "gy", 0, 0, tiled=True)
-    pairs = [[i, i + 1] for i in range(0, nx, 2)]
-    return lax.all_gather(part, "gx", axis_index_groups=pairs, tiled=True)
+    return lax.all_to_all(part, "gx", 0, 0, axis_index_groups=along, tiled=True)
 
 
 def local(adjoint, checkpoints, wall_faces):
@@ -654,7 +653,7 @@
     )
     high, packed = call(
         outer_kernel,
-        (shape(2, 8, 4, 8, 256), shape(lax.axis_size("gx") // 2, 8, 128)),
+        (shape(2, 8, 4, 8, 256), shape(2 * lax.axis_size("gy"), 8, 128)),
         [
             vm((4, 8, 10, 8, 256), f32),
             vm((4, 8, 10, 8, 256), f32),

time: 85.1 us -> 82.2 us (0.966)
  blocking collectives: 43.1 us -> 40.3 us
    all_gather x1 -> x0, blocking collectives: 7.19 us -> none  [total_rows(): return lax.all_gather(part, 'gx', axis_index_groups=pairs, tiled=True)]
    all_to_all x2, blocking collectives: 35.9 us -> 40.3 us  [the longest x1 20.9 us: total_rows(): return lax.all_to_all(part, 'gx', 0, 0, axis_index_groups=along, tiled=True)]
where the time goes in v5:
time: 82.2 us; the launch traced here: 82 us
  blocking collectives  40.3 us (49%)
  starting transfers between devices  25.3 us (31%)
  Pallas kernels  9.97 us (12%)
  waiting for transfers between devices  4.78 us (6%)
  local copies, waits for them, and re-layouts  0.93 us (1%)
    ppermute x8, starting transfers between devices, shift(): lax.ppermute(value, axis, [(i, (i + by) % size) for i in range(size)])  25.3 us
    all_to_all x1, blocking collectives, total_rows(): return lax.all_to_all(part, 'gx', 0, 0, axis_index_groups=along, tiled=True)  20.9 us
    all_to_all x1, blocking collectives, total_rows(): lax.all_to_all(packed, ('gx', 'gy'), 0, 0, axis_index_groups=planes, tile...  19.3 us
    pallas_call x7, Pallas kernels, call(): pl.pallas_call(kernel, out_shape=out_shape, in_specs=[pl.BlockSpec(memory...  9.97 us
    ppermute x8, waiting for transfers between devices, shift(): lax.ppermute(value, axis, [(i, (i + by) % size) for i in range(size)])  4.78 us
  transfers between devices with their start and end apart: 8, of which 5 were waited for; matrix products, arithmetic and copies ran while one was open for 0% of the time, Pallas kernels for 2%

profile of v5, /device:TPU:1, one launch (start us, length us, event | category | flops | bytes accessed | tf_op | source)
XLA Modules:
  0.0 82.0 jit_solution(7546846097119173464)
XLA Ops:
  0.6 2.9 %shard_map.50 = (f32[3,8,2,8,128]{4,3,2,1,0:T(8,128)}, f32[3,4,2,8,128]{4,3,2,1,0:T(8,128)}, f32[3,4,2,8,128]{4,3,2,1,0:T(8,128)}) custom-call(f32[3,8,2,8,128]{4,3,2,1,0:T(8,128)} %bitcast.4, bf16[3,8,16,128]{3,2,1,0:T(8,128)(2,1)} %bitcast.5, s32[2,2,16]{2,1,0:T(2,128)} %faces_hbm.1), custom_call_target="tpu_custom_call" | custom-call | tf_op jit(solution)/shard_map/pallas_call | solution.py:576
  3.5 4.0 %collective-permute-start = (f32[3,4,2,8,128]{4,3,2,1,0:T(8,128)}, f32[3,4,2,8,128]{4,3,2,1,0:T(8,128)S(1)}, u32[]{:S(2)}, u32[]{:S(2)}) collective-permute-start(f32[3,4,2,8,128]{4,3,2,1,0:T(8,128)} %get-tuple-element.23), channel_id=1, source_target_pairs={{0,1},{1,2},{2,3},{3,4},{4,5},{5,6},{6,7},{7,8},{8,9},{9,10},{10,1... | collective-permute-start | bytes 294920 | tf_op jit(solution)/shard_map/ppermute | solution.py:589
  7.6 5.6 %collective-permute-start.1 = (f32[3,4,2,8,128]{4,3,2,1,0:T(8,128)}, f32[3,4,2,8,128]{4,3,2,1,0:T(8,128)S(1)}, u32[]{:S(2)}, u32[]{:S(2)}) collective-permute-start(f32[3,4,2,8,128]{4,3,2,1,0:T(8,128)} %get-tuple-element.24), channel_id=1, source_target_pairs={{0,15},{1,0},{2,1},{3,2},{4,3},{5,4},{6,5},{7,6},{8,7},{9,8},{10,9... | collective-permute-start | bytes 294920 | tf_op jit(solution)/shard_map/ppermute | solution.py:589
  13.1 0.0 copy-start
  13.1 0.9 %copy-done = f32[3,8,2,8,128]{4,3,2,1,0:T(8,128)S(1)} copy-done((f32[3,8,2,8,128]{4,3,2,1,0:T(8,128)S(1)}, f32[3,8,2,8,128]{4,3,2,1,0:T(8,128)}, u32[]{:S(2)}) %copy-start) | copy-done | bytes 196632
  14.1 0.1 shard_map.51
  14.2 0.0 collective-permute-done.left_ref
  14.2 0.9 %collective-permute-done.1.right_ref = f32[3,4,2,8,128]{4,3,2,1,0:T(8,128)S(1)} collective-permute-done((f32[3,4,2,8,128]{4,3,2,1,0:T(8,128)}, f32[3,4,2,8,128]{4,3,2,1,0:T(8,128)S(1)}, u32[]{:S(2)}, u32[]{:S(2)}) %collective-permute-start.1) | collective-permute-done | bytes 98336 | tf_op jit(solution)/shard_map/ppermute | solution.py:589
  15.1 0.1 shard_map.52
  15.2 3.2 %collective-permute-start.2 = (f32[10,8,256]{2,1,0:T(8,128)S(1)}, f32[10,8,256]{2,1,0:T(8,128)S(1)}, u32[]{:S(2)}, u32[]{:S(2)}) collective-permute-start(f32[10,8,256]{2,1,0:T(8,128)S(1)} %get-tuple-element.25), channel_id=1, source_target_pairs={{0,16},{16,32},{32,48},{48,64},{64,80},{80,96},{96,112},{112,128},... | collective-permute-start | bytes 245768 | tf_op jit(solution)/shard_map/ppermute | solution.py:589
  18.4 3.9 %collective-permute-start.3 = (f32[10,8,256]{2,1,0:T(8,128)S(1)}, f32[10,8,256]{2,1,0:T(8,128)S(1)}, u32[]{:S(2)}, u32[]{:S(2)}) collective-permute-start(f32[10,8,256]{2,1,0:T(8,128)S(1)} %get-tuple-element.27), channel_id=1, source_target_pairs={{0,496},{16,0},{32,16},{48,32},{64,48},{80,64},{96,80},{112,96},{1... | collective-permute-start | bytes 245768 | tf_op jit(solution)/shard_map/ppermute | solution.py:589
  22.3 0.7 collective-permute-done.2.left_ref
  23.0 0.2 collective-permute-done.3.right_ref
  23.2 0.8 shard_map.53
  24.0 4.1 %collective-permute-start.6 = (f32[8,2,8,256]{3,2,1,0:T(8,128)S(1)}, f32[8,2,8,256]{3,2,1,0:T(8,128)S(1)}, u32[]{:S(2)}, u32[]{:S(2)}) collective-permute-start(f32[8,2,8,256]{3,2,1,0:T(8,128)S(1)} %get-tuple-element.29.mid_ref.refs_2_), channel_id=1, source_target_pairs={{0,496},{16,0},{32,16},{48,32},{64,48},{80,64},{96,80},{112,96},{1... | collective-permute-start | bytes 393224 | tf_op jit(solution)/shard_map/ppermute | solution.py:589
  28.1 0.0 collective-permute-start.4
  28.1 1.0 %collective-permute-done.6.right_ref.refs_3_ = f32[8,2,8,256]{3,2,1,0:T(8,128)S(1)} collective-permute-done((f32[8,2,8,256]{3,2,1,0:T(8,128)S(1)}, f32[8,2,8,256]{3,2,1,0:T(8,128)S(1)}, u32[]{:S(2)}, u32[]{:S(2)}) %collective-permute-start.6) | collective-permute-done | bytes 131104 | tf_op jit(solution)/shard_map/ppermute | solution.py:589
  29.1 4.5 %collective-permute-start.7 = (f32[8,2,8,256]{3,2,1,0:T(8,128)S(1)}, f32[8,2,8,256]{3,2,1,0:T(8,128)S(1)}, u32[]{:S(2)}, u32[]{:S(2)}) collective-permute-start(f32[8,2,8,256]{3,2,1,0:T(8,128)S(1)} %collective-permute-done.6.right_ref.refs_3_), channel_id=1, source_target_pairs={{0,496},{16,0},{32,16},{48,32},{64,48},{80,64},{96,80},{112,96},{1... | collective-permute-start | bytes 393224 | tf_op jit(solution)/shard_map/ppermute | solution.py:589
  33.6 0.0 collective-permute-done.4.left_ref.refs_1_
  33.6 0.0 collective-permute-start.5
  33.6 1.9 %shard_map.54 = (f32[3,8,10,8,256]{4,3,2,1,0:T(8,128)S(1)}, f32[3,8,10,8,256]{4,3,2,1,0:T(8,128)S(1)}, f32[9,8,256]{2,1,0:T(8,128)S(1)}) custom-call(f32[8,2,8,256]{3,2,1,0:T(8,128)S(1)} %collective-permute-done.4.left_ref.refs_1_, f32[8,2,8,256]{3,2,1,0:T(8,128)S(1)} %get-tuple-element.29.mid_ref.refs_2_, ...), custom_call_target="tpu_custom_call" | custom-call | flops 5000000 | bytes 4000000 | tf_op jit(solution)/shard_map/pallas_call | solution.py:576
  35.5 0.0 collective-permute-done.7.refs_4_
  35.5 2.0 %collective-permute-done.5.refs_0_ = f32[8,2,8,256]{3,2,1,0:T(8,128)S(1)} collective-permute-done((f32[8,2,8,256]{3,2,1,0:T(8,128)S(1)}, f32[8,2,8,256]{3,2,1,0:T(8,128)S(1)}, u32[]{:S(2)}, u32[]{:S(2)}) %collective-permute-start.5) | collective-permute-done | bytes 131104 | tf_op jit(solution)/shard_map/ppermute | solution.py:589
  37.5 2.9 %shard_map.55 = (f32[2,8,4,8,256]{4,3,2,1,0:T(8,128)S(1)}, f32[32,8,128]{2,1,0:T(8,128)S(1)}) custom-call(f32[8,2,8,256]{3,2,1,0:T(8,128)S(1)} %collective-permute-done.5.refs_0_, f32[8,2,8,256]{3,2,1,0:T(8,128)S(1)} %collective-permute-done.4.left_ref.refs_1_, f32[8,2,8,256]{3,2,1,0:T(8,128)S(1)} %get-tuple-element.29.mid_ref.refs_2_, ...), custom_call_target="tpu_custom_call" | custom-call | tf_op jit(solution)/shard_map/pallas_call | solution.py:576
  40.4 19.3 %all_to_all.10 = f32[32,8,128]{2,1,0:T(8,128)S(1)} all-to-all(f32[32,8,128]{2,1,0:T(8,128)S(1)} %get-tuple-element.34), channel_id=1, replica_groups={{0,16,1,17,2,18,3,19,4,20,5,21,6,22,7,23,8,24,9,25,10,26,11,27,12,28,13..., dimensions={0} | all-to-all | bytes 262144 | tf_op jit(solution)/shard_map/all_to_all | solution.py:595
  59.8 20.9 %all_to_all.11.m_ref = f32[16,8,128]{2,1,0:T(8,128)S(1)} all-to-all(f32[16,8,128]{2,1,0:T(8,128)S(1)} %broadcast_in_dim.2), channel_id=1, replica_groups={{0,32,64,96,128,160,192,224,256,288,320,352,384,416,448,480},{16,48,80,..., dimensions={0} | all-to-all | bytes 131072 | tf_op jit(solution)/shard_map/all_to_all | solution.py:598
  80.7 1.3 %shard_map.56 = (f32[3,8,2,8,128]{4,3,2,1,0:T(8,128)}, f32[8,2,8,128]{3,2,1,0:T(8,128)}) custom-call(f32[16,8,128]{2,1,0:T(8,128)S(1)} %all_to_all.11.m_ref, f32[3,8,10,8,256]{4,3,2,1,0:T(8,128)S(1)} %get-tuple-element.31.refs_5_.low_ref, f32[2,8,4,8,256]{4,3,2,1,0:T(8,128)S(1)} %get-tuple-element.35.high_ref, ...), custom_call_target="tpu_custom_call" | custom-call | tf_op jit(solution)/shard_map/pallas_call | solution.py:576
  (2 shorter events, 0.0 us)
Async XLA Ops:
  3.5 10.6 %collective-permute-start = (f32[3,4,2,8,128]{4,3,2,1,0:T(8,128)}, f32[3,4,2,8,128]{4,3,2,1,0:T(8,128)S(1)}, u32[]{:S(2)}, u32[]{:S(2)}) collective-permute-start(f32[3,4,2,8,128]{4,3,2,1,0:T(8,128)} %get-tuple-element.23), channel_id=1, source_target_pairs={{0,1},{1,2},{2,3},{3,4},{4,5},{5,6},{6,7},{7,8},{8,9},{9,10},{10,1... | collective-permute-start | bytes 294920 | tf_op jit(solution)/shard_map/ppermute | solution.py:589
  7.6 7.5 %collective-permute-start.1 = (f32[3,4,2,8,128]{4,3,2,1,0:T(8,128)}, f32[3,4,2,8,128]{4,3,2,1,0:T(8,128)S(1)}, u32[]{:S(2)}, u32[]{:S(2)}) collective-permute-start(f32[3,4,2,8,128]{4,3,2,1,0:T(8,128)} %get-tuple-element.24), channel_id=1, source_target_pairs={{0,15},{1,0},{2,1},{3,2},{4,3},{5,4},{6,5},{7,6},{8,7},{9,8},{10,9... | collective-permute-start | bytes 294920 | tf_op jit(solution)/shard_map/ppermute | solution.py:589
  13.1 0.9 %copy-start = (f32[3,8,2,8,128]{4,3,2,1,0:T(8,128)S(1)}, f32[3,8,2,8,128]{4,3,2,1,0:T(8,128)}, u32[]{:S(2)}) copy-start(f32[3,8,2,8,128]{4,3,2,1,0:T(8,128)} %get-tuple-element.21.r_ref) | copy-start | bytes 589828
  15.2 7.8 %collective-permute-start.2 = (f32[10,8,256]{2,1,0:T(8,128)S(1)}, f32[10,8,256]{2,1,0:T(8,128)S(1)}, u32[]{:S(2)}, u32[]{:S(2)}) collective-permute-start(f32[10,8,256]{2,1,0:T(8,128)S(1)} %get-tuple-element.25), channel_id=1, source_target_pairs={{0,16},{16,32},{32,48},{48,64},{64,80},{80,96},{96,112},{112,128},... | collective-permute-start | bytes 245768 | tf_op jit(solution)/shard_map/ppermute | solution.py:589
  18.4 4.8 %collective-permute-start.3 = (f32[10,8,256]{2,1,0:T(8,128)S(1)}, f32[10,8,256]{2,1,0:T(8,128)S(1)}, u32[]{:S(2)}, u32[]{:S(2)}) collective-permute-start(f32[10,8,256]{2,1,0:T(8,128)S(1)} %get-tuple-element.27), channel_id=1, source_target_pairs={{0,496},{16,0},{32,16},{48,32},{64,48},{80,64},{96,80},{112,96},{1... | collective-permute-start | bytes 245768 | tf_op jit(solution)/shard_map/ppermute | solution.py:589
  24.0 5.1 %collective-permute-start.6 = (f32[8,2,8,256]{3,2,1,0:T(8,128)S(1)}, f32[8,2,8,256]{3,2,1,0:T(8,128)S(1)}, u32[]{:S(2)}, u32[]{:S(2)}) collective-permute-start(f32[8,2,8,256]{3,2,1,0:T(8,128)S(1)} %get-tuple-element.29.mid_ref.refs_2_), channel_id=1, source_target_pairs={{0,496},{16,0},{32,16},{48,32},{64,48},{80,64},{96,80},{112,96},{1... | collective-permute-start | bytes 393224 | tf_op jit(solution)/shard_map/ppermute | solution.py:589
  28.1 5.5 %collective-permute-start.4 = (f32[8,2,8,256]{3,2,1,0:T(8,128)S(1)}, f32[8,2,8,256]{3,2,1,0:T(8,128)S(1)}, u32[]{:S(2)}, u32[]{:S(2)}) collective-permute-start(f32[8,2,8,256]{3,2,1,0:T(8,128)S(1)} %get-tuple-element.29.mid_ref.refs_2_), channel_id=1, source_target_pairs={{0,16},{16,32},{32,48},{48,64},{64,80},{80,96},{96,112},{112,128},... | collective-permute-start | bytes 393224 | tf_op jit(solution)/shard_map/ppermute | solution.py:589
  29.1 6.4 %collective-permute-start.7 = (f32[8,2,8,256]{3,2,1,0:T(8,128)S(1)}, f32[8,2,8,256]{3,2,1,0:T(8,128)S(1)}, u32[]{:S(2)}, u32[]{:S(2)}) collective-permute-start(f32[8,2,8,256]{3,2,1,0:T(8,128)S(1)} %collective-permute-done.6.right_ref.refs_3_), channel_id=1, source_target_pairs={{0,496},{16,0},{32,16},{48,32},{64,48},{80,64},{96,80},{112,96},{1... | collective-permute-start | bytes 393224 | tf_op jit(solution)/shard_map/ppermute | solution.py:589
  33.6 3.9 %collective-permute-start.5 = (f32[8,2,8,256]{3,2,1,0:T(8,128)S(1)}, f32[8,2,8,256]{3,2,1,0:T(8,128)S(1)}, u32[]{:S(2)}, u32[]{:S(2)}) collective-permute-start(f32[8,2,8,256]{3,2,1,0:T(8,128)S(1)} %collective-permute-done.4.left_ref.refs_1_), channel_id=1, source_target_pairs={{0,16},{16,32},{32,48},{48,64},{64,80},{80,96},{96,112},{112,128},... | collective-permute-start | bytes 393224 | tf_op jit(solution)/shard_map/ppermute | solution.py:589

commit v6 on v5

--- a/solution.py
+++ b/solution.py
@@ -194,7 +194,7 @@
     kcoef = row_coefs(lanes, scaled_stiff)
     wxy = node_x(lanes, node_weights) * node_y(lanes, node_weights)
     rim = rim_mask(lanes)
-    half = iota(lanes, 1) < 64
+    lane = iota(lanes, 1)
     for move in moves:
         move.wait()
     for face, wide in enumerate(expand_walls(faces_ref)):
@@ -219,6 +219,7 @@
             stretch[0] = stretch[0] + v[j] * weigh(row_turns(u[j]), dcoef)
             stretch[1] = stretch[1] + v[j] * udy[8 * j : 8 * j + 8]
             stretch[2] = stretch[2] + v[j] * z_slope(u[j])
+        ups, downs = [None] * 8, [None] * 8
         for i in range(3):
             turns = row_turns(v[i])
             planes = [v[i][z] for z in range(8)]
@@ -241,9 +242,19 @@
                     out = jnp.where(rim, wall_ref[z // 7, e], out)
                 r_ref[i, z, e] = out
                 made.append(out)
-            for z in range(4):
-                up_ref[i, z, e] = jnp.where(half, pltpu.roll(made[z], 64, axis=1), made[z + 4])
-                down_ref[i, z, e] = jnp.where(half, made[z], pltpu.roll(made[z + 4], 64, axis=1))
+            for z in range(8):
+                up, down = made[z], made[z]
+                if 0 < z < 7:
+                    up = up + jnp.where(lane == 88, pltpu.roll(up, 1, axis=1), 0.0)
+                    down = down + jnp.where(lane == 39, pltpu.roll(down, 127, axis=1), 0.0)
+                up = pltpu.roll(up, (40 * i - 88) % 128, axis=1)
+                down = pltpu.roll(down, 40 * i, axis=1) if i else down
+                here = (lane >= 40 * i) & (lane < 40 * i + 40)
+                ups[z] = up if i == 0 else jnp.where(here, up, ups[z])
+                downs[z] = down if i == 0 else jnp.where(here, down, downs[z])
+        for z in range(8):
+            up_ref[z, e] = ups[z]
+            down_ref[z, e] = downs[z]
         return carry
 
     lax.fori_loop(0, 2, body, 0)
@@ -259,7 +270,8 @@
 
 
 def join_kernel(r_ref, left_ref, right_ref, e_ref, up_ref, down_ref):
-    half = iota(128, 1) < 64
+    lane = iota(128, 1)
+    half = lane < 64
     place = iota(256, 0)
     first = place == 0
     last = place == 7
@@ -270,14 +282,14 @@
             tiles = []
             for e in range(2):
                 turned = r_ref[c, z, e]
-                left = left_ref[c, z % 4, e]
-                right = right_ref[c, z % 4, e]
-                if z >= 4:
-                    left = pltpu.roll(left, 64, axis=1)
-                else:
-                    right = pltpu.roll(right, 64, axis=1)
+                left = pltpu.roll(left_ref[z, e], (24 - 40 * c) % 128, axis=1)
+                right = pltpu.roll(right_ref[z, e], (64 - 40 * c) % 128, axis=1)
                 tile = jnp.concatenate(
-                    [jnp.where(half, left, turned), jnp.where(half, turned, right)], axis=1
+                    [
+                        jnp.where(half, jnp.where(lane >= 24, left, 0.0), turned),
+                        jnp.where(half, turned, jnp.where(lane < 104, right, 0.0)),
+                    ],
+                    axis=1,
                 )
                 e_ref[c, z, e] = tile
                 tiles.append(tile)
@@ -423,7 +435,10 @@
 
 
 def over(low, high, body):
-    lax.fori_loop(low, high, lambda e, c: (body(e), c)[1], 0, unroll=2)
+    count = high - low
+    lax.fori_loop(
+        low, high, lambda e, c: (body(e), c)[1], 0, unroll=count if count <= 4 else count // 2
+    )
 
 
 def sides(low, body):
@@ -494,8 +509,7 @@
         part = part[:, :128] + part[:, 128:]
         total = jnp.sum(jnp.sum(part, axis=0, keepdims=True), axis=1, keepdims=True)
         packed = jnp.where(lane == k, total, packed)
-    for k in range(m_out.shape[0]):
-        m_out[k] = packed
+    m_out[...] = packed
 
 
 def final_kernel(m_ref, low_ref, high_ref, w_ref, open_ref, dy_ref, out_ref, q_ref):
@@ -591,8 +605,10 @@
 
 def total_rows(packed):
     nx, ny = lax.axis_size("gx"), lax.axis_size("gy")
-    planes = [[(2 * z + c) * ny + y for y in range(ny) for c in range(2)] for z in range(nx // 2)]
-    part = lax.all_to_all(packed, ("gx", "gy"), 0, 0, axis_index_groups=planes, tiled=True)
+    pairs = [[i, i + 1] for i in range(0, nx, 2)]
+    part = lax.all_gather(packed, "gx", axis_index_groups=pairs)
+    part = jnp.broadcast_to(jnp.sum(part, axis=0, keepdims=True), (ny, 8, 128))
+    part = lax.all_to_all(part, "gy", 0, 0, tiled=True)
     part = jnp.broadcast_to(jnp.sum(part, axis=0, keepdims=True), (nx // 2, 8, 128))
     along = [[2 * z + c for z in range(nx // 2)] for c in range(2)]
     return lax.all_to_all(part, "gx", 0, 0, axis_index_groups=along, tiled=True)
@@ -603,7 +619,7 @@
     flow = checkpoints.reshape(3, 8, 16, 128)
     vm = pltpu.VMEM
     table = jax.ShapeDtypeStruct((256, 256), bf16)
-    strip = shape(3, 4, 2, 8, 128)
+    strip = shape(8, 2, 8, 128)
     rhs, up, down = call(
         rhs_kernel,
         (shape(3, 8, 2, 8, 128), strip, strip),
@@ -653,7 +669,7 @@
     )
     high, packed = call(
         outer_kernel,
-        (shape(2, 8, 4, 8, 256), shape(2 * lax.axis_size("gy"), 8, 128)),
+        (shape(2, 8, 4, 8, 256), shape(8, 128)),
         [
             vm((4, 8, 10, 8, 256), f32),
             vm((4, 8, 10, 8, 256), f32),

time: 82.2 us -> 81.7 us (level); the launches traced: 82 us -> 80.6 us
  Pallas kernels: 9.97 us -> 8.7 us
    all_to_all x1, blocking collectives: 19.3 us -> 13 us  [total_rows(): part = lax.all_to_all(part, 'gy', 0, 0, tiled=True)]
    all_gather x0 -> x1, blocking collectives: none -> 6.26 us  [total_rows(): part = lax.all_gather(packed, 'gx', axis_index_groups=pairs)]
    pallas_call x7, Pallas kernels: 9.97 us -> 8.7 us  [call(): pl.pallas_call(kernel, out_shape=out_shape, in_specs=[pl.BlockSpec(memory...]
where the time goes in v6:
time: 81.7 us; the launch traced here: 80.6 us
  blocking collectives  40.2 us (49%)
  starting transfers between devices  25.3 us (31%)
  Pallas kernels  8.7 us (11%)
  waiting for transfers between devices  4.8 us (6%)
  local copies, waits for them, and re-layouts  0.94 us (1%)
    ppermute x8, starting transfers between devices, shift(): lax.ppermute(value, axis, [(i, (i + by) % size) for i in range(size)])  25.3 us
    all_to_all x1, blocking collectives, total_rows(): return lax.all_to_all(part, 'gx', 0, 0, axis_index_groups=along, tiled=True)  20.9 us
    all_to_all x1, blocking collectives, total_rows(): part = lax.all_to_all(part, 'gy', 0, 0, tiled=True)  13 us
    pallas_call x7, Pallas kernels, call(): pl.pallas_call(kernel, out_shape=out_shape, in_specs=[pl.BlockSpec(memory...  8.7 us
    all_gather x1, blocking collectives, total_rows(): part = lax.all_gather(packed, 'gx', axis_index_groups=pairs)  6.26 us
    ppermute x8, waiting for transfers between devices, shift(): lax.ppermute(value, axis, [(i, (i + by) % size) for i in range(size)])  4.8 us
  transfers between devices with their start and end apart: 8, of which 5 were waited for; matrix products, arithmetic and copies ran while one was open for 0% of the time, Pallas kernels for 2%

profile of v6, /device:TPU:1, one launch (start us, length us, event | category | flops | bytes accessed | tf_op | source)
XLA Modules:
  0.0 80.6 jit_solution(6123027473161746284)
XLA Ops:
  0.6 3.0 %shard_map.50 = (f32[3,8,2,8,128]{4,3,2,1,0:T(8,128)}, f32[8,2,8,128]{3,2,1,0:T(8,128)}, f32[8,2,8,128]{3,2,1,0:T(8,128)}) custom-call(f32[3,8,2,8,128]{4,3,2,1,0:T(8,128)} %bitcast.6, bf16[3,8,16,128]{3,2,1,0:T(8,128)(2,1)} %bitcast.7, s32[2,2,16]{2,1,0:T(2,128)} %faces_hbm.1), custom_call_target="tpu_custom_call" | custom-call | tf_op jit(solution)/shard_map/pallas_call | solution.py:590
  3.6 4.0 %collective-permute-start = (f32[8,2,8,128]{3,2,1,0:T(8,128)}, f32[8,2,8,128]{3,2,1,0:T(8,128)S(1)}, u32[]{:S(2)}, u32[]{:S(2)}) collective-permute-start(f32[8,2,8,128]{3,2,1,0:T(8,128)} %get-tuple-element.23), channel_id=1, source_target_pairs={{0,1},{1,2},{2,3},{3,4},{4,5},{5,6},{6,7},{7,8},{8,9},{9,10},{10,1... | collective-permute-start | bytes 196616 | tf_op jit(solution)/shard_map/ppermute | solution.py:603
  7.7 5.6 %collective-permute-start.1 = (f32[8,2,8,128]{3,2,1,0:T(8,128)}, f32[8,2,8,128]{3,2,1,0:T(8,128)S(1)}, u32[]{:S(2)}, u32[]{:S(2)}) collective-permute-start(f32[8,2,8,128]{3,2,1,0:T(8,128)} %get-tuple-element.24), channel_id=1, source_target_pairs={{0,15},{1,0},{2,1},{3,2},{4,3},{5,4},{6,5},{7,6},{8,7},{9,8},{10,9... | collective-permute-start | bytes 196616 | tf_op jit(solution)/shard_map/ppermute | solution.py:603
  13.2 0.0 copy-start
  13.2 0.9 %copy-done = f32[3,8,2,8,128]{4,3,2,1,0:T(8,128)S(1)} copy-done((f32[3,8,2,8,128]{4,3,2,1,0:T(8,128)S(1)}, f32[3,8,2,8,128]{4,3,2,1,0:T(8,128)}, u32[]{:S(2)}) %copy-start) | copy-done | bytes 196632
  14.2 0.1 shard_map.51
  14.3 0.0 collective-permute-done.left_ref
  14.3 0.6 collective-permute-done.1.right_ref
  14.8 0.2 shard_map.52
  15.0 3.2 %collective-permute-start.2 = (f32[10,8,256]{2,1,0:T(8,128)S(1)}, f32[10,8,256]{2,1,0:T(8,128)S(1)}, u32[]{:S(2)}, u32[]{:S(2)}) collective-permute-start(f32[10,8,256]{2,1,0:T(8,128)S(1)} %get-tuple-element.25), channel_id=1, source_target_pairs={{0,16},{16,32},{32,48},{48,64},{64,80},{80,96},{96,112},{112,128},... | collective-permute-start | bytes 245768 | tf_op jit(solution)/shard_map/ppermute | solution.py:603
  18.2 3.9 %collective-permute-start.3 = (f32[10,8,256]{2,1,0:T(8,128)S(1)}, f32[10,8,256]{2,1,0:T(8,128)S(1)}, u32[]{:S(2)}, u32[]{:S(2)}) collective-permute-start(f32[10,8,256]{2,1,0:T(8,128)S(1)} %get-tuple-element.27), channel_id=1, source_target_pairs={{0,496},{16,0},{32,16},{48,32},{64,48},{80,64},{96,80},{112,96},{1... | collective-permute-start | bytes 245768 | tf_op jit(solution)/shard_map/ppermute | solution.py:603
  22.1 0.7 collective-permute-done.2.left_ref
  22.8 0.2 collective-permute-done.3.right_ref
  23.0 0.8 shard_map.53
  23.8 4.1 %collective-permute-start.6 = (f32[8,2,8,256]{3,2,1,0:T(8,128)S(1)}, f32[8,2,8,256]{3,2,1,0:T(8,128)S(1)}, u32[]{:S(2)}, u32[]{:S(2)}) collective-permute-start(f32[8,2,8,256]{3,2,1,0:T(8,128)S(1)} %get-tuple-element.29.mid_ref.refs_2_), channel_id=1, source_target_pairs={{0,496},{16,0},{32,16},{48,32},{64,48},{80,64},{96,80},{112,96},{1... | collective-permute-start | bytes 393224 | tf_op jit(solution)/shard_map/ppermute | solution.py:603
  27.9 0.0 collective-permute-start.4
  28.0 1.0 %collective-permute-done.6.right_ref.refs_3_ = f32[8,2,8,256]{3,2,1,0:T(8,128)S(1)} collective-permute-done((f32[8,2,8,256]{3,2,1,0:T(8,128)S(1)}, f32[8,2,8,256]{3,2,1,0:T(8,128)S(1)}, u32[]{:S(2)}, u32[]{:S(2)}) %collective-permute-start.6) | collective-permute-done | bytes 131104 | tf_op jit(solution)/shard_map/ppermute | solution.py:603
  28.9 4.5 %collective-permute-start.7 = (f32[8,2,8,256]{3,2,1,0:T(8,128)S(1)}, f32[8,2,8,256]{3,2,1,0:T(8,128)S(1)}, u32[]{:S(2)}, u32[]{:S(2)}) collective-permute-start(f32[8,2,8,256]{3,2,1,0:T(8,128)S(1)} %collective-permute-done.6.right_ref.refs_3_), channel_id=1, source_target_pairs={{0,496},{16,0},{32,16},{48,32},{64,48},{80,64},{96,80},{112,96},{1... | collective-permute-start | bytes 393224 | tf_op jit(solution)/shard_map/ppermute | solution.py:603
  33.4 0.0 collective-permute-done.4.left_ref.refs_1_
  33.4 0.0 collective-permute-start.5
  33.4 1.6 %shard_map.54 = (f32[3,8,10,8,256]{4,3,2,1,0:T(8,128)S(1)}, f32[3,8,10,8,256]{4,3,2,1,0:T(8,128)S(1)}, f32[9,8,256]{2,1,0:T(8,128)S(1)}) custom-call(f32[8,2,8,256]{3,2,1,0:T(8,128)S(1)} %collective-permute-done.4.left_ref.refs_1_, f32[8,2,8,256]{3,2,1,0:T(8,128)S(1)} %get-tuple-element.29.mid_ref.refs_2_, ...), custom_call_target="tpu_custom_call" | custom-call | flops 5000000 | bytes 4000000 | tf_op jit(solution)/shard_map/pallas_call | solution.py:590
  35.0 0.0 collective-permute-done.7.refs_4_
  35.0 2.3 %collective-permute-done.5.refs_0_ = f32[8,2,8,256]{3,2,1,0:T(8,128)S(1)} collective-permute-done((f32[8,2,8,256]{3,2,1,0:T(8,128)S(1)}, f32[8,2,8,256]{3,2,1,0:T(8,128)S(1)}, u32[]{:S(2)}, u32[]{:S(2)}) %collective-permute-start.5) | collective-permute-done | bytes 131104 | tf_op jit(solution)/shard_map/ppermute | solution.py:603
  37.4 1.8 %shard_map.55 = (f32[2,8,4,8,256]{4,3,2,1,0:T(8,128)S(1)}, f32[8,128]{1,0:T(8,128)S(1)}) custom-call(f32[8,2,8,256]{3,2,1,0:T(8,128)S(1)} %collective-permute-done.5.refs_0_, f32[8,2,8,256]{3,2,1,0:T(8,128)S(1)} %collective-permute-done.4.left_ref.refs_1_, f32[8,2,8,256]{3,2,1,0:T(8,128)S(1)} %get-tuple-element.29.mid_ref.refs_2_, ...), custom_call_target="tpu_custom_call" | custom-call | tf_op jit(solution)/shard_map/pallas_call | solution.py:590
  39.1 6.3 %all-gather = f32[16,128]{1,0:T(8,128)S(1)} all-gather(f32[8,128]{1,0:T(8,128)S(1)} %get-tuple-element.34), channel_id=2, replica_groups={{0,16},{32,48},{64,80},{96,112},{128,144},{160,176},{192,208},{224,240}..., dimensions={0}, use_global_device_ids=true | all-gather | bytes 12288 | tf_op jit(solution)/shard_map/all_gather | solution.py:609
  45.4 13.0 %all_to_all.10 = f32[16,8,128]{2,1,0:T(8,128)S(1)} all-to-all(f32[16,8,128]{2,1,0:T(8,128)S(1)} %broadcast_in_dim.4), channel_id=1, replica_groups=mesh['gx'=32,'gy'=16] {'gy'}, dimensions={0} | all-to-all | bytes 131072 | tf_op jit(solution)/shard_map/all_to_all | solution.py:611
  58.4 20.9 %all_to_all.11.m_ref = f32[16,8,128]{2,1,0:T(8,128)S(1)} all-to-all(f32[16,8,128]{2,1,0:T(8,128)S(1)} %broadcast_in_dim.5), channel_id=1, replica_groups={{0,32,64,96,128,160,192,224,256,288,320,352,384,416,448,480},{16,48,80,..., dimensions={0} | all-to-all | bytes 131072 | tf_op jit(solution)/shard_map/all_to_all | solution.py:614
  79.3 1.3 %shard_map.56 = (f32[3,8,2,8,128]{4,3,2,1,0:T(8,128)}, f32[8,2,8,128]{3,2,1,0:T(8,128)}) custom-call(f32[16,8,128]{2,1,0:T(8,128)S(1)} %all_to_all.11.m_ref, f32[3,8,10,8,256]{4,3,2,1,0:T(8,128)S(1)} %get-tuple-element.31.refs_5_.low_ref, f32[2,8,4,8,256]{4,3,2,1,0:T(8,128)S(1)} %get-tuple-element.35.high_ref, ...), custom_call_target="tpu_custom_call" | custom-call | tf_op jit(solution)/shard_map/pallas_call | solution.py:590
  (4 shorter events, 0.0 us)
Async XLA Ops:
  3.6 10.6 %collective-permute-start = (f32[8,2,8,128]{3,2,1,0:T(8,128)}, f32[8,2,8,128]{3,2,1,0:T(8,128)S(1)}, u32[]{:S(2)}, u32[]{:S(2)}) collective-permute-start(f32[8,2,8,128]{3,2,1,0:T(8,128)} %get-tuple-element.23), channel_id=1, source_target_pairs={{0,1},{1,2},{2,3},{3,4},{4,5},{5,6},{6,7},{7,8},{8,9},{9,10},{10,1... | collective-permute-start | bytes 196616 | tf_op jit(solution)/shard_map/ppermute | solution.py:603
  7.7 7.2 %collective-permute-start.1 = (f32[8,2,8,128]{3,2,1,0:T(8,128)}, f32[8,2,8,128]{3,2,1,0:T(8,128)S(1)}, u32[]{:S(2)}, u32[]{:S(2)}) collective-permute-start(f32[8,2,8,128]{3,2,1,0:T(8,128)} %get-tuple-element.24), channel_id=1, source_target_pairs={{0,15},{1,0},{2,1},{3,2},{4,3},{5,4},{6,5},{7,6},{8,7},{9,8},{10,9... | collective-permute-start | bytes 196616 | tf_op jit(solution)/shard_map/ppermute | solution.py:603
  13.2 0.9 %copy-start = (f32[3,8,2,8,128]{4,3,2,1,0:T(8,128)S(1)}, f32[3,8,2,8,128]{4,3,2,1,0:T(8,128)}, u32[]{:S(2)}) copy-start(f32[3,8,2,8,128]{4,3,2,1,0:T(8,128)} %get-tuple-element.21.r_ref) | copy-start | bytes 589828
  15.0 7.8 %collective-permute-start.2 = (f32[10,8,256]{2,1,0:T(8,128)S(1)}, f32[10,8,256]{2,1,0:T(8,128)S(1)}, u32[]{:S(2)}, u32[]{:S(2)}) collective-permute-start(f32[10,8,256]{2,1,0:T(8,128)S(1)} %get-tuple-element.25), channel_id=1, source_target_pairs={{0,16},{16,32},{32,48},{48,64},{64,80},{80,96},{96,112},{112,128},... | collective-permute-start | bytes 245768 | tf_op jit(solution)/shard_map/ppermute | solution.py:603
  18.2 4.8 %collective-permute-start.3 = (f32[10,8,256]{2,1,0:T(8,128)S(1)}, f32[10,8,256]{2,1,0:T(8,128)S(1)}, u32[]{:S(2)}, u32[]{:S(2)}) collective-permute-start(f32[10,8,256]{2,1,0:T(8,128)S(1)} %get-tuple-element.27), channel_id=1, source_target_pairs={{0,496},{16,0},{32,16},{48,32},{64,48},{80,64},{96,80},{112,96},{1... | collective-permute-start | bytes 245768 | tf_op jit(solution)/shard_map/ppermute | solution.py:603
  23.8 5.1 %collective-permute-start.6 = (f32[8,2,8,256]{3,2,1,0:T(8,128)S(1)}, f32[8,2,8,256]{3,2,1,0:T(8,128)S(1)}, u32[]{:S(2)}, u32[]{:S(2)}) collective-permute-start(f32[8,2,8,256]{3,2,1,0:T(8,128)S(1)} %get-tuple-element.29.mid_ref.refs_2_), channel_id=1, source_target_pairs={{0,496},{16,0},{32,16},{48,32},{64,48},{80,64},{96,80},{112,96},{1... | collective-permute-start | bytes 393224 | tf_op jit(solution)/shard_map/ppermute | solution.py:603
  27.9 5.5 %collective-permute-start.4 = (f32[8,2,8,256]{3,2,1,0:T(8,128)S(1)}, f32[8,2,8,256]{3,2,1,0:T(8,128)S(1)}, u32[]{:S(2)}, u32[]{:S(2)}) collective-permute-start(f32[8,2,8,256]{3,2,1,0:T(8,128)S(1)} %get-tuple-element.29.mid_ref.refs_2_), channel_id=1, source_target_pairs={{0,16},{16,32},{32,48},{48,64},{64,80},{80,96},{96,112},{112,128},... | collective-permute-start | bytes 393224 | tf_op jit(solution)/shard_map/ppermute | solution.py:603
  28.9 6.1 %collective-permute-start.7 = (f32[8,2,8,256]{3,2,1,0:T(8,128)S(1)}, f32[8,2,8,256]{3,2,1,0:T(8,128)S(1)}, u32[]{:S(2)}, u32[]{:S(2)}) collective-permute-start(f32[8,2,8,256]{3,2,1,0:T(8,128)S(1)} %collective-permute-done.6.right_ref.refs_3_), channel_id=1, source_target_pairs={{0,496},{16,0},{32,16},{48,32},{64,48},{80,64},{96,80},{112,96},{1... | collective-permute-start | bytes 393224 | tf_op jit(solution)/shard_map/ppermute | solution.py:603
  33.4 3.9 %collective-permute-start.5 = (f32[8,2,8,256]{3,2,1,0:T(8,128)S(1)}, f32[8,2,8,256]{3,2,1,0:T(8,128)S(1)}, u32[]{:S(2)}, u32[]{:S(2)}) collective-permute-start(f32[8,2,8,256]{3,2,1,0:T(8,128)S(1)} %collective-permute-done.4.left_ref.refs_1_), channel_id=1, source_target_pairs={{0,16},{16,32},{32,48},{48,64},{64,80},{80,96},{96,112},{112,128},... | collective-permute-start | bytes 393224 | tf_op jit(solution)/shard_map/ppermute | solution.py:603

commit v7 on v6

--- a/solution.py
+++ b/solution.py
@@ -509,7 +509,8 @@
         part = part[:, :128] + part[:, 128:]
         total = jnp.sum(jnp.sum(part, axis=0, keepdims=True), axis=1, keepdims=True)
         packed = jnp.where(lane == k, total, packed)
-    m_out[...] = packed
+    for k in range(m_out.shape[0]):
+        m_out[k] = packed
 
 
 def final_kernel(m_ref, low_ref, high_ref, w_ref, open_ref, dy_ref, out_ref, q_ref):
@@ -605,10 +606,8 @@
 
 def total_rows(packed):
     nx, ny = lax.axis_size("gx"), lax.axis_size("gy")
-    pairs = [[i, i + 1] for i in range(0, nx, 2)]
-    part = lax.all_gather(packed, "gx", axis_index_groups=pairs)
-    part = jnp.broadcast_to(jnp.sum(part, axis=0, keepdims=True), (ny, 8, 128))
-    part = lax.all_to_all(part, "gy", 0, 0, tiled=True)
+    planes = [[(2 * z + c) * ny + y for y in range(ny) for c in range(2)] for z in range(nx // 2)]
+    part = lax.all_to_all(packed, ("gx", "gy"), 0, 0, axis_index_groups=planes, tiled=True)
     part = jnp.broadcast_to(jnp.sum(part, axis=0, keepdims=True), (nx // 2, 8, 128))
     along = [[2 * z + c for z in range(nx // 2)] for c in range(2)]
     return lax.all_to_all(part, "gx", 0, 0, axis_index_groups=along, tiled=True)
@@ -657,6 +656,7 @@
     )
     left = shift(source, "gx", 1)
     right = shift(source, "gx", -1)
+    right, left = lax.optimization_barrier((right, left))
     left2 = shift(left, "gx", 1)
     right2 = shift(right, "gx", -1)
     cost = pl.CostEstimate(flops=5 * 10**6, bytes_accessed=4 * 10**6, transcendentals=0)
@@ -669,7 +669,7 @@
     )
     high, packed = call(
         outer_kernel,
-        (shape(2, 8, 4, 8, 256), shape(8, 128)),
+        (shape(2, 8, 4, 8, 256), shape(2 * lax.axis_size("gy"), 8, 128)),
         [
             vm((4, 8, 10, 8, 256), f32),
             vm((4, 8, 10, 8, 256), f32),

time: 81.7 us -> 78.3 us (0.958); the launches traced: 80.6 us -> 78 us
  waiting for transfers between devices: 4.8 us -> 2.49 us
    all_gather x1 -> x0, blocking collectives: 6.26 us -> none  [total_rows(): part = lax.all_gather(packed, 'gx', axis_index_groups=pairs)]
    all_to_all x1, blocking collectives: 13 us -> 18.5 us  [total_rows(): lax.all_to_all(packed, ('gx', 'gy'), 0, 0, axis_index_groups=planes, tile...]
    ppermute x8, waiting for transfers between devices: 4.8 us -> 2.49 us  [shift(): lax.ppermute(value, axis, [(i, (i + by) % size) for i in range(size)])]
where the time goes in v7:
time: 78.3 us; the launch traced here: 78 us
  blocking collectives  39.7 us (51%)
  starting transfers between devices  25.4 us (32%)
  Pallas kernels  8.71 us (11%)
  waiting for transfers between devices  2.49 us (3%)
  local copies, waits for them, and re-layouts  0.93 us (1%)
    ppermute x8, starting transfers between devices, shift(): lax.ppermute(value, axis, [(i, (i + by) % size) for i in range(size)])  25.4 us
    all_to_all x1, blocking collectives, total_rows(): return lax.all_to_all(part, 'gx', 0, 0, axis_index_groups=along, tiled=True)  21.2 us
    all_to_all x1, blocking collectives, total_rows(): lax.all_to_all(packed, ('gx', 'gy'), 0, 0, axis_index_groups=planes, tile...  18.5 us
    pallas_call x7, Pallas kernels, call(): pl.pallas_call(kernel, out_shape=out_shape, in_specs=[pl.BlockSpec(memory...  8.71 us
    ppermute x8, waiting for transfers between devices, shift(): lax.ppermute(value, axis, [(i, (i + by) % size) for i in range(size)])  2.49 us
  transfers between devices with their start and end apart: 8, of which 5 were waited for; matrix products, arithmetic and copies ran while one was open for 0% of the time, Pallas kernels for 2%

profile of v7, /device:TPU:1, one launch (start us, length us, event | category | flops | bytes accessed | tf_op | source)
XLA Modules:
  0.0 78.0 jit_solution(6037103173905331455)
XLA Ops:
  0.6 3.0 %shard_map.50 = (f32[3,8,2,8,128]{4,3,2,1,0:T(8,128)}, f32[8,2,8,128]{3,2,1,0:T(8,128)}, f32[8,2,8,128]{3,2,1,0:T(8,128)}) custom-call(f32[3,8,2,8,128]{4,3,2,1,0:T(8,128)} %bitcast.4, bf16[3,8,16,128]{3,2,1,0:T(8,128)(2,1)} %bitcast.5, s32[2,2,16]{2,1,0:T(2,128)} %faces_hbm.1), custom_call_target="tpu_custom_call" | custom-call | tf_op jit(solution)/shard_map/pallas_call | solution.py:591
  3.6 4.0 %collective-permute-start = (f32[8,2,8,128]{3,2,1,0:T(8,128)}, f32[8,2,8,128]{3,2,1,0:T(8,128)S(1)}, u32[]{:S(2)}, u32[]{:S(2)}) collective-permute-start(f32[8,2,8,128]{3,2,1,0:T(8,128)} %get-tuple-element.25), channel_id=1, source_target_pairs={{0,1},{1,2},{2,3},{3,4},{4,5},{5,6},{6,7},{7,8},{8,9},{9,10},{10,1... | collective-permute-start | bytes 196616 | tf_op jit(solution)/shard_map/ppermute | solution.py:604
  7.7 5.6 %collective-permute-start.1 = (f32[8,2,8,128]{3,2,1,0:T(8,128)}, f32[8,2,8,128]{3,2,1,0:T(8,128)S(1)}, u32[]{:S(2)}, u32[]{:S(2)}) collective-permute-start(f32[8,2,8,128]{3,2,1,0:T(8,128)} %get-tuple-element.26), channel_id=1, source_target_pairs={{0,15},{1,0},{2,1},{3,2},{4,3},{5,4},{6,5},{7,6},{8,7},{9,8},{10,9... | collective-permute-start | bytes 196616 | tf_op jit(solution)/shard_map/ppermute | solution.py:604
  13.2 0.0 copy-start
  13.2 0.9 %copy-done = f32[3,8,2,8,128]{4,3,2,1,0:T(8,128)S(1)} copy-done((f32[3,8,2,8,128]{4,3,2,1,0:T(8,128)S(1)}, f32[3,8,2,8,128]{4,3,2,1,0:T(8,128)}, u32[]{:S(2)}) %copy-start) | copy-done | bytes 196632
  14.2 0.1 shard_map.51
  14.3 0.0 collective-permute-done.left_ref
  14.3 0.6 collective-permute-done.1.right_ref
  14.8 0.2 shard_map.52
  15.0 3.2 %collective-permute-start.2 = (f32[10,8,256]{2,1,0:T(8,128)S(1)}, f32[10,8,256]{2,1,0:T(8,128)S(1)}, u32[]{:S(2)}, u32[]{:S(2)}) collective-permute-start(f32[10,8,256]{2,1,0:T(8,128)S(1)} %get-tuple-element.27), channel_id=1, source_target_pairs={{0,16},{16,32},{32,48},{48,64},{64,80},{80,96},{96,112},{112,128},... | collective-permute-start | bytes 245768 | tf_op jit(solution)/shard_map/ppermute | solution.py:604
  18.2 3.9 %collective-permute-start.3 = (f32[10,8,256]{2,1,0:T(8,128)S(1)}, f32[10,8,256]{2,1,0:T(8,128)S(1)}, u32[]{:S(2)}, u32[]{:S(2)}) collective-permute-start(f32[10,8,256]{2,1,0:T(8,128)S(1)} %get-tuple-element.29), channel_id=1, source_target_pairs={{0,496},{16,0},{32,16},{48,32},{64,48},{80,64},{96,80},{112,96},{1... | collective-permute-start | bytes 245768 | tf_op jit(solution)/shard_map/ppermute | solution.py:604
  22.1 0.7 collective-permute-done.2.left_ref
  22.8 0.2 collective-permute-done.3.right_ref
  23.0 0.8 %shard_map.53 = (f32[8,2,8,256]{3,2,1,0:T(8,128)S(1)}, f32[3,8,2,8,128]{4,3,2,1,0:T(8,128)S(1)}, f32[2,2,8,128]{3,2,1,0:T(8,128)S(1)}) custom-call(f32[10,8,256]{2,1,0:T(8,128)S(1)} %collective-permute-done.2.left_ref, f32[3,8,2,8,256]{4,3,2,1,0:T(8,128)S(1)} %get-tuple-element.28.mid_ref, f32[10,8,256]{2,1,0:T(8,128)S(1)} %collective-permute-done.3.right_ref, ...), custom_call_target="tpu_custom_call" | custom-call | tf_op jit(solution)/shard_map/pallas_call | solution.py:591
  23.8 0.0 collective-permute-start.5
  23.8 4.1 %collective-permute-start.4 = (f32[8,2,8,256]{3,2,1,0:T(8,128)S(1)}, f32[8,2,8,256]{3,2,1,0:T(8,128)S(1)}, u32[]{:S(2)}, u32[]{:S(2)}) collective-permute-start(f32[8,2,8,256]{3,2,1,0:T(8,128)S(1)} %get-tuple-element.31.mid_ref.refs_2_), channel_id=1, source_target_pairs={{0,496},{16,0},{32,16},{48,32},{64,48},{80,64},{96,80},{112,96},{1... | collective-permute-start | bytes 393224 | tf_op jit(solution)/shard_map/ppermute | solution.py:604
  28.0 0.8 %collective-permute-done.5.left_ref.refs_1_ = f32[8,2,8,256]{3,2,1,0:T(8,128)S(1)} collective-permute-done((f32[8,2,8,256]{3,2,1,0:T(8,128)S(1)}, f32[8,2,8,256]{3,2,1,0:T(8,128)S(1)}, u32[]{:S(2)}, u32[]{:S(2)}) %collective-permute-start.5) | collective-permute-done | bytes 131104 | tf_op jit(solution)/shard_map/ppermute | solution.py:604
  28.8 0.2 collective-permute-done.4.right_ref.refs_3_
  29.0 0.0 collective-permute-start.6
  29.0 4.6 %collective-permute-start.7 = (f32[8,2,8,256]{3,2,1,0:T(8,128)S(1)}, f32[8,2,8,256]{3,2,1,0:T(8,128)S(1)}, u32[]{:S(2)}, u32[]{:S(2)}) collective-permute-start(f32[8,2,8,256]{3,2,1,0:T(8,128)S(1)} %collective-permute-done.4.right_ref.refs_3_), channel_id=1, source_target_pairs={{0,496},{16,0},{32,16},{48,32},{64,48},{80,64},{96,80},{112,96},{1... | collective-permute-start | bytes 393224 | tf_op jit(solution)/shard_map/ppermute | solution.py:604
  33.6 1.6 %shard_map.54 = (f32[3,8,10,8,256]{4,3,2,1,0:T(8,128)S(1)}, f32[3,8,10,8,256]{4,3,2,1,0:T(8,128)S(1)}, f32[9,8,256]{2,1,0:T(8,128)S(1)}) custom-call(f32[8,2,8,256]{3,2,1,0:T(8,128)S(1)} %collective-permute-done.5.left_ref.refs_1_, f32[8,2,8,256]{3,2,1,0:T(8,128)S(1)} %get-tuple-element.31.mid_ref.refs_2_, ...), custom_call_target="tpu_custom_call" | custom-call | flops 5000000 | bytes 4000000 | tf_op jit(solution)/shard_map/pallas_call | solution.py:591
  35.2 0.0 collective-permute-done.6.refs_0_
  35.2 0.0 collective-permute-done.7.refs_4_
  35.2 1.8 %shard_map.55 = (f32[2,8,4,8,256]{4,3,2,1,0:T(8,128)S(1)}, f32[32,8,128]{2,1,0:T(8,128)S(1)}) custom-call(f32[8,2,8,256]{3,2,1,0:T(8,128)S(1)} %collective-permute-done.6.refs_0_, f32[8,2,8,256]{3,2,1,0:T(8,128)S(1)} %collective-permute-done.5.left_ref.refs_1_, f32[8,2,8,256]{3,2,1,0:T(8,128)S(1)} %get-tuple-element.31.mid_ref.refs_2_, ...), custom_call_target="tpu_custom_call" | custom-call | tf_op jit(solution)/shard_map/pallas_call | solution.py:591
  37.0 18.5 %all_to_all.10 = f32[32,8,128]{2,1,0:T(8,128)S(1)} all-to-all(f32[32,8,128]{2,1,0:T(8,128)S(1)} %get-tuple-element.38), channel_id=1, replica_groups={{0,16,1,17,2,18,3,19,4,20,5,21,6,22,7,23,8,24,9,25,10,26,11,27,12,28,13..., dimensions={0} | all-to-all | bytes 262144 | tf_op jit(solution)/shard_map/all_to_all | solution.py:610
  55.5 21.2 %all_to_all.11.m_ref = f32[16,8,128]{2,1,0:T(8,128)S(1)} all-to-all(f32[16,8,128]{2,1,0:T(8,128)S(1)} %broadcast_in_dim.2), channel_id=1, replica_groups={{0,32,64,96,128,160,192,224,256,288,320,352,384,416,448,480},{16,48,80,..., dimensions={0} | all-to-all | bytes 131072 | tf_op jit(solution)/shard_map/all_to_all | solution.py:613
  76.8 1.3 %shard_map.56 = (f32[3,8,2,8,128]{4,3,2,1,0:T(8,128)}, f32[8,2,8,128]{3,2,1,0:T(8,128)}) custom-call(f32[16,8,128]{2,1,0:T(8,128)S(1)} %all_to_all.11.m_ref, f32[3,8,10,8,256]{4,3,2,1,0:T(8,128)S(1)} %get-tuple-element.35.refs_5_.low_ref, f32[2,8,4,8,256]{4,3,2,1,0:T(8,128)S(1)} %get-tuple-element.39.high_ref, ...), custom_call_target="tpu_custom_call" | custom-call | tf_op jit(solution)/shard_map/pallas_call | solution.py:591
  (2 shorter events, 0.0 us)
Async XLA Ops:
  3.6 10.6 %collective-permute-start = (f32[8,2,8,128]{3,2,1,0:T(8,128)}, f32[8,2,8,128]{3,2,1,0:T(8,128)S(1)}, u32[]{:S(2)}, u32[]{:S(2)}) collective-permute-start(f32[8,2,8,128]{3,2,1,0:T(8,128)} %get-tuple-element.25), channel_id=1, source_target_pairs={{0,1},{1,2},{2,3},{3,4},{4,5},{5,6},{6,7},{7,8},{8,9},{9,10},{10,1... | collective-permute-start | bytes 196616 | tf_op jit(solution)/shard_map/ppermute | solution.py:604
  7.7 7.2 %collective-permute-start.1 = (f32[8,2,8,128]{3,2,1,0:T(8,128)}, f32[8,2,8,128]{3,2,1,0:T(8,128)S(1)}, u32[]{:S(2)}, u32[]{:S(2)}) collective-permute-start(f32[8,2,8,128]{3,2,1,0:T(8,128)} %get-tuple-element.26), channel_id=1, source_target_pairs={{0,15},{1,0},{2,1},{3,2},{4,3},{5,4},{6,5},{7,6},{8,7},{9,8},{10,9... | collective-permute-start | bytes 196616 | tf_op jit(solution)/shard_map/ppermute | solution.py:604
  13.2 0.9 %copy-start = (f32[3,8,2,8,128]{4,3,2,1,0:T(8,128)S(1)}, f32[3,8,2,8,128]{4,3,2,1,0:T(8,128)}, u32[]{:S(2)}) copy-start(f32[3,8,2,8,128]{4,3,2,1,0:T(8,128)} %get-tuple-element.23.r_ref) | copy-start | bytes 589828
  15.0 7.8 %collective-permute-start.2 = (f32[10,8,256]{2,1,0:T(8,128)S(1)}, f32[10,8,256]{2,1,0:T(8,128)S(1)}, u32[]{:S(2)}, u32[]{:S(2)}) collective-permute-start(f32[10,8,256]{2,1,0:T(8,128)S(1)} %get-tuple-element.27), channel_id=1, source_target_pairs={{0,16},{16,32},{32,48},{48,64},{64,80},{80,96},{96,112},{112,128},... | collective-permute-start | bytes 245768 | tf_op jit(solution)/shard_map/ppermute | solution.py:604
  18.2 4.8 %collective-permute-start.3 = (f32[10,8,256]{2,1,0:T(8,128)S(1)}, f32[10,8,256]{2,1,0:T(8,128)S(1)}, u32[]{:S(2)}, u32[]{:S(2)}) collective-permute-start(f32[10,8,256]{2,1,0:T(8,128)S(1)} %get-tuple-element.29), channel_id=1, source_target_pairs={{0,496},{16,0},{32,16},{48,32},{64,48},{80,64},{96,80},{112,96},{1... | collective-permute-start | bytes 245768 | tf_op jit(solution)/shard_map/ppermute | solution.py:604
  23.8 5.0 %collective-permute-start.5 = (f32[8,2,8,256]{3,2,1,0:T(8,128)S(1)}, f32[8,2,8,256]{3,2,1,0:T(8,128)S(1)}, u32[]{:S(2)}, u32[]{:S(2)}) collective-permute-start(f32[8,2,8,256]{3,2,1,0:T(8,128)S(1)} %get-tuple-element.31.mid_ref.refs_2_), channel_id=1, source_target_pairs={{0,16},{16,32},{32,48},{48,64},{64,80},{80,96},{96,112},{112,128},... | collective-permute-start | bytes 393224 | tf_op jit(solution)/shard_map/ppermute | solution.py:604
  23.8 5.1 %collective-permute-start.4 = (f32[8,2,8,256]{3,2,1,0:T(8,128)S(1)}, f32[8,2,8,256]{3,2,1,0:T(8,128)S(1)}, u32[]{:S(2)}, u32[]{:S(2)}) collective-permute-start(f32[8,2,8,256]{3,2,1,0:T(8,128)S(1)} %get-tuple-element.31.mid_ref.refs_2_), channel_id=1, source_target_pairs={{0,496},{16,0},{32,16},{48,32},{64,48},{80,64},{96,80},{112,96},{1... | collective-permute-start | bytes 393224 | tf_op jit(solution)/shard_map/ppermute | solution.py:604
  29.0 6.2 %collective-permute-start.6 = (f32[8,2,8,256]{3,2,1,0:T(8,128)S(1)}, f32[8,2,8,256]{3,2,1,0:T(8,128)S(1)}, u32[]{:S(2)}, u32[]{:S(2)}) collective-permute-start(f32[8,2,8,256]{3,2,1,0:T(8,128)S(1)} %collective-permute-done.5.left_ref.refs_1_), channel_id=1, source_target_pairs={{0,16},{16,32},{32,48},{48,64},{64,80},{80,96},{96,112},{112,128},... | collective-permute-start | bytes 393224 | tf_op jit(solution)/shard_map/ppermute | solution.py:604
  29.0 6.2 %collective-permute-start.7 = (f32[8,2,8,256]{3,2,1,0:T(8,128)S(1)}, f32[8,2,8,256]{3,2,1,0:T(8,128)S(1)}, u32[]{:S(2)}, u32[]{:S(2)}) collective-permute-start(f32[8,2,8,256]{3,2,1,0:T(8,128)S(1)} %collective-permute-done.4.right_ref.refs_3_), channel_id=1, source_target_pairs={{0,496},{16,0},{32,16},{48,32},{64,48},{80,64},{96,80},{112,96},{1... | collective-permute-start | bytes 393224 | tf_op jit(solution)/shard_map/ppermute | solution.py:604

commit v8 on v7

--- a/solution.py
+++ b/solution.py
@@ -509,17 +509,17 @@
         part = part[:, :128] + part[:, 128:]
         total = jnp.sum(jnp.sum(part, axis=0, keepdims=True), axis=1, keepdims=True)
         packed = jnp.where(lane == k, total, packed)
-    for k in range(m_out.shape[0]):
-        m_out[k] = packed
+    for k in range(m_out.shape[0] // 8):
+        m_out[8 * k : 8 * k + 8] = packed
 
 
 def final_kernel(m_ref, low_ref, high_ref, w_ref, open_ref, dy_ref, out_ref, q_ref):
     lanes = 256
-    parts = [m_ref[k] for k in range(m_ref.shape[0])]
+    parts = [m_ref[8 * k : 8 * k + 8] for k in range(m_ref.shape[0] // 8)]
     while len(parts) > 1:
         odd = parts[len(parts) // 2 * 2 :]
         parts = [parts[k] + parts[k + 1] for k in range(0, len(parts) - 1, 2)] + odd
-    sums = parts[0]
+    sums = jnp.broadcast_to(jnp.sum(parts[0], axis=0, keepdims=True), (8, 128))
     lane = iota(128, 1)
 
     def moment(k):
@@ -608,7 +608,7 @@
     nx, ny = lax.axis_size("gx"), lax.axis_size("gy")
     planes = [[(2 * z + c) * ny + y for y in range(ny) for c in range(2)] for z in range(nx // 2)]
     part = lax.all_to_all(packed, ("gx", "gy"), 0, 0, axis_index_groups=planes, tiled=True)
-    part = jnp.broadcast_to(jnp.sum(part, axis=0, keepdims=True), (nx // 2, 8, 128))
+    part = jnp.broadcast_to(jnp.sum(part, axis=0, keepdims=True), (nx // 2, 128))
     along = [[2 * z + c for z in range(nx // 2)] for c in range(2)]
     return lax.all_to_all(part, "gx", 0, 0, axis_index_groups=along, tiled=True)
 
@@ -669,7 +669,7 @@
     )
     high, packed = call(
         outer_kernel,
-        (shape(2, 8, 4, 8, 256), shape(2 * lax.axis_size("gy"), 8, 128)),
+        (shape(2, 8, 4, 8, 256), shape(2 * lax.axis_size("gy"), 128)),
         [
             vm((4, 8, 10, 8, 256), f32),
             vm((4, 8, 10, 8, 256), f32),

time: 78.3 us -> 77.2 us (0.986)
  blocking collectives: 39.7 us -> 38.7 us
where the time goes in v8:
time: 77.2 us; the launch traced here: 77 us
  blocking collectives  38.7 us (50%)
  starting transfers between devices  25.4 us (33%)
  Pallas kernels  8.7 us (11%)
  waiting for transfers between devices  2.49 us (3%)
  local copies, waits for them, and re-layouts  0.93 us (1%)
    ppermute x8, starting transfers between devices, shift(): lax.ppermute(value, axis, [(i, (i + by) % size) for i in range(size)])  25.4 us
    all_to_all x1, blocking collectives, total_rows(): return lax.all_to_all(part, 'gx', 0, 0, axis_index_groups=along, tiled=True)  20.9 us
    all_to_all x1, blocking collectives, total_rows(): lax.all_to_all(packed, ('gx', 'gy'), 0, 0, axis_index_groups=planes, tile...  17.8 us
    pallas_call x7, Pallas kernels, call(): pl.pallas_call(kernel, out_shape=out_shape, in_specs=[pl.BlockSpec(memory...  8.7 us
    ppermute x8, waiting for transfers between devices, shift(): lax.ppermute(value, axis, [(i, (i + by) % size) for i in range(size)])  2.49 us
  transfers between devices with their start and end apart: 8, of which 5 were waited for; matrix products, arithmetic and copies ran while one was open for 0% of the time, Pallas kernels for 2%

profile of v8, /device:TPU:1, one launch (start us, length us, event | category | flops | bytes accessed | tf_op | source)
XLA Modules:
  0.0 77.0 jit_solution(14052247881535893642)
XLA Ops:
  0.6 3.0 %shard_map.50 = (f32[3,8,2,8,128]{4,3,2,1,0:T(8,128)}, f32[8,2,8,128]{3,2,1,0:T(8,128)}, f32[8,2,8,128]{3,2,1,0:T(8,128)}) custom-call(f32[3,8,2,8,128]{4,3,2,1,0:T(8,128)} %bitcast.10, bf16[3,8,16,128]{3,2,1,0:T(8,128)(2,1)} %bitcast.11, s32[2,2,16]{2,1,0:T(2,128)} %faces_hbm.1), custom_call_target="tpu_custom_call" | custom-call | tf_op jit(solution)/shard_map/pallas_call | solution.py:591
  3.6 4.0 %collective-permute-start = (f32[8,2,8,128]{3,2,1,0:T(8,128)}, f32[8,2,8,128]{3,2,1,0:T(8,128)S(1)}, u32[]{:S(2)}, u32[]{:S(2)}) collective-permute-start(f32[8,2,8,128]{3,2,1,0:T(8,128)} %get-tuple-element.25), channel_id=1, source_target_pairs={{0,1},{1,2},{2,3},{3,4},{4,5},{5,6},{6,7},{7,8},{8,9},{9,10},{10,1... | collective-permute-start | bytes 196616 | tf_op jit(solution)/shard_map/ppermute | solution.py:604
  7.7 5.6 %collective-permute-start.1 = (f32[8,2,8,128]{3,2,1,0:T(8,128)}, f32[8,2,8,128]{3,2,1,0:T(8,128)S(1)}, u32[]{:S(2)}, u32[]{:S(2)}) collective-permute-start(f32[8,2,8,128]{3,2,1,0:T(8,128)} %get-tuple-element.26), channel_id=1, source_target_pairs={{0,15},{1,0},{2,1},{3,2},{4,3},{5,4},{6,5},{7,6},{8,7},{9,8},{10,9... | collective-permute-start | bytes 196616 | tf_op jit(solution)/shard_map/ppermute | solution.py:604
  13.2 0.0 copy-start
  13.2 0.9 %copy-done = f32[3,8,2,8,128]{4,3,2,1,0:T(8,128)S(1)} copy-done((f32[3,8,2,8,128]{4,3,2,1,0:T(8,128)S(1)}, f32[3,8,2,8,128]{4,3,2,1,0:T(8,128)}, u32[]{:S(2)}) %copy-start) | copy-done | bytes 196632
  14.2 0.1 shard_map.51
  14.3 0.0 collective-permute-done.left_ref
  14.3 0.6 collective-permute-done.1.right_ref
  14.8 0.2 shard_map.52
  15.0 3.2 %collective-permute-start.2 = (f32[10,8,256]{2,1,0:T(8,128)S(1)}, f32[10,8,256]{2,1,0:T(8,128)S(1)}, u32[]{:S(2)}, u32[]{:S(2)}) collective-permute-start(f32[10,8,256]{2,1,0:T(8,128)S(1)} %get-tuple-element.27), channel_id=1, source_target_pairs={{0,16},{16,32},{32,48},{48,64},{64,80},{80,96},{96,112},{112,128},... | collective-permute-start | bytes 245768 | tf_op jit(solution)/shard_map/ppermute | solution.py:604
  18.2 3.9 %collective-permute-start.3 = (f32[10,8,256]{2,1,0:T(8,128)S(1)}, f32[10,8,256]{2,1,0:T(8,128)S(1)}, u32[]{:S(2)}, u32[]{:S(2)}) collective-permute-start(f32[10,8,256]{2,1,0:T(8,128)S(1)} %get-tuple-element.29), channel_id=1, source_target_pairs={{0,496},{16,0},{32,16},{48,32},{64,48},{80,64},{96,80},{112,96},{1... | collective-permute-start | bytes 245768 | tf_op jit(solution)/shard_map/ppermute | solution.py:604
  22.1 0.7 collective-permute-done.2.left_ref
  22.8 0.2 collective-permute-done.3.right_ref
  23.0 0.8 %shard_map.53 = (f32[8,2,8,256]{3,2,1,0:T(8,128)S(1)}, f32[3,8,2,8,128]{4,3,2,1,0:T(8,128)S(1)}, f32[2,2,8,128]{3,2,1,0:T(8,128)S(1)}) custom-call(f32[10,8,256]{2,1,0:T(8,128)S(1)} %collective-permute-done.2.left_ref, f32[3,8,2,8,256]{4,3,2,1,0:T(8,128)S(1)} %get-tuple-element.28.mid_ref, f32[10,8,256]{2,1,0:T(8,128)S(1)} %collective-permute-done.3.right_ref, ...), custom_call_target="tpu_custom_call" | custom-call | tf_op jit(solution)/shard_map/pallas_call | solution.py:591
  23.8 0.0 collective-permute-start.5
  23.8 4.1 %collective-permute-start.4 = (f32[8,2,8,256]{3,2,1,0:T(8,128)S(1)}, f32[8,2,8,256]{3,2,1,0:T(8,128)S(1)}, u32[]{:S(2)}, u32[]{:S(2)}) collective-permute-start(f32[8,2,8,256]{3,2,1,0:T(8,128)S(1)} %get-tuple-element.31.mid_ref.refs_2_), channel_id=1, source_target_pairs={{0,496},{16,0},{32,16},{48,32},{64,48},{80,64},{96,80},{112,96},{1... | collective-permute-start | bytes 393224 | tf_op jit(solution)/shard_map/ppermute | solution.py:604
  28.0 0.8 %collective-permute-done.5.left_ref.refs_1_ = f32[8,2,8,256]{3,2,1,0:T(8,128)S(1)} collective-permute-done((f32[8,2,8,256]{3,2,1,0:T(8,128)S(1)}, f32[8,2,8,256]{3,2,1,0:T(8,128)S(1)}, u32[]{:S(2)}, u32[]{:S(2)}) %collective-permute-start.5) | collective-permute-done | bytes 131104 | tf_op jit(solution)/shard_map/ppermute | solution.py:604
  28.8 0.2 collective-permute-done.4.right_ref.refs_3_
  29.0 0.0 collective-permute-start.6
  29.0 4.6 %collective-permute-start.7 = (f32[8,2,8,256]{3,2,1,0:T(8,128)S(1)}, f32[8,2,8,256]{3,2,1,0:T(8,128)S(1)}, u32[]{:S(2)}, u32[]{:S(2)}) collective-permute-start(f32[8,2,8,256]{3,2,1,0:T(8,128)S(1)} %collective-permute-done.4.right_ref.refs_3_), channel_id=1, source_target_pairs={{0,496},{16,0},{32,16},{48,32},{64,48},{80,64},{96,80},{112,96},{1... | collective-permute-start | bytes 393224 | tf_op jit(solution)/shard_map/ppermute | solution.py:604
  33.6 1.6 %shard_map.54 = (f32[3,8,10,8,256]{4,3,2,1,0:T(8,128)S(1)}, f32[3,8,10,8,256]{4,3,2,1,0:T(8,128)S(1)}, f32[9,8,256]{2,1,0:T(8,128)S(1)}) custom-call(f32[8,2,8,256]{3,2,1,0:T(8,128)S(1)} %collective-permute-done.5.left_ref.refs_1_, f32[8,2,8,256]{3,2,1,0:T(8,128)S(1)} %get-tuple-element.31.mid_ref.refs_2_, ...), custom_call_target="tpu_custom_call" | custom-call | flops 5000000 | bytes 4000000 | tf_op jit(solution)/shard_map/pallas_call | solution.py:591
  35.2 0.0 collective-permute-done.6.refs_0_
  35.2 0.0 collective-permute-done.7.refs_4_
  35.2 1.8 %shard_map.55 = (f32[2,8,4,8,256]{4,3,2,1,0:T(8,128)S(1)}, f32[32,128]{1,0:T(8,128)S(1)}) custom-call(f32[8,2,8,256]{3,2,1,0:T(8,128)S(1)} %collective-permute-done.6.refs_0_, f32[8,2,8,256]{3,2,1,0:T(8,128)S(1)} %collective-permute-done.5.left_ref.refs_1_, f32[8,2,8,256]{3,2,1,0:T(8,128)S(1)} %get-tuple-element.31.mid_ref.refs_2_, ...), custom_call_target="tpu_custom_call" | custom-call | tf_op jit(solution)/shard_map/pallas_call | solution.py:591
  37.0 17.8 %all_to_all.17 = f32[32,1,128]{2,1,0:T(1,128)S(1)} all-to-all(f32[32,1,128]{2,1,0:T(1,128)S(1)} %bitcast.9), channel_id=1, replica_groups={{0,16,1,17,2,18,3,19,4,20,5,21,6,22,7,23,8,24,9,25,10,26,11,27,12,28,13..., dimensions={0} | all-to-all | bytes 32768 | tf_op jit(solution)/shard_map/all_to_all | solution.py:610
  54.7 0.1 reduce_sum.9
  54.8 20.9 %all_to_all.18 = f32[16,1,128]{2,1,0:T(1,128)S(1)} all-to-all(f32[16,1,128]{2,1,0:T(1,128)S(1)} %broadcast_in_dim.2), channel_id=1, replica_groups={{0,32,64,96,128,160,192,224,256,288,320,352,384,416,448,480},{16,48,80,..., dimensions={0} | all-to-all | bytes 16384 | tf_op jit(solution)/shard_map/all_to_all | solution.py:613
  75.7 1.3 %shard_map.56 = (f32[3,8,2,8,128]{4,3,2,1,0:T(8,128)}, f32[8,2,8,128]{3,2,1,0:T(8,128)}) custom-call(f32[16,128]{1,0:T(8,128)S(1)} %bitcast.8, f32[3,8,10,8,256]{4,3,2,1,0:T(8,128)S(1)} %get-tuple-element.35.refs_5_.low_ref, f32[2,8,4,8,256]{4,3,2,1,0:T(8,128)S(1)} %get-tuple-element.39.high_ref, f32[3,8,2,8,128]{4,3,2,1,0:T(8,128)S(1)} %get-tuple-element.40.w_ref, ...), custom_call_target="tpu_custom_call" | custom-call | tf_op jit(solution)/shard_map/pallas_call | solution.py:591
  (1 shorter events, 0.0 us)
Async XLA Ops:
  3.6 10.6 %collective-permute-start = (f32[8,2,8,128]{3,2,1,0:T(8,128)}, f32[8,2,8,128]{3,2,1,0:T(8,128)S(1)}, u32[]{:S(2)}, u32[]{:S(2)}) collective-permute-start(f32[8,2,8,128]{3,2,1,0:T(8,128)} %get-tuple-element.25), channel_id=1, source_target_pairs={{0,1},{1,2},{2,3},{3,4},{4,5},{5,6},{6,7},{7,8},{8,9},{9,10},{10,1... | collective-permute-start | bytes 196616 | tf_op jit(solution)/shard_map/ppermute | solution.py:604
  7.7 7.2 %collective-permute-start.1 = (f32[8,2,8,128]{3,2,1,0:T(8,128)}, f32[8,2,8,128]{3,2,1,0:T(8,128)S(1)}, u32[]{:S(2)}, u32[]{:S(2)}) collective-permute-start(f32[8,2,8,128]{3,2,1,0:T(8,128)} %get-tuple-element.26), channel_id=1, source_target_pairs={{0,15},{1,0},{2,1},{3,2},{4,3},{5,4},{6,5},{7,6},{8,7},{9,8},{10,9... | collective-permute-start | bytes 196616 | tf_op jit(solution)/shard_map/ppermute | solution.py:604
  13.2 0.9 %copy-start = (f32[3,8,2,8,128]{4,3,2,1,0:T(8,128)S(1)}, f32[3,8,2,8,128]{4,3,2,1,0:T(8,128)}, u32[]{:S(2)}) copy-start(f32[3,8,2,8,128]{4,3,2,1,0:T(8,128)} %get-tuple-element.23.r_ref) | copy-start | bytes 589828
  15.0 7.8 %collective-permute-start.2 = (f32[10,8,256]{2,1,0:T(8,128)S(1)}, f32[10,8,256]{2,1,0:T(8,128)S(1)}, u32[]{:S(2)}, u32[]{:S(2)}) collective-permute-start(f32[10,8,256]{2,1,0:T(8,128)S(1)} %get-tuple-element.27), channel_id=1, source_target_pairs={{0,16},{16,32},{32,48},{48,64},{64,80},{80,96},{96,112},{112,128},... | collective-permute-start | bytes 245768 | tf_op jit(solution)/shard_map/ppermute | solution.py:604
  18.2 4.8 %collective-permute-start.3 = (f32[10,8,256]{2,1,0:T(8,128)S(1)}, f32[10,8,256]{2,1,0:T(8,128)S(1)}, u32[]{:S(2)}, u32[]{:S(2)}) collective-permute-start(f32[10,8,256]{2,1,0:T(8,128)S(1)} %get-tuple-element.29), channel_id=1, source_target_pairs={{0,496},{16,0},{32,16},{48,32},{64,48},{80,64},{96,80},{112,96},{1... | collective-permute-start | bytes 245768 | tf_op jit(solution)/shard_map/ppermute | solution.py:604
  23.8 5.0 %collective-permute-start.5 = (f32[8,2,8,256]{3,2,1,0:T(8,128)S(1)}, f32[8,2,8,256]{3,2,1,0:T(8,128)S(1)}, u32[]{:S(2)}, u32[]{:S(2)}) collective-permute-start(f32[8,2,8,256]{3,2,1,0:T(8,128)S(1)} %get-tuple-element.31.mid_ref.refs_2_), channel_id=1, source_target_pairs={{0,16},{16,32},{32,48},{48,64},{64,80},{80,96},{96,112},{112,128},... | collective-permute-start | bytes 393224 | tf_op jit(solution)/shard_map/ppermute | solution.py:604
  23.8 5.1 %collective-permute-start.4 = (f32[8,2,8,256]{3,2,1,0:T(8,128)S(1)}, f32[8,2,8,256]{3,2,1,0:T(8,128)S(1)}, u32[]{:S(2)}, u32[]{:S(2)}) collective-permute-start(f32[8,2,8,256]{3,2,1,0:T(8,128)S(1)} %get-tuple-element.31.mid_ref.refs_2_), channel_id=1, source_target_pairs={{0,496},{16,0},{32,16},{48,32},{64,48},{80,64},{96,80},{112,96},{1... | collective-permute-start | bytes 393224 | tf_op jit(solution)/shard_map/ppermute | solution.py:604
  29.0 6.2 %collective-permute-start.6 = (f32[8,2,8,256]{3,2,1,0:T(8,128)S(1)}, f32[8,2,8,256]{3,2,1,0:T(8,128)S(1)}, u32[]{:S(2)}, u32[]{:S(2)}) collective-permute-start(f32[8,2,8,256]{3,2,1,0:T(8,128)S(1)} %collective-permute-done.5.left_ref.refs_1_), channel_id=1, source_target_pairs={{0,16},{16,32},{32,48},{48,64},{64,80},{80,96},{96,112},{112,128},... | collective-permute-start | bytes 393224 | tf_op jit(solution)/shard_map/ppermute | solution.py:604
  29.0 6.2 %collective-permute-start.7 = (f32[8,2,8,256]{3,2,1,0:T(8,128)S(1)}, f32[8,2,8,256]{3,2,1,0:T(8,128)S(1)}, u32[]{:S(2)}, u32[]{:S(2)}) collective-permute-start(f32[8,2,8,256]{3,2,1,0:T(8,128)S(1)} %collective-permute-done.4.right_ref.refs_3_), channel_id=1, source_target_pairs={{0,496},{16,0},{32,16},{48,32},{64,48},{80,64},{96,80},{112,96},{1... | collective-permute-start | bytes 393224 | tf_op jit(solution)/shard_map/ppermute | solution.py:604

commit v9 on v8

--- a/solution.py
+++ b/solution.py
@@ -257,7 +257,7 @@
             down_ref[z, e] = downs[z]
         return carry
 
-    lax.fori_loop(0, 2, body, 0)
+    lax.fori_loop(0, 2, body, 0, unroll=2)
 
 
 def hold_kernel(r_ref, turned_ref, dy_ref, ky_ref):
@@ -318,7 +318,7 @@
     return first_x, last_x, first_y, last_y
 
 
-def source_kernel(left_ref, mid_ref, right_ref, dy_ref, b_ref, w_ref, open_ref, t_ref):
+def source_kernel(left_ref, mid_ref, right_ref, dy_ref, b_ref, pack_ref, w_ref, open_ref, t_ref):
     lanes = 256
     dcoef = row_coefs(lanes, deriv)
     wx = node_x(lanes, node_weights)
@@ -328,6 +328,7 @@
     inv = node_x(lanes, inverse_mass) * node_y(lanes, inverse_mass)
     first_x, last_x, first_y, last_y = flags(lanes)
     inside = 1.0 - rim_mask(lanes).astype(f32)
+    half = iota(128, 1) < 64
 
     def wall(tile):
         return jnp.broadcast_to(tile[0:1, :], (8, lanes))
@@ -379,12 +380,28 @@
         faces = mid_ref[0, :, e]
         rows = sum_rows(slope[e - 1], slope[e], slope[e + 1], first_x, last_x)
         total = rows * (wx * my * wy) + t_ref[:, e]
+        edges = []
         for z in range(8):
             got = total[z] * float(-node_weights[z])
             if z in (0, 7):
                 face = wall(faces[z])
                 got = jnp.where(inside > 0.5, got * face, face)
             b_ref[z, e] = got
+            pack_ref[z, e] = own_lanes(got[None])[0]
+            edges.append(jnp.where(half, got[:, :128], got[:, 128:]))
+        for z in range(4):
+            pack_ref[8 + z, e] = jnp.where(
+                half, pltpu.roll(edges[z], 96, axis=1), pltpu.roll(edges[z + 4], 32, axis=1)
+            )
+
+
+def unpack(ref, z, e):
+    lane = iota(128, 1)
+    middle = pltpu.roll(ref[z, e], 64, axis=1)
+    edge = pltpu.roll(ref[8 + z % 4, e], 32 if z < 4 else 96, axis=1)
+    low = jnp.where(lane >= 64, middle, jnp.where(lane >= 32, edge, 0.0))
+    high = jnp.where(lane < 64, middle, jnp.where(lane < 96, edge, 0.0))
+    return jnp.concatenate([low, high], axis=1)
 
 
 def fold(value):
@@ -394,16 +411,15 @@
     return total
 
 
-def load_block(ref, at, v_ref, p_ref, rim, fill):
+def load_block(read, at, v_ref, p_ref, rim):
     for e in range(2):
         for z in range(8):
-            got = ref[z, e]
+            got = read(z, e)
             if z in (0, 7):
                 face = jnp.broadcast_to(got[0:1, :], got.shape)
                 p_ref[z // 7, at + e] = jnp.where(rim, 0.0, face)
                 got = jnp.where(rim, 0.0, got)
-            if fill:
-                v_ref[0, z, at + e] = got
+            v_ref[0, z, at + e] = got
 
 
 def krylov_tools(ky_ref, v_ref, k_ref, p_ref):
@@ -447,8 +463,9 @@
 
 def inner_kernel(left_ref, mid_ref, right_ref, ky_ref, v_ref, k_ref, acc_ref, p_ref):
     rim = rim_mask(256)
-    for at, ref in ((2, left_ref), (4, mid_ref), (6, right_ref)):
-        load_block(ref, at, v_ref, p_ref, rim, True)
+    load_block(lambda z, e: unpack(left_ref, z, e), 2, v_ref, p_ref, rim)
+    load_block(lambda z, e: mid_ref[z, e], 4, v_ref, p_ref, rim)
+    load_block(lambda z, e: unpack(right_ref, z, e), 6, v_ref, p_ref, rim)
     apply, step = krylov_tools(ky_ref, v_ref, k_ref, p_ref)
     slot = 0
     for j in range(3):
@@ -465,13 +482,15 @@
             over(3 + j, 7 - j, lambda e, j=j: step(j, e))
 
 
-def outer_kernel(*refs):
-    blocks = refs[:5]
-    v_in, k_in, acc_ref, ky_ref, v_out, m_out, v_ref, k_ref, p_ref = refs[5:]
+def outer_kernel(
+    left_ref, right_ref, v_in, k_in, acc_ref, p_in, ky_ref, v_out, m_out, v_ref, k_ref, p_ref
+):
     lanes = 256
     rim = rim_mask(lanes)
-    for k, ref in enumerate(blocks):
-        load_block(ref, 2 * k, v_ref, p_ref, rim, k in (0, 4))
+    load_block(lambda z, e: unpack(left_ref, z, e), 0, v_ref, p_ref, rim)
+    load_block(lambda z, e: unpack(right_ref, z, e), 8, v_ref, p_ref, rim)
+    for e in range(2, 8):
+        p_ref[:, e] = p_in[:, e]
     for j, els in ((0, (2, 3, 4, 5, 6, 7)), (1, (3, 4, 5, 6)), (2, (4, 5))):
         for e in els:
             v_ref[j, :, e] = v_in[j, :, e]
@@ -648,22 +667,27 @@
     )
     before = shift(up, "gx", 1)
     after = shift(down, "gx", -1)
-    source, moved, opened = call(
+    source, pack, moved, opened = call(
         source_kernel,
-        (shape(8, 2, 8, 256), shape(3, 8, 2, 8, 128), shape(2, 2, 8, 128)),
+        (shape(8, 2, 8, 256), shape(12, 2, 8, 128), shape(3, 8, 2, 8, 128), shape(2, 2, 8, 128)),
         [vm((8, 2, 8, 256), f32)],
         before, wide, after, dy,
     )
-    left = shift(source, "gx", 1)
-    right = shift(source, "gx", -1)
+    left = shift(pack, "gx", 1)
+    right = shift(pack, "gx", -1)
     right, left = lax.optimization_barrier((right, left))
     left2 = shift(left, "gx", 1)
     right2 = shift(right, "gx", -1)
     cost = pl.CostEstimate(flops=5 * 10**6, bytes_accessed=4 * 10**6, transcendentals=0)
-    low, images, acc = call(
+    low, images, acc, faces = call(
         inner_kernel,
-        (shape(3, 8, 10, 8, 256), shape(3, 8, 10, 8, 256), shape(9, 8, 256)),
-        [vm((2, 10, 8, 256), f32)],
+        (
+            shape(3, 8, 10, 8, 256),
+            shape(3, 8, 10, 8, 256),
+            shape(9, 8, 256),
+            shape(2, 10, 8, 256),
+        ),
+        [],
         left, source, right, ky,
         cost=cost,
     )
@@ -675,7 +699,7 @@
             vm((4, 8, 10, 8, 256), f32),
             vm((2, 10, 8, 256), f32),
         ],
-        left2, left, source, right, right2, low, images, acc, ky,
+        left2, right2, low, images, acc, faces, ky,
     )
     velocity, pressure = call(
         final_kernel,

time: 77.2 us -> 76.3 us (0.988)
  no operation moved by 1% of the time
where the time goes in v9:
time: 76.3 us; the launch traced here: 76.1 us
  blocking collectives  38.2 us (50%)
  starting transfers between devices  25.1 us (33%)
  Pallas kernels  8.57 us (11%)
  waiting for transfers between devices  2.45 us (3%)
  local copies, waits for them, and re-layouts  0.93 us (1%)
    ppermute x8, starting transfers between devices, shift(): lax.ppermute(value, axis, [(i, (i + by) % size) for i in range(size)])  25.1 us
    all_to_all x1, blocking collectives, total_rows(): return lax.all_to_all(part, 'gx', 0, 0, axis_index_groups=along, tiled=True)  20.9 us
    all_to_all x1, blocking collectives, total_rows(): lax.all_to_all(packed, ('gx', 'gy'), 0, 0, axis_index_groups=planes, tile...  17.3 us
    pallas_call x7, Pallas kernels, call(): pl.pallas_call(kernel, out_shape=out_shape, in_specs=[pl.BlockSpec(memory...  8.57 us
    ppermute x8, waiting for transfers between devices, shift(): lax.ppermute(value, axis, [(i, (i + by) % size) for i in range(size)])  2.45 us
  transfers between devices with their start and end apart: 8, of which 5 were waited for; matrix products, arithmetic and copies ran while one was open for 0% of the time, Pallas kernels for 2%

profile of v9, /device:TPU:1, one launch (start us, length us, event | category | flops | bytes accessed | tf_op | source)
XLA Modules:
  0.0 76.1 jit_solution(13945454451072386726)
XLA Ops:
  0.6 2.6 %shard_map.50 = (f32[3,8,2,8,128]{4,3,2,1,0:T(8,128)}, f32[8,2,8,128]{3,2,1,0:T(8,128)}, f32[8,2,8,128]{3,2,1,0:T(8,128)}) custom-call(f32[3,8,2,8,128]{4,3,2,1,0:T(8,128)} %bitcast.10, bf16[3,8,16,128]{3,2,1,0:T(8,128)(2,1)} %bitcast.11, s32[2,2,16]{2,1,0:T(2,128)} %faces_hbm.1), custom_call_target="tpu_custom_call" | custom-call | tf_op jit(solution)/shard_map/pallas_call | solution.py:610
  3.3 4.0 %collective-permute-start = (f32[8,2,8,128]{3,2,1,0:T(8,128)}, f32[8,2,8,128]{3,2,1,0:T(8,128)S(1)}, u32[]{:S(2)}, u32[]{:S(2)}) collective-permute-start(f32[8,2,8,128]{3,2,1,0:T(8,128)} %get-tuple-element.27), channel_id=1, source_target_pairs={{0,1},{1,2},{2,3},{3,4},{4,5},{5,6},{6,7},{7,8},{8,9},{9,10},{10,1... | collective-permute-start | bytes 196616 | tf_op jit(solution)/shard_map/ppermute | solution.py:623
  7.3 5.6 %collective-permute-start.1 = (f32[8,2,8,128]{3,2,1,0:T(8,128)}, f32[8,2,8,128]{3,2,1,0:T(8,128)S(1)}, u32[]{:S(2)}, u32[]{:S(2)}) collective-permute-start(f32[8,2,8,128]{3,2,1,0:T(8,128)} %get-tuple-element.28), channel_id=1, source_target_pairs={{0,15},{1,0},{2,1},{3,2},{4,3},{5,4},{6,5},{7,6},{8,7},{9,8},{10,9... | collective-permute-start | bytes 196616 | tf_op jit(solution)/shard_map/ppermute | solution.py:623
  12.9 0.0 copy-start
  12.9 0.9 %copy-done = f32[3,8,2,8,128]{4,3,2,1,0:T(8,128)S(1)} copy-done((f32[3,8,2,8,128]{4,3,2,1,0:T(8,128)S(1)}, f32[3,8,2,8,128]{4,3,2,1,0:T(8,128)}, u32[]{:S(2)}) %copy-start) | copy-done | bytes 196632
  13.8 0.1 shard_map.51
  13.9 0.0 collective-permute-done.left_ref
  13.9 0.6 collective-permute-done.1.right_ref
  14.5 0.2 shard_map.52
  14.7 3.2 %collective-permute-start.2 = (f32[10,8,256]{2,1,0:T(8,128)S(1)}, f32[10,8,256]{2,1,0:T(8,128)S(1)}, u32[]{:S(2)}, u32[]{:S(2)}) collective-permute-start(f32[10,8,256]{2,1,0:T(8,128)S(1)} %get-tuple-element.29), channel_id=1, source_target_pairs={{0,16},{16,32},{32,48},{48,64},{64,80},{80,96},{96,112},{112,128},... | collective-permute-start | bytes 245768 | tf_op jit(solution)/shard_map/ppermute | solution.py:623
  17.9 3.9 %collective-permute-start.3 = (f32[10,8,256]{2,1,0:T(8,128)S(1)}, f32[10,8,256]{2,1,0:T(8,128)S(1)}, u32[]{:S(2)}, u32[]{:S(2)}) collective-permute-start(f32[10,8,256]{2,1,0:T(8,128)S(1)} %get-tuple-element.31), channel_id=1, source_target_pairs={{0,496},{16,0},{32,16},{48,32},{64,48},{80,64},{96,80},{112,96},{1... | collective-permute-start | bytes 245768 | tf_op jit(solution)/shard_map/ppermute | solution.py:623
  21.7 0.7 collective-permute-done.2.left_ref
  22.5 0.2 collective-permute-done.3.right_ref
  22.7 0.9 %shard_map.53 = (f32[8,2,8,256]{3,2,1,0:T(8,128)S(1)}, f32[12,2,8,128]{3,2,1,0:T(8,128)S(1)}, f32[3,8,2,8,128]{4,3,2,1,0:T(8,128)S(1)}, f32[2,2,8,128]{3,2,1,0:T(8,128)S(1)}) custom-call(f32[10,8,256]{2,1,0:T(8,128)S(1)} %collective-permute-done.2.left_ref, f32[3,8,2,8,256]{4,3,2,1,0:T(8,128)S(1)} %get-tuple-element.30.mid_ref, ...), custom_call_target="tpu_custom_call" | custom-call | tf_op jit(solution)/shard_map/pallas_call | solution.py:610
  23.5 0.0 collective-permute-start.5
  23.6 4.1 %collective-permute-start.4 = (f32[12,2,8,128]{3,2,1,0:T(8,128)S(1)}, f32[12,2,8,128]{3,2,1,0:T(8,128)S(1)}, u32[]{:S(2)}, u32[]{:S(2)}) collective-permute-start(f32[12,2,8,128]{3,2,1,0:T(8,128)S(1)} %get-tuple-element.33), channel_id=1, source_target_pairs={{0,496},{16,0},{32,16},{48,32},{64,48},{80,64},{96,80},{112,96},{1... | collective-permute-start | bytes 294920 | tf_op jit(solution)/shard_map/ppermute | solution.py:623
  27.7 0.8 %collective-permute-done.5.left_ref = f32[12,2,8,128]{3,2,1,0:T(8,128)S(1)} collective-permute-done((f32[12,2,8,128]{3,2,1,0:T(8,128)S(1)}, f32[12,2,8,128]{3,2,1,0:T(8,128)S(1)}, u32[]{:S(2)}, u32[]{:S(2)}) %collective-permute-start.5) | collective-permute-done | bytes 98336 | tf_op jit(solution)/shard_map/ppermute | solution.py:623
  28.5 0.2 collective-permute-done.4.right_ref
  28.7 0.0 collective-permute-start.6
  28.7 4.3 %collective-permute-start.7 = (f32[12,2,8,128]{3,2,1,0:T(8,128)S(1)}, f32[12,2,8,128]{3,2,1,0:T(8,128)S(1)}, u32[]{:S(2)}, u32[]{:S(2)}) collective-permute-start(f32[12,2,8,128]{3,2,1,0:T(8,128)S(1)} %collective-permute-done.4.right_ref), channel_id=1, source_target_pairs={{0,496},{16,0},{32,16},{48,32},{64,48},{80,64},{96,80},{112,96},{1... | collective-permute-start | bytes 294920 | tf_op jit(solution)/shard_map/ppermute | solution.py:623
  32.9 1.7 %shard_map.54 = (f32[3,8,10,8,256]{4,3,2,1,0:T(8,128)S(1)}, f32[3,8,10,8,256]{4,3,2,1,0:T(8,128)S(1)}, f32[9,8,256]{2,1,0:T(8,128)S(1)}, f32[2,10,8,256]{3,2,1,0:T(8,128)S(1)}) custom-call(f32[12,2,8,128]{3,2,1,0:T(8,128)S(1)} %collective-permute-done.5.left_ref, f32[8,2,8,256]{3,2,1,0:T(8,128)S(1)} %get-tuple-element.36.mid_ref, ...), custom_call_target="tpu_custom_call" | custom-call | flops 5000000 | bytes 4000000 | tf_op jit(solution)/shard_map/pallas_call | solution.py:610
  34.6 0.0 collective-permute-done.6.left_ref
  34.6 0.0 collective-permute-done.7.right_ref
  34.6 1.8 %shard_map.55 = (f32[2,8,4,8,256]{4,3,2,1,0:T(8,128)S(1)}, f32[32,128]{1,0:T(8,128)S(1)}) custom-call(f32[12,2,8,128]{3,2,1,0:T(8,128)S(1)} %collective-permute-done.6.left_ref, f32[12,2,8,128]{3,2,1,0:T(8,128)S(1)} %collective-permute-done.7.right_ref, f32[3,8,10,8,256]{4,3,2,1,0:T(8,128)S(1)} %get-tuple-element.38.v_in.low_ref, ...), custom_call_target="tpu_custom_call" | custom-call | tf_op jit(solution)/shard_map/pallas_call | solution.py:610
  36.5 17.3 %all_to_all.17 = f32[32,1,128]{2,1,0:T(1,128)S(1)} all-to-all(f32[32,1,128]{2,1,0:T(1,128)S(1)} %bitcast.9), channel_id=1, replica_groups={{0,16,1,17,2,18,3,19,4,20,5,21,6,22,7,23,8,24,9,25,10,26,11,27,12,28,13..., dimensions={0} | all-to-all | bytes 32768 | tf_op jit(solution)/shard_map/all_to_all | solution.py:629
  53.8 0.1 reduce_sum.9
  53.9 20.9 %all_to_all.18 = f32[16,1,128]{2,1,0:T(1,128)S(1)} all-to-all(f32[16,1,128]{2,1,0:T(1,128)S(1)} %broadcast_in_dim.2), channel_id=1, replica_groups={{0,32,64,96,128,160,192,224,256,288,320,352,384,416,448,480},{16,48,80,..., dimensions={0} | all-to-all | bytes 16384 | tf_op jit(solution)/shard_map/all_to_all | solution.py:632
  74.8 1.3 %shard_map.56 = (f32[3,8,2,8,128]{4,3,2,1,0:T(8,128)}, f32[8,2,8,128]{3,2,1,0:T(8,128)}) custom-call(f32[16,128]{1,0:T(8,128)S(1)} %bitcast.8, f32[3,8,10,8,256]{4,3,2,1,0:T(8,128)S(1)} %get-tuple-element.38.v_in.low_ref, f32[2,8,4,8,256]{4,3,2,1,0:T(8,128)S(1)} %get-tuple-element.43.high_ref, f32[3,8,2,8,128]{4,3,2,1,0:T(8,128)S(1)} %get-tuple-element.44.w_ref, ...), custom_call_target="tpu_custom_call" | custom-call | tf_op jit(solution)/shard_map/pallas_call | solution.py:610
  (1 shorter events, 0.0 us)
Async XLA Ops:
  3.3 10.6 %collective-permute-start = (f32[8,2,8,128]{3,2,1,0:T(8,128)}, f32[8,2,8,128]{3,2,1,0:T(8,128)S(1)}, u32[]{:S(2)}, u32[]{:S(2)}) collective-permute-start(f32[8,2,8,128]{3,2,1,0:T(8,128)} %get-tuple-element.27), channel_id=1, source_target_pairs={{0,1},{1,2},{2,3},{3,4},{4,5},{5,6},{6,7},{7,8},{8,9},{9,10},{10,1... | collective-permute-start | bytes 196616 | tf_op jit(solution)/shard_map/ppermute | solution.py:623
  7.3 7.2 %collective-permute-start.1 = (f32[8,2,8,128]{3,2,1,0:T(8,128)}, f32[8,2,8,128]{3,2,1,0:T(8,128)S(1)}, u32[]{:S(2)}, u32[]{:S(2)}) collective-permute-start(f32[8,2,8,128]{3,2,1,0:T(8,128)} %get-tuple-element.28), channel_id=1, source_target_pairs={{0,15},{1,0},{2,1},{3,2},{4,3},{5,4},{6,5},{7,6},{8,7},{9,8},{10,9... | collective-permute-start | bytes 196616 | tf_op jit(solution)/shard_map/ppermute | solution.py:623
  12.9 0.9 %copy-start = (f32[3,8,2,8,128]{4,3,2,1,0:T(8,128)S(1)}, f32[3,8,2,8,128]{4,3,2,1,0:T(8,128)}, u32[]{:S(2)}) copy-start(f32[3,8,2,8,128]{4,3,2,1,0:T(8,128)} %get-tuple-element.25.r_ref) | copy-start | bytes 589828
  14.7 7.8 %collective-permute-start.2 = (f32[10,8,256]{2,1,0:T(8,128)S(1)}, f32[10,8,256]{2,1,0:T(8,128)S(1)}, u32[]{:S(2)}, u32[]{:S(2)}) collective-permute-start(f32[10,8,256]{2,1,0:T(8,128)S(1)} %get-tuple-element.29), channel_id=1, source_target_pairs={{0,16},{16,32},{32,48},{48,64},{64,80},{80,96},{96,112},{112,128},... | collective-permute-start | bytes 245768 | tf_op jit(solution)/shard_map/ppermute | solution.py:623
  17.9 4.8 %collective-permute-start.3 = (f32[10,8,256]{2,1,0:T(8,128)S(1)}, f32[10,8,256]{2,1,0:T(8,128)S(1)}, u32[]{:S(2)}, u32[]{:S(2)}) collective-permute-start(f32[10,8,256]{2,1,0:T(8,128)S(1)} %get-tuple-element.31), channel_id=1, source_target_pairs={{0,496},{16,0},{32,16},{48,32},{64,48},{80,64},{96,80},{112,96},{1... | collective-permute-start | bytes 245768 | tf_op jit(solution)/shard_map/ppermute | solution.py:623
  23.5 4.9 %collective-permute-start.5 = (f32[12,2,8,128]{3,2,1,0:T(8,128)S(1)}, f32[12,2,8,128]{3,2,1,0:T(8,128)S(1)}, u32[]{:S(2)}, u32[]{:S(2)}) collective-permute-start(f32[12,2,8,128]{3,2,1,0:T(8,128)S(1)} %get-tuple-element.33), channel_id=1, source_target_pairs={{0,16},{16,32},{32,48},{48,64},{64,80},{80,96},{96,112},{112,128},... | collective-permute-start | bytes 294920 | tf_op jit(solution)/shard_map/ppermute | solution.py:623
  23.6 5.1 %collective-permute-start.4 = (f32[12,2,8,128]{3,2,1,0:T(8,128)S(1)}, f32[12,2,8,128]{3,2,1,0:T(8,128)S(1)}, u32[]{:S(2)}, u32[]{:S(2)}) collective-permute-start(f32[12,2,8,128]{3,2,1,0:T(8,128)S(1)} %get-tuple-element.33), channel_id=1, source_target_pairs={{0,496},{16,0},{32,16},{48,32},{64,48},{80,64},{96,80},{112,96},{1... | collective-permute-start | bytes 294920 | tf_op jit(solution)/shard_map/ppermute | solution.py:623
  28.7 6.0 %collective-permute-start.6 = (f32[12,2,8,128]{3,2,1,0:T(8,128)S(1)}, f32[12,2,8,128]{3,2,1,0:T(8,128)S(1)}, u32[]{:S(2)}, u32[]{:S(2)}) collective-permute-start(f32[12,2,8,128]{3,2,1,0:T(8,128)S(1)} %collective-permute-done.5.left_ref), channel_id=1, source_target_pairs={{0,16},{16,32},{32,48},{48,64},{64,80},{80,96},{96,112},{112,128},... | collective-permute-start | bytes 294920 | tf_op jit(solution)/shard_map/ppermute | solution.py:623
  28.7 6.0 %collective-permute-start.7 = (f32[12,2,8,128]{3,2,1,0:T(8,128)S(1)}, f32[12,2,8,128]{3,2,1,0:T(8,128)S(1)}, u32[]{:S(2)}, u32[]{:S(2)}) collective-permute-start(f32[12,2,8,128]{3,2,1,0:T(8,128)S(1)} %collective-permute-done.4.right_ref), channel_id=1, source_target_pairs={{0,496},{16,0},{32,16},{48,32},{64,48},{80,64},{96,80},{112,96},{1... | collective-permute-start | bytes 294920 | tf_op jit(solution)/shard_map/ppermute | solution.py:623

commit v10 on v9

--- a/solution.py
+++ b/solution.py
@@ -623,13 +623,27 @@
     return lax.ppermute(value, axis, [(i, (i + by) % size) for i in range(size)])
 
 
+def sum_groups(nx, ny):
+    side = 4 if ny % 4 == 0 else 1
+    near = [
+        [(2 * z + c) * ny + x * side + y for y in range(side) for c in range(2)]
+        for z in range(nx // 2)
+        for x in range(ny // side)
+    ]
+    far = [
+        [(2 * z + c) * ny + x * side + y for z in range(nx // 2) for x in range(ny // side)]
+        for y in range(side)
+        for c in range(2)
+    ]
+    return near, far
+
+
 def total_rows(packed):
-    nx, ny = lax.axis_size("gx"), lax.axis_size("gy")
-    planes = [[(2 * z + c) * ny + y for y in range(ny) for c in range(2)] for z in range(nx // 2)]
-    part = lax.all_to_all(packed, ("gx", "gy"), 0, 0, axis_index_groups=planes, tiled=True)
-    part = jnp.broadcast_to(jnp.sum(part, axis=0, keepdims=True), (nx // 2, 128))
-    along = [[2 * z + c for z in range(nx // 2)] for c in range(2)]
-    return lax.all_to_all(part, "gx", 0, 0, axis_index_groups=along, tiled=True)
+    near, far = sum_groups(lax.axis_size("gx"), lax.axis_size("gy"))
+    both = ("gx", "gy")
+    part = lax.all_to_all(packed, both, 0, 0, axis_index_groups=near, tiled=True)
+    part = jnp.broadcast_to(jnp.sum(part, axis=0, keepdims=True), (len(far[0]), 128))
+    return lax.all_to_all(part, both, 0, 0, axis_index_groups=far, tiled=True)
 
 
 def local(adjoint, checkpoints, wall_faces):
@@ -693,7 +707,7 @@
     )
     high, packed = call(
         outer_kernel,
-        (shape(2, 8, 4, 8, 256), shape(2 * lax.axis_size("gy"), 128)),
+        (shape(2, 8, 4, 8, 256), shape(len(sum_groups(lax.axis_size("gx"), lax.axis_size("gy"))[0][0]), 128)),
         [
             vm((4, 8, 10, 8, 256), f32),
             vm((4, 8, 10, 8, 256), f32),

time: 76.3 us -> 76.9 us (level)
  no operation moved by 1% of the time
where the time goes in v10:
time: 76.9 us; the launch traced here: 76.6 us
  blocking collectives  38.8 us (50%)
  starting transfers between devices  25.1 us (33%)
  Pallas kernels  8.57 us (11%)
  waiting for transfers between devices  2.45 us (3%)
  local copies, waits for them, and re-layouts  0.94 us (1%)
    all_to_all x1, blocking collectives, total_rows(): return lax.all_to_all(part, both, 0, 0, axis_index_groups=far, tiled=True)  27.2 us
    ppermute x8, starting transfers between devices, shift(): lax.ppermute(value, axis, [(i, (i + by) % size) for i in range(size)])  25.1 us
    all_to_all x1, blocking collectives, total_rows(): lax.all_to_all(packed, both, 0, 0, axis_index_groups=near, tiled=True)  11.6 us
    pallas_call x7, Pallas kernels, call(): pl.pallas_call(kernel, out_shape=out_shape, in_specs=[pl.BlockSpec(memory...  8.57 us
    ppermute x8, waiting for transfers between devices, shift(): lax.ppermute(value, axis, [(i, (i + by) % size) for i in range(size)])  2.45 us
  transfers between devices with their start and end apart: 8, of which 5 were waited for; matrix products, arithmetic and copies ran while one was open for 0% of the time, Pallas kernels for 2%

profile of v10, /device:TPU:1, one launch (start us, length us, event | category | flops | bytes accessed | tf_op | source)
XLA Modules:
  0.0 76.6 jit_solution(3054806406200995935)
XLA Ops:
  0.6 2.6 %shard_map.50 = (f32[3,8,2,8,128]{4,3,2,1,0:T(8,128)}, f32[8,2,8,128]{3,2,1,0:T(8,128)}, f32[8,2,8,128]{3,2,1,0:T(8,128)}) custom-call(f32[3,8,2,8,128]{4,3,2,1,0:T(8,128)} %bitcast.10, bf16[3,8,16,128]{3,2,1,0:T(8,128)(2,1)} %bitcast.11, s32[2,2,16]{2,1,0:T(2,128)} %faces_hbm.1), custom_call_target="tpu_custom_call" | custom-call | tf_op jit(solution)/shard_map/pallas_call | solution.py:610
  3.3 4.0 %collective-permute-start = (f32[8,2,8,128]{3,2,1,0:T(8,128)}, f32[8,2,8,128]{3,2,1,0:T(8,128)S(1)}, u32[]{:S(2)}, u32[]{:S(2)}) collective-permute-start(f32[8,2,8,128]{3,2,1,0:T(8,128)} %get-tuple-element.27), channel_id=1, source_target_pairs={{0,1},{1,2},{2,3},{3,4},{4,5},{5,6},{6,7},{7,8},{8,9},{9,10},{10,1... | collective-permute-start | bytes 196616 | tf_op jit(solution)/shard_map/ppermute | solution.py:623
  7.3 5.6 %collective-permute-start.1 = (f32[8,2,8,128]{3,2,1,0:T(8,128)}, f32[8,2,8,128]{3,2,1,0:T(8,128)S(1)}, u32[]{:S(2)}, u32[]{:S(2)}) collective-permute-start(f32[8,2,8,128]{3,2,1,0:T(8,128)} %get-tuple-element.28), channel_id=1, source_target_pairs={{0,15},{1,0},{2,1},{3,2},{4,3},{5,4},{6,5},{7,6},{8,7},{9,8},{10,9... | collective-permute-start | bytes 196616 | tf_op jit(solution)/shard_map/ppermute | solution.py:623
  12.9 0.0 copy-start
  12.9 0.9 %copy-done = f32[3,8,2,8,128]{4,3,2,1,0:T(8,128)S(1)} copy-done((f32[3,8,2,8,128]{4,3,2,1,0:T(8,128)S(1)}, f32[3,8,2,8,128]{4,3,2,1,0:T(8,128)}, u32[]{:S(2)}) %copy-start) | copy-done | bytes 196632
  13.8 0.1 shard_map.51
  13.9 0.0 collective-permute-done.left_ref
  13.9 0.6 collective-permute-done.1.right_ref
  14.5 0.2 shard_map.52
  14.7 3.2 %collective-permute-start.2 = (f32[10,8,256]{2,1,0:T(8,128)S(1)}, f32[10,8,256]{2,1,0:T(8,128)S(1)}, u32[]{:S(2)}, u32[]{:S(2)}) collective-permute-start(f32[10,8,256]{2,1,0:T(8,128)S(1)} %get-tuple-element.29), channel_id=1, source_target_pairs={{0,16},{16,32},{32,48},{48,64},{64,80},{80,96},{96,112},{112,128},... | collective-permute-start | bytes 245768 | tf_op jit(solution)/shard_map/ppermute | solution.py:623
  17.9 3.9 %collective-permute-start.3 = (f32[10,8,256]{2,1,0:T(8,128)S(1)}, f32[10,8,256]{2,1,0:T(8,128)S(1)}, u32[]{:S(2)}, u32[]{:S(2)}) collective-permute-start(f32[10,8,256]{2,1,0:T(8,128)S(1)} %get-tuple-element.31), channel_id=1, source_target_pairs={{0,496},{16,0},{32,16},{48,32},{64,48},{80,64},{96,80},{112,96},{1... | collective-permute-start | bytes 245768 | tf_op jit(solution)/shard_map/ppermute | solution.py:623
  21.7 0.7 collective-permute-done.2.left_ref
  22.5 0.2 collective-permute-done.3.right_ref
  22.7 0.9 %shard_map.53 = (f32[8,2,8,256]{3,2,1,0:T(8,128)S(1)}, f32[12,2,8,128]{3,2,1,0:T(8,128)S(1)}, f32[3,8,2,8,128]{4,3,2,1,0:T(8,128)S(1)}, f32[2,2,8,128]{3,2,1,0:T(8,128)S(1)}) custom-call(f32[10,8,256]{2,1,0:T(8,128)S(1)} %collective-permute-done.2.left_ref, f32[3,8,2,8,256]{4,3,2,1,0:T(8,128)S(1)} %get-tuple-element.30.mid_ref, ...), custom_call_target="tpu_custom_call" | custom-call | tf_op jit(solution)/shard_map/pallas_call | solution.py:610
  23.5 0.0 collective-permute-start.5
  23.6 4.1 %collective-permute-start.4 = (f32[12,2,8,128]{3,2,1,0:T(8,128)S(1)}, f32[12,2,8,128]{3,2,1,0:T(8,128)S(1)}, u32[]{:S(2)}, u32[]{:S(2)}) collective-permute-start(f32[12,2,8,128]{3,2,1,0:T(8,128)S(1)} %get-tuple-element.33), channel_id=1, source_target_pairs={{0,496},{16,0},{32,16},{48,32},{64,48},{80,64},{96,80},{112,96},{1... | collective-permute-start | bytes 294920 | tf_op jit(solution)/shard_map/ppermute | solution.py:623
  27.7 0.8 %collective-permute-done.5.left_ref = f32[12,2,8,128]{3,2,1,0:T(8,128)S(1)} collective-permute-done((f32[12,2,8,128]{3,2,1,0:T(8,128)S(1)}, f32[12,2,8,128]{3,2,1,0:T(8,128)S(1)}, u32[]{:S(2)}, u32[]{:S(2)}) %collective-permute-start.5) | collective-permute-done | bytes 98336 | tf_op jit(solution)/shard_map/ppermute | solution.py:623
  28.5 0.2 collective-permute-done.4.right_ref
  28.7 0.0 collective-permute-start.6
  28.7 4.3 %collective-permute-start.7 = (f32[12,2,8,128]{3,2,1,0:T(8,128)S(1)}, f32[12,2,8,128]{3,2,1,0:T(8,128)S(1)}, u32[]{:S(2)}, u32[]{:S(2)}) collective-permute-start(f32[12,2,8,128]{3,2,1,0:T(8,128)S(1)} %collective-permute-done.4.right_ref), channel_id=1, source_target_pairs={{0,496},{16,0},{32,16},{48,32},{64,48},{80,64},{96,80},{112,96},{1... | collective-permute-start | bytes 294920 | tf_op jit(solution)/shard_map/ppermute | solution.py:623
  32.9 1.7 %shard_map.54 = (f32[3,8,10,8,256]{4,3,2,1,0:T(8,128)S(1)}, f32[3,8,10,8,256]{4,3,2,1,0:T(8,128)S(1)}, f32[9,8,256]{2,1,0:T(8,128)S(1)}, f32[2,10,8,256]{3,2,1,0:T(8,128)S(1)}) custom-call(f32[12,2,8,128]{3,2,1,0:T(8,128)S(1)} %collective-permute-done.5.left_ref, f32[8,2,8,256]{3,2,1,0:T(8,128)S(1)} %get-tuple-element.36.mid_ref, ...), custom_call_target="tpu_custom_call" | custom-call | flops 5000000 | bytes 4000000 | tf_op jit(solution)/shard_map/pallas_call | solution.py:610
  34.6 0.0 collective-permute-done.6.left_ref
  34.6 0.0 collective-permute-done.7.right_ref
  34.6 1.8 %shard_map.55 = (f32[2,8,4,8,256]{4,3,2,1,0:T(8,128)S(1)}, f32[8,128]{1,0:T(8,128)S(1)}) custom-call(f32[12,2,8,128]{3,2,1,0:T(8,128)S(1)} %collective-permute-done.6.left_ref, f32[12,2,8,128]{3,2,1,0:T(8,128)S(1)} %collective-permute-done.7.right_ref, f32[3,8,10,8,256]{4,3,2,1,0:T(8,128)S(1)} %get-tuple-element.38.v_in.low_ref, ...), custom_call_target="tpu_custom_call" | custom-call | tf_op jit(solution)/shard_map/pallas_call | solution.py:610
  36.5 11.6 %all_to_all.17 = f32[8,1,128]{2,1,0:T(1,128)S(1)} all-to-all(f32[8,1,128]{2,1,0:T(1,128)S(1)} %bitcast.9), channel_id=1, replica_groups={{0,16,1,17,2,18,3,19},{4,20,5,21,6,22,7,23},{8,24,9,25,10,26,11,27},{12..., dimensions={0} | all-to-all | bytes 8192 | tf_op jit(solution)/shard_map/all_to_all | solution.py:644
  48.1 27.2 %all_to_all.18 = f32[64,1,128]{2,1,0:T(1,128)S(1)} all-to-all(f32[64,1,128]{2,1,0:T(1,128)S(1)} %broadcast_in_dim.2), channel_id=1, replica_groups={{0,4,8,12,32,36,40,44,64,68,72,76,96,100,104,108,128,132,136,140,160,16..., dimensions={0} | all-to-all | bytes 65536 | tf_op jit(solution)/shard_map/all_to_all | solution.py:646
  75.3 1.3 %shard_map.56 = (f32[3,8,2,8,128]{4,3,2,1,0:T(8,128)}, f32[8,2,8,128]{3,2,1,0:T(8,128)}) custom-call(f32[64,128]{1,0:T(8,128)S(1)} %bitcast.8, f32[3,8,10,8,256]{4,3,2,1,0:T(8,128)S(1)} %get-tuple-element.38.v_in.low_ref, f32[2,8,4,8,256]{4,3,2,1,0:T(8,128)S(1)} %get-tuple-element.43.high_ref, f32[3,8,2,8,128]{4,3,2,1,0:T(8,128)S(1)} %get-tuple-element.44.w_ref, ...), custom_call_target="tpu_custom_call" | custom-call | tf_op jit(solution)/shard_map/pallas_call | solution.py:610
  (2 shorter events, 0.0 us)
Async XLA Ops:
  3.3 10.6 %collective-permute-start = (f32[8,2,8,128]{3,2,1,0:T(8,128)}, f32[8,2,8,128]{3,2,1,0:T(8,128)S(1)}, u32[]{:S(2)}, u32[]{:S(2)}) collective-permute-start(f32[8,2,8,128]{3,2,1,0:T(8,128)} %get-tuple-element.27), channel_id=1, source_target_pairs={{0,1},{1,2},{2,3},{3,4},{4,5},{5,6},{6,7},{7,8},{8,9},{9,10},{10,1... | collective-permute-start | bytes 196616 | tf_op jit(solution)/shard_map/ppermute | solution.py:623
  7.3 7.2 %collective-permute-start.1 = (f32[8,2,8,128]{3,2,1,0:T(8,128)}, f32[8,2,8,128]{3,2,1,0:T(8,128)S(1)}, u32[]{:S(2)}, u32[]{:S(2)}) collective-permute-start(f32[8,2,8,128]{3,2,1,0:T(8,128)} %get-tuple-element.28), channel_id=1, source_target_pairs={{0,15},{1,0},{2,1},{3,2},{4,3},{5,4},{6,5},{7,6},{8,7},{9,8},{10,9... | collective-permute-start | bytes 196616 | tf_op jit(solution)/shard_map/ppermute | solution.py:623
  12.9 0.9 %copy-start = (f32[3,8,2,8,128]{4,3,2,1,0:T(8,128)S(1)}, f32[3,8,2,8,128]{4,3,2,1,0:T(8,128)}, u32[]{:S(2)}) copy-start(f32[3,8,2,8,128]{4,3,2,1,0:T(8,128)} %get-tuple-element.25.r_ref) | copy-start | bytes 589828
  14.7 7.8 %collective-permute-start.2 = (f32[10,8,256]{2,1,0:T(8,128)S(1)}, f32[10,8,256]{2,1,0:T(8,128)S(1)}, u32[]{:S(2)}, u32[]{:S(2)}) collective-permute-start(f32[10,8,256]{2,1,0:T(8,128)S(1)} %get-tuple-element.29), channel_id=1, source_target_pairs={{0,16},{16,32},{32,48},{48,64},{64,80},{80,96},{96,112},{112,128},... | collective-permute-start | bytes 245768 | tf_op jit(solution)/shard_map/ppermute | solution.py:623
  17.9 4.8 %collective-permute-start.3 = (f32[10,8,256]{2,1,0:T(8,128)S(1)}, f32[10,8,256]{2,1,0:T(8,128)S(1)}, u32[]{:S(2)}, u32[]{:S(2)}) collective-permute-start(f32[10,8,256]{2,1,0:T(8,128)S(1)} %get-tuple-element.31), channel_id=1, source_target_pairs={{0,496},{16,0},{32,16},{48,32},{64,48},{80,64},{96,80},{112,96},{1... | collective-permute-start | bytes 245768 | tf_op jit(solution)/shard_map/ppermute | solution.py:623
  23.5 4.9 %collective-permute-start.5 = (f32[12,2,8,128]{3,2,1,0:T(8,128)S(1)}, f32[12,2,8,128]{3,2,1,0:T(8,128)S(1)}, u32[]{:S(2)}, u32[]{:S(2)}) collective-permute-start(f32[12,2,8,128]{3,2,1,0:T(8,128)S(1)} %get-tuple-element.33), channel_id=1, source_target_pairs={{0,16},{16,32},{32,48},{48,64},{64,80},{80,96},{96,112},{112,128},... | collective-permute-start | bytes 294920 | tf_op jit(solution)/shard_map/ppermute | solution.py:623
  23.6 5.1 %collective-permute-start.4 = (f32[12,2,8,128]{3,2,1,0:T(8,128)S(1)}, f32[12,2,8,128]{3,2,1,0:T(8,128)S(1)}, u32[]{:S(2)}, u32[]{:S(2)}) collective-permute-start(f32[12,2,8,128]{3,2,1,0:T(8,128)S(1)} %get-tuple-element.33), channel_id=1, source_target_pairs={{0,496},{16,0},{32,16},{48,32},{64,48},{80,64},{96,80},{112,96},{1... | collective-permute-start | bytes 294920 | tf_op jit(solution)/shard_map/ppermute | solution.py:623
  28.7 6.0 %collective-permute-start.6 = (f32[12,2,8,128]{3,2,1,0:T(8,128)S(1)}, f32[12,2,8,128]{3,2,1,0:T(8,128)S(1)}, u32[]{:S(2)}, u32[]{:S(2)}) collective-permute-start(f32[12,2,8,128]{3,2,1,0:T(8,128)S(1)} %collective-permute-done.5.left_ref), channel_id=1, source_target_pairs={{0,16},{16,32},{32,48},{48,64},{64,80},{80,96},{96,112},{112,128},... | collective-permute-start | bytes 294920 | tf_op jit(solution)/shard_map/ppermute | solution.py:623
  28.7 6.0 %collective-permute-start.7 = (f32[12,2,8,128]{3,2,1,0:T(8,128)S(1)}, f32[12,2,8,128]{3,2,1,0:T(8,128)S(1)}, u32[]{:S(2)}, u32[]{:S(2)}) collective-permute-start(f32[12,2,8,128]{3,2,1,0:T(8,128)S(1)} %collective-permute-done.4.right_ref), channel_id=1, source_target_pairs={{0,496},{16,0},{32,16},{48,32},{64,48},{80,64},{96,80},{112,96},{1... | collective-permute-start | bytes 294920 | tf_op jit(solution)/shard_map/ppermute | solution.py:623

commit v11 on v9

--- a/solution.py
+++ b/solution.py
@@ -461,41 +461,50 @@
     over(0, 4, lambda t: body(low + t + (t // 2) * (6 - 2 * low)))
 
 
-def inner_kernel(left_ref, mid_ref, right_ref, ky_ref, v_ref, k_ref, acc_ref, p_ref):
+def pack_sums(parts, packed):
+    lane = iota(256, 1)
+    own = (lane >= 64) & (lane < 192)
+    share = node_x(256, 1.0 / copies) * node_y(256, 1.0 / copies)
+    lane = iota(128, 1)
+    for k, part in parts.items():
+        part = jnp.where(own, part, 0.0)
+        if k >= 10:
+            part = part * share
+        part = part[:, :128] + part[:, 128:]
+        total = jnp.sum(jnp.sum(part, axis=0, keepdims=True), axis=1, keepdims=True)
+        packed = jnp.where(lane == k, total, packed)
+    return packed
+
+
+def own_product(former, latter):
+    return fold(former(4) * latter(4)) + fold(former(5) * latter(5))
+
+
+def inner_kernel(left_ref, mid_ref, right_ref, ky_ref, v_ref, k_ref, p_ref, sum_ref):
     rim = rim_mask(256)
     load_block(lambda z, e: unpack(left_ref, z, e), 2, v_ref, p_ref, rim)
     load_block(lambda z, e: mid_ref[z, e], 4, v_ref, p_ref, rim)
     load_block(lambda z, e: unpack(right_ref, z, e), 6, v_ref, p_ref, rim)
     apply, step = krylov_tools(ky_ref, v_ref, k_ref, p_ref)
-    slot = 0
+    parts = {}
     for j in range(3):
         over(2 + j, 8 - j, lambda e, j=j: apply(j, e))
         for i in range(j + 1):
-            acc_ref[slot + i] = fold(v_ref[i, :, 4] * k_ref[j, :, 4]) + fold(
-                v_ref[i, :, 5] * k_ref[j, :, 5]
+            parts[j * (j + 1) // 2 + i] = own_product(
+                lambda e, i=i: v_ref[i, :, e], lambda e, j=j: k_ref[j, :, e]
             )
-        acc_ref[6 + j] = fold(v_ref[j, :, 4] * v_ref[0, :, 4]) + fold(
-            v_ref[j, :, 5] * v_ref[0, :, 5]
-        )
-        slot += j + 1
+        parts[10 + j] = own_product(lambda e, j=j: v_ref[j, :, e], lambda e: v_ref[0, :, e])
         if j < 2:
             over(3 + j, 7 - j, lambda e, j=j: step(j, e))
+    sum_ref[...] = pack_sums(parts, jnp.zeros((8, 128), f32))
 
 
 def outer_kernel(
-    left_ref, right_ref, v_in, k_in, acc_ref, p_in, ky_ref, v_out, m_out, v_ref, k_ref, p_ref
+    left_ref, right_ref, sum_ref, ky_ref, v_in, k_in, p_in, v_ref, k_ref, p_ref, m_out
 ):
-    lanes = 256
-    rim = rim_mask(lanes)
+    rim = rim_mask(256)
     load_block(lambda z, e: unpack(left_ref, z, e), 0, v_ref, p_ref, rim)
     load_block(lambda z, e: unpack(right_ref, z, e), 8, v_ref, p_ref, rim)
-    for e in range(2, 8):
-        p_ref[:, e] = p_in[:, e]
-    for j, els in ((0, (2, 3, 4, 5, 6, 7)), (1, (3, 4, 5, 6)), (2, (4, 5))):
-        for e in els:
-            v_ref[j, :, e] = v_in[j, :, e]
-            if j or e not in (4, 5):
-                k_ref[j, :, e] = k_in[j, :, e]
     apply, step = krylov_tools(ky_ref, v_ref, k_ref, p_ref)
     for j in range(3):
         sides(j, lambda e, j=j: apply(j, e))
@@ -504,35 +513,16 @@
         else:
             over(3, 7, lambda e: step(2, e))
     over(4, 6, lambda e: apply(3, e))
-    for e in range(4):
-        v_out[0, :, e] = v_ref[2, :, 3 + e]
-        v_out[1, :, e] = v_ref[3, :, 3 + e]
-    energy = [acc_ref[k] for k in range(6)]
+    parts = {}
     for i in range(ROUNDS):
-        energy.append(
-            fold(v_ref[i, :, 4] * k_ref[3, :, 4]) + fold(v_ref[i, :, 5] * k_ref[3, :, 5])
-        )
-    load = [acc_ref[6 + k] for k in range(3)]
-    load.append(
-        fold(v_ref[3, :, 4] * v_ref[0, :, 4]) + fold(v_ref[3, :, 5] * v_ref[0, :, 5])
-    )
-    lane = iota(lanes, 1)
-    own = (lane >= 64) & (lane < 192)
-    share = node_x(lanes, 1.0 / copies) * node_y(lanes, 1.0 / copies)
-    lane = iota(128, 1)
-    packed = jnp.zeros((8, 128), f32)
-    for k, part in enumerate(energy + load):
-        part = jnp.where(own, part, 0.0)
-        if k >= 10:
-            part = part * share
-        part = part[:, :128] + part[:, 128:]
-        total = jnp.sum(jnp.sum(part, axis=0, keepdims=True), axis=1, keepdims=True)
-        packed = jnp.where(lane == k, total, packed)
+        parts[6 + i] = own_product(lambda e, i=i: v_ref[i, :, e], lambda e: k_ref[3, :, e])
+    parts[13] = own_product(lambda e: v_ref[3, :, e], lambda e: v_ref[0, :, e])
+    packed = pack_sums(parts, sum_ref[...])
     for k in range(m_out.shape[0] // 8):
         m_out[8 * k : 8 * k + 8] = packed
 
 
-def final_kernel(m_ref, low_ref, high_ref, w_ref, open_ref, dy_ref, out_ref, q_ref):
+def final_kernel(m_ref, v_ref, w_ref, open_ref, dy_ref, out_ref, q_ref):
     lanes = 256
     parts = [m_ref[8 * k : 8 * k + 8] for k in range(m_ref.shape[0] // 8)]
     while len(parts) > 1:
@@ -583,8 +573,9 @@
     mean_y = node_y(lanes, 1.0 / copies)
     q, slope = [], []
     for e in range(4):
-        got = low_ref[0, :, 3 + e] * coef[0] + low_ref[1, :, 3 + e] * coef[1]
-        got = got + high_ref[0, :, e] * coef[2] + high_ref[1, :, e] * coef[3]
+        got = v_ref[0, :, 3 + e] * coef[0]
+        for j in range(1, ROUNDS):
+            got = got + v_ref[j, :, 3 + e] * coef[j]
         q.append(got)
         slope.append(weigh(row_turns(got), dcoef))
     for e in range(2):
@@ -606,7 +597,7 @@
     return jax.ShapeDtypeStruct(dims, f32)
 
 
-def call(kernel, out_shape, scratch, *args, space=pltpu.VMEM, vmem=48, cost=None):
+def call(kernel, out_shape, scratch, *args, space=pltpu.VMEM, vmem=48, cost=None, aliases={}):
     return pl.pallas_call(
         kernel,
         out_shape=out_shape,
@@ -614,6 +605,7 @@
         out_specs=jax.tree.map(lambda s: pl.BlockSpec(memory_space=pltpu.VMEM), out_shape),
         scratch_shapes=scratch,
         cost_estimate=cost,
+        input_output_aliases=aliases,
         compiler_params=pltpu.CompilerParams(vmem_limit_bytes=int(vmem * 2**20)),
     )(*args)
 
@@ -679,33 +671,22 @@
     left2 = shift(left, "gx", 1)
     right2 = shift(right, "gx", -1)
     cost = pl.CostEstimate(flops=5 * 10**6, bytes_accessed=4 * 10**6, transcendentals=0)
-    low, images, acc, faces = call(
-        inner_kernel,
-        (
-            shape(3, 8, 10, 8, 256),
-            shape(3, 8, 10, 8, 256),
-            shape(9, 8, 256),
-            shape(2, 10, 8, 256),
-        ),
+    state = (shape(4, 8, 10, 8, 256), shape(4, 8, 10, 8, 256), shape(2, 10, 8, 256))
+    basis, images, faces, known = call(
+        inner_kernel, state + (shape(8, 128),), [], left, source, right, ky, cost=cost
+    )
+    basis, images, faces, packed = call(
+        outer_kernel,
+        state + (shape(2 * lax.axis_size("gy"), 128),),
         [],
-        left, source, right, ky,
-        cost=cost,
-    )
-    high, packed = call(
-        outer_kernel,
-        (shape(2, 8, 4, 8, 256), shape(2 * lax.axis_size("gy"), 128)),
-        [
-            vm((4, 8, 10, 8, 256), f32),
-            vm((4, 8, 10, 8, 256), f32),
-            vm((2, 10, 8, 256), f32),
-        ],
-        left2, right2, low, images, acc, faces, ky,
+        left2, right2, known, ky, basis, images, faces,
+        aliases={4: 0, 5: 1, 6: 2},
     )
     velocity, pressure = call(
         final_kernel,
         (shape(3, 8, 2, 8, 128), shape(8, 2, 8, 128)),
         [],
-        total_rows(packed), low, high, moved, opened, dy,
+        total_rows(packed), basis, moved, opened, dy,
     )
     return velocity.reshape(3, 8, 16, 128), pressure.reshape(8, 16, 128)
 

time: 76.3 us -> 76.3 us (level)
  no operation moved by 1% of the time
where the time goes in v11:
time: 76.3 us; the launch traced here: 76.1 us
  blocking collectives  38.2 us (50%)
  starting transfers between devices  25.1 us (33%)
  Pallas kernels  8.63 us (11%)
  waiting for transfers between devices  2.45 us (3%)
  local copies, waits for them, and re-layouts  0.93 us (1%)
    ppermute x8, starting transfers between devices, shift(): lax.ppermute(value, axis, [(i, (i + by) % size) for i in range(size)])  25.1 us
    all_to_all x1, blocking collectives, total_rows(): return lax.all_to_all(part, 'gx', 0, 0, axis_index_groups=along, tiled=True)  20.9 us
    all_to_all x1, blocking collectives, total_rows(): lax.all_to_all(packed, ('gx', 'gy'), 0, 0, axis_index_groups=planes, tile...  17.3 us
    pallas_call x7, Pallas kernels, call(): pl.pallas_call(kernel, out_shape=out_shape, in_specs=[pl.BlockSpec(memory...  8.63 us
    ppermute x8, waiting for transfers between devices, shift(): lax.ppermute(value, axis, [(i, (i + by) % size) for i in range(size)])  2.45 us
  transfers between devices with their start and end apart: 8, of which 5 were waited for; matrix products, arithmetic and copies ran while one was open for 0% of the time, Pallas kernels for 2%

profile of v11, /device:TPU:1, one launch (start us, length us, event | category | flops | bytes accessed | tf_op | source)
XLA Modules:
  0.0 76.1 jit_solution(4318090203015869264)
XLA Ops:
  0.6 2.6 %shard_map.50 = (f32[3,8,2,8,128]{4,3,2,1,0:T(8,128)}, f32[8,2,8,128]{3,2,1,0:T(8,128)}, f32[8,2,8,128]{3,2,1,0:T(8,128)}) custom-call(f32[3,8,2,8,128]{4,3,2,1,0:T(8,128)} %bitcast.10, bf16[3,8,16,128]{3,2,1,0:T(8,128)(2,1)} %bitcast.11, s32[2,2,16]{2,1,0:T(2,128)} %faces_hbm.1), custom_call_target="tpu_custom_call" | custom-call | tf_op jit(solution)/shard_map/pallas_call | solution.py:601
  3.3 4.0 %collective-permute-start = (f32[8,2,8,128]{3,2,1,0:T(8,128)}, f32[8,2,8,128]{3,2,1,0:T(8,128)S(1)}, u32[]{:S(2)}, u32[]{:S(2)}) collective-permute-start(f32[8,2,8,128]{3,2,1,0:T(8,128)} %get-tuple-element.27), channel_id=1, source_target_pairs={{0,1},{1,2},{2,3},{3,4},{4,5},{5,6},{6,7},{7,8},{8,9},{9,10},{10,1... | collective-permute-start | bytes 196616 | tf_op jit(solution)/shard_map/ppermute | solution.py:615
  7.3 5.6 %collective-permute-start.1 = (f32[8,2,8,128]{3,2,1,0:T(8,128)}, f32[8,2,8,128]{3,2,1,0:T(8,128)S(1)}, u32[]{:S(2)}, u32[]{:S(2)}) collective-permute-start(f32[8,2,8,128]{3,2,1,0:T(8,128)} %get-tuple-element.28), channel_id=1, source_target_pairs={{0,15},{1,0},{2,1},{3,2},{4,3},{5,4},{6,5},{7,6},{8,7},{9,8},{10,9... | collective-permute-start | bytes 196616 | tf_op jit(solution)/shard_map/ppermute | solution.py:615
  12.9 0.0 copy-start
  12.9 0.9 %copy-done = f32[3,8,2,8,128]{4,3,2,1,0:T(8,128)S(1)} copy-done((f32[3,8,2,8,128]{4,3,2,1,0:T(8,128)S(1)}, f32[3,8,2,8,128]{4,3,2,1,0:T(8,128)}, u32[]{:S(2)}) %copy-start) | copy-done | bytes 196632
  13.8 0.1 shard_map.51
  13.9 0.0 collective-permute-done.left_ref
  13.9 0.6 collective-permute-done.1.right_ref
  14.5 0.2 shard_map.52
  14.7 3.2 %collective-permute-start.2 = (f32[10,8,256]{2,1,0:T(8,128)S(1)}, f32[10,8,256]{2,1,0:T(8,128)S(1)}, u32[]{:S(2)}, u32[]{:S(2)}) collective-permute-start(f32[10,8,256]{2,1,0:T(8,128)S(1)} %get-tuple-element.29), channel_id=1, source_target_pairs={{0,16},{16,32},{32,48},{48,64},{64,80},{80,96},{96,112},{112,128},... | collective-permute-start | bytes 245768 | tf_op jit(solution)/shard_map/ppermute | solution.py:615
  17.9 3.9 %collective-permute-start.3 = (f32[10,8,256]{2,1,0:T(8,128)S(1)}, f32[10,8,256]{2,1,0:T(8,128)S(1)}, u32[]{:S(2)}, u32[]{:S(2)}) collective-permute-start(f32[10,8,256]{2,1,0:T(8,128)S(1)} %get-tuple-element.31), channel_id=1, source_target_pairs={{0,496},{16,0},{32,16},{48,32},{64,48},{80,64},{96,80},{112,96},{1... | collective-permute-start | bytes 245768 | tf_op jit(solution)/shard_map/ppermute | solution.py:615
  21.7 0.7 collective-permute-done.2.left_ref
  22.5 0.2 collective-permute-done.3.right_ref
  22.7 0.9 %shard_map.53 = (f32[8,2,8,256]{3,2,1,0:T(8,128)S(1)}, f32[12,2,8,128]{3,2,1,0:T(8,128)S(1)}, f32[3,8,2,8,128]{4,3,2,1,0:T(8,128)S(1)}, f32[2,2,8,128]{3,2,1,0:T(8,128)S(1)}) custom-call(f32[10,8,256]{2,1,0:T(8,128)S(1)} %collective-permute-done.2.left_ref, f32[3,8,2,8,256]{4,3,2,1,0:T(8,128)S(1)} %get-tuple-element.30.mid_ref, ...), custom_call_target="tpu_custom_call" | custom-call | tf_op jit(solution)/shard_map/pallas_call | solution.py:601
  23.5 0.0 collective-permute-start.5
  23.6 4.1 %collective-permute-start.4 = (f32[12,2,8,128]{3,2,1,0:T(8,128)S(1)}, f32[12,2,8,128]{3,2,1,0:T(8,128)S(1)}, u32[]{:S(2)}, u32[]{:S(2)}) collective-permute-start(f32[12,2,8,128]{3,2,1,0:T(8,128)S(1)} %get-tuple-element.33), channel_id=1, source_target_pairs={{0,496},{16,0},{32,16},{48,32},{64,48},{80,64},{96,80},{112,96},{1... | collective-permute-start | bytes 294920 | tf_op jit(solution)/shard_map/ppermute | solution.py:615
  27.7 0.8 %collective-permute-done.5.left_ref = f32[12,2,8,128]{3,2,1,0:T(8,128)S(1)} collective-permute-done((f32[12,2,8,128]{3,2,1,0:T(8,128)S(1)}, f32[12,2,8,128]{3,2,1,0:T(8,128)S(1)}, u32[]{:S(2)}, u32[]{:S(2)}) %collective-permute-start.5) | collective-permute-done | bytes 98336 | tf_op jit(solution)/shard_map/ppermute | solution.py:615
  28.5 0.2 collective-permute-done.4.right_ref
  28.7 0.0 collective-permute-start.6
  28.7 4.3 %collective-permute-start.7 = (f32[12,2,8,128]{3,2,1,0:T(8,128)S(1)}, f32[12,2,8,128]{3,2,1,0:T(8,128)S(1)}, u32[]{:S(2)}, u32[]{:S(2)}) collective-permute-start(f32[12,2,8,128]{3,2,1,0:T(8,128)S(1)} %collective-permute-done.4.right_ref), channel_id=1, source_target_pairs={{0,496},{16,0},{32,16},{48,32},{64,48},{80,64},{96,80},{112,96},{1... | collective-permute-start | bytes 294920 | tf_op jit(solution)/shard_map/ppermute | solution.py:615
  32.9 1.7 %shard_map.54 = (f32[4,8,10,8,256]{4,3,2,1,0:T(8,128)S(1)}, f32[4,8,10,8,256]{4,3,2,1,0:T(8,128)S(1)}, f32[2,10,8,256]{3,2,1,0:T(8,128)S(1)}, f32[8,128]{1,0:T(8,128)S(1)}) custom-call(f32[12,2,8,128]{3,2,1,0:T(8,128)S(1)} %collective-permute-done.5.left_ref, f32[8,2,8,256]{3,2,1,0:T(8,128)S(1)} %get-tuple-element.36.mid_ref, ...), custom_call_target="tpu_custom_call" | custom-call | flops 5000000 | bytes 4000000 | tf_op jit(solution)/shard_map/pallas_call | solution.py:601
  34.7 0.0 collective-permute-done.6.left_ref
  34.7 0.0 collective-permute-done.7.right_ref
  34.7 1.8 %shard_map.55 = (f32[4,8,10,8,256]{4,3,2,1,0:T(8,128)S(1)}, f32[4,8,10,8,256]{4,3,2,1,0:T(8,128)S(1)}, f32[2,10,8,256]{3,2,1,0:T(8,128)S(1)}, f32[32,128]{1,0:T(8,128)S(1)}) custom-call(f32[12,2,8,128]{3,2,1,0:T(8,128)S(1)} %collective-permute-done.6.left_ref, ...), custom_call_target="tpu_custom_call", output_to_operand_aliasing={{0}: (4, {}), {1}: (5, {}), {2}: (6, {})} | custom-call | tf_op jit(solution)/shard_map/pallas_call | solution.py:601
  36.5 17.3 %all_to_all.17 = f32[32,1,128]{2,1,0:T(1,128)S(1)} all-to-all(f32[32,1,128]{2,1,0:T(1,128)S(1)} %bitcast.9), channel_id=1, replica_groups={{0,16,1,17,2,18,3,19,4,20,5,21,6,22,7,23,8,24,9,25,10,26,11,27,12,28,13..., dimensions={0} | all-to-all | bytes 32768 | tf_op jit(solution)/shard_map/all_to_all | solution.py:621
  53.8 0.1 reduce_sum.9
  53.9 20.9 %all_to_all.18 = f32[16,1,128]{2,1,0:T(1,128)S(1)} all-to-all(f32[16,1,128]{2,1,0:T(1,128)S(1)} %broadcast_in_dim.2), channel_id=1, replica_groups={{0,32,64,96,128,160,192,224,256,288,320,352,384,416,448,480},{16,48,80,..., dimensions={0} | all-to-all | bytes 16384 | tf_op jit(solution)/shard_map/all_to_all | solution.py:624
  74.8 1.3 %shard_map.56 = (f32[3,8,2,8,128]{4,3,2,1,0:T(8,128)}, f32[8,2,8,128]{3,2,1,0:T(8,128)}) custom-call(f32[16,128]{1,0:T(8,128)S(1)} %bitcast.8, f32[4,8,10,8,256]{4,3,2,1,0:T(8,128)S(1)} %get-tuple-element.43.v_ref, f32[3,8,2,8,128]{4,3,2,1,0:T(8,128)S(1)} %get-tuple-element.44.w_ref, f32[2,2,8,128]{3,2,1,0:T(8,128)S(1)} %get-tuple-element.45.open_ref, ...), custom_call_target="tpu_custom_call" | custom-call | tf_op jit(solution)/shard_map/pallas_call | solution.py:601
  (1 shorter events, 0.0 us)
Async XLA Ops:
  3.3 10.6 %collective-permute-start = (f32[8,2,8,128]{3,2,1,0:T(8,128)}, f32[8,2,8,128]{3,2,1,0:T(8,128)S(1)}, u32[]{:S(2)}, u32[]{:S(2)}) collective-permute-start(f32[8,2,8,128]{3,2,1,0:T(8,128)} %get-tuple-element.27), channel_id=1, source_target_pairs={{0,1},{1,2},{2,3},{3,4},{4,5},{5,6},{6,7},{7,8},{8,9},{9,10},{10,1... | collective-permute-start | bytes 196616 | tf_op jit(solution)/shard_map/ppermute | solution.py:615
  7.3 7.2 %collective-permute-start.1 = (f32[8,2,8,128]{3,2,1,0:T(8,128)}, f32[8,2,8,128]{3,2,1,0:T(8,128)S(1)}, u32[]{:S(2)}, u32[]{:S(2)}) collective-permute-start(f32[8,2,8,128]{3,2,1,0:T(8,128)} %get-tuple-element.28), channel_id=1, source_target_pairs={{0,15},{1,0},{2,1},{3,2},{4,3},{5,4},{6,5},{7,6},{8,7},{9,8},{10,9... | collective-permute-start | bytes 196616 | tf_op jit(solution)/shard_map/ppermute | solution.py:615
  12.9 0.9 %copy-start = (f32[3,8,2,8,128]{4,3,2,1,0:T(8,128)S(1)}, f32[3,8,2,8,128]{4,3,2,1,0:T(8,128)}, u32[]{:S(2)}) copy-start(f32[3,8,2,8,128]{4,3,2,1,0:T(8,128)} %get-tuple-element.25.r_ref) | copy-start | bytes 589828
  14.7 7.8 %collective-permute-start.2 = (f32[10,8,256]{2,1,0:T(8,128)S(1)}, f32[10,8,256]{2,1,0:T(8,128)S(1)}, u32[]{:S(2)}, u32[]{:S(2)}) collective-permute-start(f32[10,8,256]{2,1,0:T(8,128)S(1)} %get-tuple-element.29), channel_id=1, source_target_pairs={{0,16},{16,32},{32,48},{48,64},{64,80},{80,96},{96,112},{112,128},... | collective-permute-start | bytes 245768 | tf_op jit(solution)/shard_map/ppermute | solution.py:615
  17.9 4.8 %collective-permute-start.3 = (f32[10,8,256]{2,1,0:T(8,128)S(1)}, f32[10,8,256]{2,1,0:T(8,128)S(1)}, u32[]{:S(2)}, u32[]{:S(2)}) collective-permute-start(f32[10,8,256]{2,1,0:T(8,128)S(1)} %get-tuple-element.31), channel_id=1, source_target_pairs={{0,496},{16,0},{32,16},{48,32},{64,48},{80,64},{96,80},{112,96},{1... | collective-permute-start | bytes 245768 | tf_op jit(solution)/shard_map/ppermute | solution.py:615
  23.5 4.9 %collective-permute-start.5 = (f32[12,2,8,128]{3,2,1,0:T(8,128)S(1)}, f32[12,2,8,128]{3,2,1,0:T(8,128)S(1)}, u32[]{:S(2)}, u32[]{:S(2)}) collective-permute-start(f32[12,2,8,128]{3,2,1,0:T(8,128)S(1)} %get-tuple-element.33), channel_id=1, source_target_pairs={{0,16},{16,32},{32,48},{48,64},{64,80},{80,96},{96,112},{112,128},... | collective-permute-start | bytes 294920 | tf_op jit(solution)/shard_map/ppermute | solution.py:615
  23.6 5.1 %collective-permute-start.4 = (f32[12,2,8,128]{3,2,1,0:T(8,128)S(1)}, f32[12,2,8,128]{3,2,1,0:T(8,128)S(1)}, u32[]{:S(2)}, u32[]{:S(2)}) collective-permute-start(f32[12,2,8,128]{3,2,1,0:T(8,128)S(1)} %get-tuple-element.33), channel_id=1, source_target_pairs={{0,496},{16,0},{32,16},{48,32},{64,48},{80,64},{96,80},{112,96},{1... | collective-permute-start | bytes 294920 | tf_op jit(solution)/shard_map/ppermute | solution.py:615
  28.7 6.0 %collective-permute-start.6 = (f32[12,2,8,128]{3,2,1,0:T(8,128)S(1)}, f32[12,2,8,128]{3,2,1,0:T(8,128)S(1)}, u32[]{:S(2)}, u32[]{:S(2)}) collective-permute-start(f32[12,2,8,128]{3,2,1,0:T(8,128)S(1)} %collective-permute-done.5.left_ref), channel_id=1, source_target_pairs={{0,16},{16,32},{32,48},{48,64},{64,80},{80,96},{96,112},{112,128},... | collective-permute-start | bytes 294920 | tf_op jit(solution)/shard_map/ppermute | solution.py:615
  28.7 6.0 %collective-permute-start.7 = (f32[12,2,8,128]{3,2,1,0:T(8,128)S(1)}, f32[12,2,8,128]{3,2,1,0:T(8,128)S(1)}, u32[]{:S(2)}, u32[]{:S(2)}) collective-permute-start(f32[12,2,8,128]{3,2,1,0:T(8,128)S(1)} %collective-permute-done.4.right_ref), channel_id=1, source_target_pairs={{0,496},{16,0},{32,16},{48,32},{64,48},{80,64},{96,80},{112,96},{1... | collective-permute-start | bytes 294920 | tf_op jit(solution)/shard_map/ppermute | solution.py:615

commit v12 on v11

--- a/solution.py
+++ b/solution.py
@@ -452,13 +452,16 @@
 
 def over(low, high, body):
     count = high - low
-    lax.fori_loop(
-        low, high, lambda e, c: (body(e), c)[1], 0, unroll=count if count <= 4 else count // 2
-    )
+    if count <= 4:
+        for e in range(low, high):
+            body(e)
+    else:
+        lax.fori_loop(low, high, lambda e, c: (body(e), c)[1], 0, unroll=count // 2)
 
 
 def sides(low, body):
-    over(0, 4, lambda t: body(low + t + (t // 2) * (6 - 2 * low)))
+    for e in (low, low + 1, 8 - low, 9 - low):
+        body(e)
 
 
 def pack_sums(parts, packed):

time: 76.3 us -> 76.3 us (level)
  no operation moved by 1% of the time
where the time goes in v12:
time: 76.3 us; the launch traced here: 76.1 us
  blocking collectives  38.2 us (50%)
  starting transfers between devices  25.1 us (33%)
  Pallas kernels  8.63 us (11%)
  waiting for transfers between devices  2.45 us (3%)
  local copies, waits for them, and re-layouts  0.93 us (1%)
    ppermute x8, starting transfers between devices, shift(): lax.ppermute(value, axis, [(i, (i + by) % size) for i in range(size)])  25.1 us
    all_to_all x1, blocking collectives, total_rows(): return lax.all_to_all(part, 'gx', 0, 0, axis_index_groups=along, tiled=True)  20.9 us
    all_to_all x1, blocking collectives, total_rows(): lax.all_to_all(packed, ('gx', 'gy'), 0, 0, axis_index_groups=planes, tile...  17.3 us
    pallas_call x7, Pallas kernels, call(): pl.pallas_call(kernel, out_shape=out_shape, in_specs=[pl.BlockSpec(memory...  8.63 us
    ppermute x8, waiting for transfers between devices, shift(): lax.ppermute(value, axis, [(i, (i + by) % size) for i in range(size)])  2.45 us
  transfers between devices with their start and end apart: 8, of which 5 were waited for; matrix products, arithmetic and copies ran while one was open for 0% of the time, Pallas kernels for 2%

profile of v12, /device:TPU:1, one launch (start us, length us, event | category | flops | bytes accessed | tf_op | source)
XLA Modules:
  0.0 76.1 jit_solution(4318090203015869264)
XLA Ops:
  0.6 2.6 %shard_map.50 = (f32[3,8,2,8,128]{4,3,2,1,0:T(8,128)}, f32[8,2,8,128]{3,2,1,0:T(8,128)}, f32[8,2,8,128]{3,2,1,0:T(8,128)}) custom-call(f32[3,8,2,8,128]{4,3,2,1,0:T(8,128)} %bitcast.10, bf16[3,8,16,128]{3,2,1,0:T(8,128)(2,1)} %bitcast.11, s32[2,2,16]{2,1,0:T(2,128)} %faces_hbm.1), custom_call_target="tpu_custom_call" | custom-call | tf_op jit(solution)/shard_map/pallas_call | solution.py:604
  3.3 4.0 %collective-permute-start = (f32[8,2,8,128]{3,2,1,0:T(8,128)}, f32[8,2,8,128]{3,2,1,0:T(8,128)S(1)}, u32[]{:S(2)}, u32[]{:S(2)}) collective-permute-start(f32[8,2,8,128]{3,2,1,0:T(8,128)} %get-tuple-element.27), channel_id=1, source_target_pairs={{0,1},{1,2},{2,3},{3,4},{4,5},{5,6},{6,7},{7,8},{8,9},{9,10},{10,1... | collective-permute-start | bytes 196616 | tf_op jit(solution)/shard_map/ppermute | solution.py:618
  7.3 5.6 %collective-permute-start.1 = (f32[8,2,8,128]{3,2,1,0:T(8,128)}, f32[8,2,8,128]{3,2,1,0:T(8,128)S(1)}, u32[]{:S(2)}, u32[]{:S(2)}) collective-permute-start(f32[8,2,8,128]{3,2,1,0:T(8,128)} %get-tuple-element.28), channel_id=1, source_target_pairs={{0,15},{1,0},{2,1},{3,2},{4,3},{5,4},{6,5},{7,6},{8,7},{9,8},{10,9... | collective-permute-start | bytes 196616 | tf_op jit(solution)/shard_map/ppermute | solution.py:618
  12.9 0.0 copy-start
  12.9 0.9 %copy-done = f32[3,8,2,8,128]{4,3,2,1,0:T(8,128)S(1)} copy-done((f32[3,8,2,8,128]{4,3,2,1,0:T(8,128)S(1)}, f32[3,8,2,8,128]{4,3,2,1,0:T(8,128)}, u32[]{:S(2)}) %copy-start) | copy-done | bytes 196632
  13.8 0.1 shard_map.51
  13.9 0.0 collective-permute-done.left_ref
  13.9 0.6 collective-permute-done.1.right_ref
  14.5 0.2 shard_map.52
  14.7 3.2 %collective-permute-start.2 = (f32[10,8,256]{2,1,0:T(8,128)S(1)}, f32[10,8,256]{2,1,0:T(8,128)S(1)}, u32[]{:S(2)}, u32[]{:S(2)}) collective-permute-start(f32[10,8,256]{2,1,0:T(8,128)S(1)} %get-tuple-element.29), channel_id=1, source_target_pairs={{0,16},{16,32},{32,48},{48,64},{64,80},{80,96},{96,112},{112,128},... | collective-permute-start | bytes 245768 | tf_op jit(solution)/shard_map/ppermute | solution.py:618
  17.9 3.9 %collective-permute-start.3 = (f32[10,8,256]{2,1,0:T(8,128)S(1)}, f32[10,8,256]{2,1,0:T(8,128)S(1)}, u32[]{:S(2)}, u32[]{:S(2)}) collective-permute-start(f32[10,8,256]{2,1,0:T(8,128)S(1)} %get-tuple-element.31), channel_id=1, source_target_pairs={{0,496},{16,0},{32,16},{48,32},{64,48},{80,64},{96,80},{112,96},{1... | collective-permute-start | bytes 245768 | tf_op jit(solution)/shard_map/ppermute | solution.py:618
  21.7 0.7 collective-permute-done.2.left_ref
  22.5 0.2 collective-permute-done.3.right_ref
  22.7 0.9 %shard_map.53 = (f32[8,2,8,256]{3,2,1,0:T(8,128)S(1)}, f32[12,2,8,128]{3,2,1,0:T(8,128)S(1)}, f32[3,8,2,8,128]{4,3,2,1,0:T(8,128)S(1)}, f32[2,2,8,128]{3,2,1,0:T(8,128)S(1)}) custom-call(f32[10,8,256]{2,1,0:T(8,128)S(1)} %collective-permute-done.2.left_ref, f32[3,8,2,8,256]{4,3,2,1,0:T(8,128)S(1)} %get-tuple-element.30.mid_ref, ...), custom_call_target="tpu_custom_call" | custom-call | tf_op jit(solution)/shard_map/pallas_call | solution.py:604
  23.5 0.0 collective-permute-start.5
  23.6 4.1 %collective-permute-start.4 = (f32[12,2,8,128]{3,2,1,0:T(8,128)S(1)}, f32[12,2,8,128]{3,2,1,0:T(8,128)S(1)}, u32[]{:S(2)}, u32[]{:S(2)}) collective-permute-start(f32[12,2,8,128]{3,2,1,0:T(8,128)S(1)} %get-tuple-element.33), channel_id=1, source_target_pairs={{0,496},{16,0},{32,16},{48,32},{64,48},{80,64},{96,80},{112,96},{1... | collective-permute-start | bytes 294920 | tf_op jit(solution)/shard_map/ppermute | solution.py:618
  27.7 0.8 %collective-permute-done.5.left_ref = f32[12,2,8,128]{3,2,1,0:T(8,128)S(1)} collective-permute-done((f32[12,2,8,128]{3,2,1,0:T(8,128)S(1)}, f32[12,2,8,128]{3,2,1,0:T(8,128)S(1)}, u32[]{:S(2)}, u32[]{:S(2)}) %collective-permute-start.5) | collective-permute-done | bytes 98336 | tf_op jit(solution)/shard_map/ppermute | solution.py:618
  28.5 0.2 collective-permute-done.4.right_ref
  28.7 0.0 collective-permute-start.6
  28.7 4.3 %collective-permute-start.7 = (f32[12,2,8,128]{3,2,1,0:T(8,128)S(1)}, f32[12,2,8,128]{3,2,1,0:T(8,128)S(1)}, u32[]{:S(2)}, u32[]{:S(2)}) collective-permute-start(f32[12,2,8,128]{3,2,1,0:T(8,128)S(1)} %collective-permute-done.4.right_ref), channel_id=1, source_target_pairs={{0,496},{16,0},{32,16},{48,32},{64,48},{80,64},{96,80},{112,96},{1... | collective-permute-start | bytes 294920 | tf_op jit(solution)/shard_map/ppermute | solution.py:618
  32.9 1.7 %shard_map.54 = (f32[4,8,10,8,256]{4,3,2,1,0:T(8,128)S(1)}, f32[4,8,10,8,256]{4,3,2,1,0:T(8,128)S(1)}, f32[2,10,8,256]{3,2,1,0:T(8,128)S(1)}, f32[8,128]{1,0:T(8,128)S(1)}) custom-call(f32[12,2,8,128]{3,2,1,0:T(8,128)S(1)} %collective-permute-done.5.left_ref, f32[8,2,8,256]{3,2,1,0:T(8,128)S(1)} %get-tuple-element.36.mid_ref, ...), custom_call_target="tpu_custom_call" | custom-call | flops 5000000 | bytes 4000000 | tf_op jit(solution)/shard_map/pallas_call | solution.py:604
  34.7 0.0 collective-permute-done.6.left_ref
  34.7 0.0 collective-permute-done.7.right_ref
  34.7 1.8 %shard_map.55 = (f32[4,8,10,8,256]{4,3,2,1,0:T(8,128)S(1)}, f32[4,8,10,8,256]{4,3,2,1,0:T(8,128)S(1)}, f32[2,10,8,256]{3,2,1,0:T(8,128)S(1)}, f32[32,128]{1,0:T(8,128)S(1)}) custom-call(f32[12,2,8,128]{3,2,1,0:T(8,128)S(1)} %collective-permute-done.6.left_ref, ...), custom_call_target="tpu_custom_call", output_to_operand_aliasing={{0}: (4, {}), {1}: (5, {}), {2}: (6, {})} | custom-call | tf_op jit(solution)/shard_map/pallas_call | solution.py:604
  36.5 17.3 %all_to_all.17 = f32[32,1,128]{2,1,0:T(1,128)S(1)} all-to-all(f32[32,1,128]{2,1,0:T(1,128)S(1)} %bitcast.9), channel_id=1, replica_groups={{0,16,1,17,2,18,3,19,4,20,5,21,6,22,7,23,8,24,9,25,10,26,11,27,12,28,13..., dimensions={0} | all-to-all | bytes 32768 | tf_op jit(solution)/shard_map/all_to_all | solution.py:624
  53.8 0.1 reduce_sum.9
  53.9 20.9 %all_to_all.18 = f32[16,1,128]{2,1,0:T(1,128)S(1)} all-to-all(f32[16,1,128]{2,1,0:T(1,128)S(1)} %broadcast_in_dim.2), channel_id=1, replica_groups={{0,32,64,96,128,160,192,224,256,288,320,352,384,416,448,480},{16,48,80,..., dimensions={0} | all-to-all | bytes 16384 | tf_op jit(solution)/shard_map/all_to_all | solution.py:627
  74.8 1.3 %shard_map.56 = (f32[3,8,2,8,128]{4,3,2,1,0:T(8,128)}, f32[8,2,8,128]{3,2,1,0:T(8,128)}) custom-call(f32[16,128]{1,0:T(8,128)S(1)} %bitcast.8, f32[4,8,10,8,256]{4,3,2,1,0:T(8,128)S(1)} %get-tuple-element.43.v_ref, f32[3,8,2,8,128]{4,3,2,1,0:T(8,128)S(1)} %get-tuple-element.44.w_ref, f32[2,2,8,128]{3,2,1,0:T(8,128)S(1)} %get-tuple-element.45.open_ref, ...), custom_call_target="tpu_custom_call" | custom-call | tf_op jit(solution)/shard_map/pallas_call | solution.py:604
  (1 shorter events, 0.0 us)
Async XLA Ops:
  3.3 10.6 %collective-permute-start = (f32[8,2,8,128]{3,2,1,0:T(8,128)}, f32[8,2,8,128]{3,2,1,0:T(8,128)S(1)}, u32[]{:S(2)}, u32[]{:S(2)}) collective-permute-start(f32[8,2,8,128]{3,2,1,0:T(8,128)} %get-tuple-element.27), channel_id=1, source_target_pairs={{0,1},{1,2},{2,3},{3,4},{4,5},{5,6},{6,7},{7,8},{8,9},{9,10},{10,1... | collective-permute-start | bytes 196616 | tf_op jit(solution)/shard_map/ppermute | solution.py:618
  7.3 7.2 %collective-permute-start.1 = (f32[8,2,8,128]{3,2,1,0:T(8,128)}, f32[8,2,8,128]{3,2,1,0:T(8,128)S(1)}, u32[]{:S(2)}, u32[]{:S(2)}) collective-permute-start(f32[8,2,8,128]{3,2,1,0:T(8,128)} %get-tuple-element.28), channel_id=1, source_target_pairs={{0,15},{1,0},{2,1},{3,2},{4,3},{5,4},{6,5},{7,6},{8,7},{9,8},{10,9... | collective-permute-start | bytes 196616 | tf_op jit(solution)/shard_map/ppermute | solution.py:618
  12.9 0.9 %copy-start = (f32[3,8,2,8,128]{4,3,2,1,0:T(8,128)S(1)}, f32[3,8,2,8,128]{4,3,2,1,0:T(8,128)}, u32[]{:S(2)}) copy-start(f32[3,8,2,8,128]{4,3,2,1,0:T(8,128)} %get-tuple-element.25.r_ref) | copy-start | bytes 589828
  14.7 7.8 %collective-permute-start.2 = (f32[10,8,256]{2,1,0:T(8,128)S(1)}, f32[10,8,256]{2,1,0:T(8,128)S(1)}, u32[]{:S(2)}, u32[]{:S(2)}) collective-permute-start(f32[10,8,256]{2,1,0:T(8,128)S(1)} %get-tuple-element.29), channel_id=1, source_target_pairs={{0,16},{16,32},{32,48},{48,64},{64,80},{80,96},{96,112},{112,128},... | collective-permute-start | bytes 245768 | tf_op jit(solution)/shard_map/ppermute | solution.py:618
  17.9 4.8 %collective-permute-start.3 = (f32[10,8,256]{2,1,0:T(8,128)S(1)}, f32[10,8,256]{2,1,0:T(8,128)S(1)}, u32[]{:S(2)}, u32[]{:S(2)}) collective-permute-start(f32[10,8,256]{2,1,0:T(8,128)S(1)} %get-tuple-element.31), channel_id=1, source_target_pairs={{0,496},{16,0},{32,16},{48,32},{64,48},{80,64},{96,80},{112,96},{1... | collective-permute-start | bytes 245768 | tf_op jit(solution)/shard_map/ppermute | solution.py:618
  23.5 4.9 %collective-permute-start.5 = (f32[12,2,8,128]{3,2,1,0:T(8,128)S(1)}, f32[12,2,8,128]{3,2,1,0:T(8,128)S(1)}, u32[]{:S(2)}, u32[]{:S(2)}) collective-permute-start(f32[12,2,8,128]{3,2,1,0:T(8,128)S(1)} %get-tuple-element.33), channel_id=1, source_target_pairs={{0,16},{16,32},{32,48},{48,64},{64,80},{80,96},{96,112},{112,128},... | collective-permute-start | bytes 294920 | tf_op jit(solution)/shard_map/ppermute | solution.py:618
  23.6 5.1 %collective-permute-start.4 = (f32[12,2,8,128]{3,2,1,0:T(8,128)S(1)}, f32[12,2,8,128]{3,2,1,0:T(8,128)S(1)}, u32[]{:S(2)}, u32[]{:S(2)}) collective-permute-start(f32[12,2,8,128]{3,2,1,0:T(8,128)S(1)} %get-tuple-element.33), channel_id=1, source_target_pairs={{0,496},{16,0},{32,16},{48,32},{64,48},{80,64},{96,80},{112,96},{1... | collective-permute-start | bytes 294920 | tf_op jit(solution)/shard_map/ppermute | solution.py:618
  28.7 6.0 %collective-permute-start.6 = (f32[12,2,8,128]{3,2,1,0:T(8,128)S(1)}, f32[12,2,8,128]{3,2,1,0:T(8,128)S(1)}, u32[]{:S(2)}, u32[]{:S(2)}) collective-permute-start(f32[12,2,8,128]{3,2,1,0:T(8,128)S(1)} %collective-permute-done.5.left_ref), channel_id=1, source_target_pairs={{0,16},{16,32},{32,48},{48,64},{64,80},{80,96},{96,112},{112,128},... | collective-permute-start | bytes 294920 | tf_op jit(solution)/shard_map/ppermute | solution.py:618
  28.7 6.0 %collective-permute-start.7 = (f32[12,2,8,128]{3,2,1,0:T(8,128)S(1)}, f32[12,2,8,128]{3,2,1,0:T(8,128)S(1)}, u32[]{:S(2)}, u32[]{:S(2)}) collective-permute-start(f32[12,2,8,128]{3,2,1,0:T(8,128)S(1)} %collective-permute-done.4.right_ref), channel_id=1, source_target_pairs={{0,496},{16,0},{32,16},{48,32},{64,48},{80,64},{96,80},{112,96},{1... | collective-permute-start | bytes 294920 | tf_op jit(solution)/shard_map/ppermute | solution.py:618

commit v13 on v11

--- a/solution.py
+++ b/solution.py
@@ -617,8 +617,10 @@
 
 def total_rows(packed):
     nx, ny = lax.axis_size("gx"), lax.axis_size("gy")
-    planes = [[(2 * z + c) * ny + y for y in range(ny) for c in range(2)] for z in range(nx // 2)]
-    part = lax.all_to_all(packed, ("gx", "gy"), 0, 0, axis_index_groups=planes, tiled=True)
+    pairs = [[i, i + 1] for i in range(0, nx, 2)]
+    part = lax.all_gather(packed, "gx", axis_index_groups=pairs)
+    part = jnp.broadcast_to(part[0, :1] + part[1, :1], (ny, 128))
+    part = lax.all_to_all(part, "gy", 0, 0, tiled=True)
     part = jnp.broadcast_to(jnp.sum(part, axis=0, keepdims=True), (nx // 2, 128))
     along = [[2 * z + c for z in range(nx // 2)] for c in range(2)]
     return lax.all_to_all(part, "gx", 0, 0, axis_index_groups=along, tiled=True)
@@ -677,7 +679,7 @@
     )
     basis, images, faces, packed = call(
         outer_kernel,
-        state + (shape(2 * lax.axis_size("gy"), 128),),
+        state + (shape(8, 128),),
         [],
         left2, right2, known, ky, basis, images, faces,
         aliases={4: 0, 5: 1, 6: 2},

time: 76.3 us -> 77.8 us (1.020)
  blocking collectives: 38.2 us -> 39 us
    all_gather x0 -> x1, blocking collectives: none -> 5.01 us  [total_rows(): part = lax.all_gather(packed, 'gx', axis_index_groups=pairs)]
    all_to_all x1, blocking collectives: 17.3 us -> 12.9 us  [total_rows(): part = lax.all_to_all(part, 'gy', 0, 0, tiled=True)]
where the time goes in v13:
time: 77.8 us; the launch traced here: 76.9 us
  blocking collectives  39 us (50%)
  starting transfers between devices  25.1 us (32%)
  Pallas kernels  8.62 us (11%)
  waiting for transfers between devices  2.45 us (3%)
  local copies, waits for them, and re-layouts  0.94 us (1%)
    ppermute x8, starting transfers between devices, shift(): lax.ppermute(value, axis, [(i, (i + by) % size) for i in range(size)])  25.1 us
    all_to_all x1, blocking collectives, total_rows(): return lax.all_to_all(part, 'gx', 0, 0, axis_index_groups=along, tiled=True)  21.1 us
    all_to_all x1, blocking collectives, total_rows(): part = lax.all_to_all(part, 'gy', 0, 0, tiled=True)  12.9 us
    pallas_call x7, Pallas kernels, call(): pl.pallas_call(kernel, out_shape=out_shape, in_specs=[pl.BlockSpec(memory...  8.62 us
    all_gather x1, blocking collectives, total_rows(): part = lax.all_gather(packed, 'gx', axis_index_groups=pairs)  5.01 us
    ppermute x8, waiting for transfers between devices, shift(): lax.ppermute(value, axis, [(i, (i + by) % size) for i in range(size)])  2.45 us
  transfers between devices with their start and end apart: 8, of which 5 were waited for; matrix products, arithmetic and copies ran while one was open for 0% of the time, Pallas kernels for 2%

profile of v13, /device:TPU:1, one launch (start us, length us, event | category | flops | bytes accessed | tf_op | source)
XLA Modules:
  0.0 76.9 jit_solution(4143155445392952813)
XLA Ops:
  0.6 2.6 %shard_map.50 = (f32[3,8,2,8,128]{4,3,2,1,0:T(8,128)}, f32[8,2,8,128]{3,2,1,0:T(8,128)}, f32[8,2,8,128]{3,2,1,0:T(8,128)}) custom-call(f32[3,8,2,8,128]{4,3,2,1,0:T(8,128)} %bitcast.10, bf16[3,8,16,128]{3,2,1,0:T(8,128)(2,1)} %bitcast.11, s32[2,2,16]{2,1,0:T(2,128)} %faces_hbm.1), custom_call_target="tpu_custom_call" | custom-call | tf_op jit(solution)/shard_map/pallas_call | solution.py:601
  3.3 4.0 %collective-permute-start = (f32[8,2,8,128]{3,2,1,0:T(8,128)}, f32[8,2,8,128]{3,2,1,0:T(8,128)S(1)}, u32[]{:S(2)}, u32[]{:S(2)}) collective-permute-start(f32[8,2,8,128]{3,2,1,0:T(8,128)} %get-tuple-element.27), channel_id=1, source_target_pairs={{0,1},{1,2},{2,3},{3,4},{4,5},{5,6},{6,7},{7,8},{8,9},{9,10},{10,1... | collective-permute-start | bytes 196616 | tf_op jit(solution)/shard_map/ppermute | solution.py:615
  7.3 5.6 %collective-permute-start.1 = (f32[8,2,8,128]{3,2,1,0:T(8,128)}, f32[8,2,8,128]{3,2,1,0:T(8,128)S(1)}, u32[]{:S(2)}, u32[]{:S(2)}) collective-permute-start(f32[8,2,8,128]{3,2,1,0:T(8,128)} %get-tuple-element.28), channel_id=1, source_target_pairs={{0,15},{1,0},{2,1},{3,2},{4,3},{5,4},{6,5},{7,6},{8,7},{9,8},{10,9... | collective-permute-start | bytes 196616 | tf_op jit(solution)/shard_map/ppermute | solution.py:615
  12.9 0.0 copy-start
  12.9 0.9 %copy-done = f32[3,8,2,8,128]{4,3,2,1,0:T(8,128)S(1)} copy-done((f32[3,8,2,8,128]{4,3,2,1,0:T(8,128)S(1)}, f32[3,8,2,8,128]{4,3,2,1,0:T(8,128)}, u32[]{:S(2)}) %copy-start) | copy-done | bytes 196632
  13.8 0.1 shard_map.51
  13.9 0.0 collective-permute-done.left_ref
  13.9 0.6 collective-permute-done.1.right_ref
  14.5 0.2 shard_map.52
  14.7 3.2 %collective-permute-start.2 = (f32[10,8,256]{2,1,0:T(8,128)S(1)}, f32[10,8,256]{2,1,0:T(8,128)S(1)}, u32[]{:S(2)}, u32[]{:S(2)}) collective-permute-start(f32[10,8,256]{2,1,0:T(8,128)S(1)} %get-tuple-element.29), channel_id=1, source_target_pairs={{0,16},{16,32},{32,48},{48,64},{64,80},{80,96},{96,112},{112,128},... | collective-permute-start | bytes 245768 | tf_op jit(solution)/shard_map/ppermute | solution.py:615
  17.9 3.9 %collective-permute-start.3 = (f32[10,8,256]{2,1,0:T(8,128)S(1)}, f32[10,8,256]{2,1,0:T(8,128)S(1)}, u32[]{:S(2)}, u32[]{:S(2)}) collective-permute-start(f32[10,8,256]{2,1,0:T(8,128)S(1)} %get-tuple-element.31), channel_id=1, source_target_pairs={{0,496},{16,0},{32,16},{48,32},{64,48},{80,64},{96,80},{112,96},{1... | collective-permute-start | bytes 245768 | tf_op jit(solution)/shard_map/ppermute | solution.py:615
  21.7 0.7 collective-permute-done.2.left_ref
  22.5 0.2 collective-permute-done.3.right_ref
  22.7 0.9 %shard_map.53 = (f32[8,2,8,256]{3,2,1,0:T(8,128)S(1)}, f32[12,2,8,128]{3,2,1,0:T(8,128)S(1)}, f32[3,8,2,8,128]{4,3,2,1,0:T(8,128)S(1)}, f32[2,2,8,128]{3,2,1,0:T(8,128)S(1)}) custom-call(f32[10,8,256]{2,1,0:T(8,128)S(1)} %collective-permute-done.2.left_ref, f32[3,8,2,8,256]{4,3,2,1,0:T(8,128)S(1)} %get-tuple-element.30.mid_ref, ...), custom_call_target="tpu_custom_call" | custom-call | tf_op jit(solution)/shard_map/pallas_call | solution.py:601
  23.5 0.0 collective-permute-start.5
  23.6 4.1 %collective-permute-start.4 = (f32[12,2,8,128]{3,2,1,0:T(8,128)S(1)}, f32[12,2,8,128]{3,2,1,0:T(8,128)S(1)}, u32[]{:S(2)}, u32[]{:S(2)}) collective-permute-start(f32[12,2,8,128]{3,2,1,0:T(8,128)S(1)} %get-tuple-element.33), channel_id=1, source_target_pairs={{0,496},{16,0},{32,16},{48,32},{64,48},{80,64},{96,80},{112,96},{1... | collective-permute-start | bytes 294920 | tf_op jit(solution)/shard_map/ppermute | solution.py:615
  27.7 0.8 %collective-permute-done.5.left_ref = f32[12,2,8,128]{3,2,1,0:T(8,128)S(1)} collective-permute-done((f32[12,2,8,128]{3,2,1,0:T(8,128)S(1)}, f32[12,2,8,128]{3,2,1,0:T(8,128)S(1)}, u32[]{:S(2)}, u32[]{:S(2)}) %collective-permute-start.5) | collective-permute-done | bytes 98336 | tf_op jit(solution)/shard_map/ppermute | solution.py:615
  28.5 0.2 collective-permute-done.4.right_ref
  28.7 0.0 collective-permute-start.6
  28.7 4.3 %collective-permute-start.7 = (f32[12,2,8,128]{3,2,1,0:T(8,128)S(1)}, f32[12,2,8,128]{3,2,1,0:T(8,128)S(1)}, u32[]{:S(2)}, u32[]{:S(2)}) collective-permute-start(f32[12,2,8,128]{3,2,1,0:T(8,128)S(1)} %collective-permute-done.4.right_ref), channel_id=1, source_target_pairs={{0,496},{16,0},{32,16},{48,32},{64,48},{80,64},{96,80},{112,96},{1... | collective-permute-start | bytes 294920 | tf_op jit(solution)/shard_map/ppermute | solution.py:615
  32.9 1.7 %shard_map.54 = (f32[4,8,10,8,256]{4,3,2,1,0:T(8,128)S(1)}, f32[4,8,10,8,256]{4,3,2,1,0:T(8,128)S(1)}, f32[2,10,8,256]{3,2,1,0:T(8,128)S(1)}, f32[8,128]{1,0:T(8,128)S(1)}) custom-call(f32[12,2,8,128]{3,2,1,0:T(8,128)S(1)} %collective-permute-done.5.left_ref, f32[8,2,8,256]{3,2,1,0:T(8,128)S(1)} %get-tuple-element.36.mid_ref, ...), custom_call_target="tpu_custom_call" | custom-call | flops 5000000 | bytes 4000000 | tf_op jit(solution)/shard_map/pallas_call | solution.py:601
  34.7 0.0 collective-permute-done.6.left_ref
  34.7 0.0 collective-permute-done.7.right_ref
  34.7 1.8 %shard_map.55 = (f32[4,8,10,8,256]{4,3,2,1,0:T(8,128)S(1)}, f32[4,8,10,8,256]{4,3,2,1,0:T(8,128)S(1)}, f32[2,10,8,256]{3,2,1,0:T(8,128)S(1)}, f32[8,128]{1,0:T(8,128)S(1)}) custom-call(f32[12,2,8,128]{3,2,1,0:T(8,128)S(1)} %collective-permute-done.6.left_ref, ...), custom_call_target="tpu_custom_call", output_to_operand_aliasing={{0}: (4, {}), {1}: (5, {}), {2}: (6, {})} | custom-call | tf_op jit(solution)/shard_map/pallas_call | solution.py:601
  36.5 5.0 %all-gather = f32[16,128]{1,0:T(8,128)S(1)} all-gather(f32[8,128]{1,0:T(8,128)S(1)} %get-tuple-element.42), channel_id=2, replica_groups={{0,16},{32,48},{64,80},{96,112},{128,144},{160,176},{192,208},{224,240}..., dimensions={0}, use_global_device_ids=true | all-gather | bytes 12288 | tf_op jit(solution)/shard_map/all_gather | solution.py:621
  41.6 12.9 %all_to_all.14 = f32[16,1,128]{2,1,0:T(1,128)S(1)} all-to-all(f32[16,1,128]{2,1,0:T(1,128)S(1)} %broadcast_in_dim.4), channel_id=1, replica_groups=mesh['gx'=32,'gy'=16] {'gy'}, dimensions={0} | all-to-all | bytes 16384 | tf_op jit(solution)/shard_map/all_to_all | solution.py:623
  54.5 21.1 %all_to_all.15 = f32[16,1,128]{2,1,0:T(1,128)S(1)} all-to-all(f32[16,1,128]{2,1,0:T(1,128)S(1)} %broadcast_in_dim.5), channel_id=1, replica_groups={{0,32,64,96,128,160,192,224,256,288,320,352,384,416,448,480},{16,48,80,..., dimensions={0} | all-to-all | bytes 16384 | tf_op jit(solution)/shard_map/all_to_all | solution.py:626
  75.6 1.3 %shard_map.56 = (f32[3,8,2,8,128]{4,3,2,1,0:T(8,128)}, f32[8,2,8,128]{3,2,1,0:T(8,128)}) custom-call(f32[16,128]{1,0:T(8,128)S(1)} %bitcast.9, f32[4,8,10,8,256]{4,3,2,1,0:T(8,128)S(1)} %get-tuple-element.43.v_ref, f32[3,8,2,8,128]{4,3,2,1,0:T(8,128)S(1)} %get-tuple-element.44.w_ref, f32[2,2,8,128]{3,2,1,0:T(8,128)S(1)} %get-tuple-element.45.open_ref, ...), custom_call_target="tpu_custom_call" | custom-call | tf_op jit(solution)/shard_map/pallas_call | solution.py:601
  (4 shorter events, 0.0 us)
Async XLA Ops:
  3.3 10.6 %collective-permute-start = (f32[8,2,8,128]{3,2,1,0:T(8,128)}, f32[8,2,8,128]{3,2,1,0:T(8,128)S(1)}, u32[]{:S(2)}, u32[]{:S(2)}) collective-permute-start(f32[8,2,8,128]{3,2,1,0:T(8,128)} %get-tuple-element.27), channel_id=1, source_target_pairs={{0,1},{1,2},{2,3},{3,4},{4,5},{5,6},{6,7},{7,8},{8,9},{9,10},{10,1... | collective-permute-start | bytes 196616 | tf_op jit(solution)/shard_map/ppermute | solution.py:615
  7.3 7.2 %collective-permute-start.1 = (f32[8,2,8,128]{3,2,1,0:T(8,128)}, f32[8,2,8,128]{3,2,1,0:T(8,128)S(1)}, u32[]{:S(2)}, u32[]{:S(2)}) collective-permute-start(f32[8,2,8,128]{3,2,1,0:T(8,128)} %get-tuple-element.28), channel_id=1, source_target_pairs={{0,15},{1,0},{2,1},{3,2},{4,3},{5,4},{6,5},{7,6},{8,7},{9,8},{10,9... | collective-permute-start | bytes 196616 | tf_op jit(solution)/shard_map/ppermute | solution.py:615
  12.9 0.9 %copy-start = (f32[3,8,2,8,128]{4,3,2,1,0:T(8,128)S(1)}, f32[3,8,2,8,128]{4,3,2,1,0:T(8,128)}, u32[]{:S(2)}) copy-start(f32[3,8,2,8,128]{4,3,2,1,0:T(8,128)} %get-tuple-element.25.r_ref) | copy-start | bytes 589828
  14.7 7.8 %collective-permute-start.2 = (f32[10,8,256]{2,1,0:T(8,128)S(1)}, f32[10,8,256]{2,1,0:T(8,128)S(1)}, u32[]{:S(2)}, u32[]{:S(2)}) collective-permute-start(f32[10,8,256]{2,1,0:T(8,128)S(1)} %get-tuple-element.29), channel_id=1, source_target_pairs={{0,16},{16,32},{32,48},{48,64},{64,80},{80,96},{96,112},{112,128},... | collective-permute-start | bytes 245768 | tf_op jit(solution)/shard_map/ppermute | solution.py:615
  17.9 4.8 %collective-permute-start.3 = (f32[10,8,256]{2,1,0:T(8,128)S(1)}, f32[10,8,256]{2,1,0:T(8,128)S(1)}, u32[]{:S(2)}, u32[]{:S(2)}) collective-permute-start(f32[10,8,256]{2,1,0:T(8,128)S(1)} %get-tuple-element.31), channel_id=1, source_target_pairs={{0,496},{16,0},{32,16},{48,32},{64,48},{80,64},{96,80},{112,96},{1... | collective-permute-start | bytes 245768 | tf_op jit(solution)/shard_map/ppermute | solution.py:615
  23.5 4.9 %collective-permute-start.5 = (f32[12,2,8,128]{3,2,1,0:T(8,128)S(1)}, f32[12,2,8,128]{3,2,1,0:T(8,128)S(1)}, u32[]{:S(2)}, u32[]{:S(2)}) collective-permute-start(f32[12,2,8,128]{3,2,1,0:T(8,128)S(1)} %get-tuple-element.33), channel_id=1, source_target_pairs={{0,16},{16,32},{32,48},{48,64},{64,80},{80,96},{96,112},{112,128},... | collective-permute-start | bytes 294920 | tf_op jit(solution)/shard_map/ppermute | solution.py:615
  23.6 5.1 %collective-permute-start.4 = (f32[12,2,8,128]{3,2,1,0:T(8,128)S(1)}, f32[12,2,8,128]{3,2,1,0:T(8,128)S(1)}, u32[]{:S(2)}, u32[]{:S(2)}) collective-permute-start(f32[12,2,8,128]{3,2,1,0:T(8,128)S(1)} %get-tuple-element.33), channel_id=1, source_target_pairs={{0,496},{16,0},{32,16},{48,32},{64,48},{80,64},{96,80},{112,96},{1... | collective-permute-start | bytes 294920 | tf_op jit(solution)/shard_map/ppermute | solution.py:615
  28.7 6.0 %collective-permute-start.6 = (f32[12,2,8,128]{3,2,1,0:T(8,128)S(1)}, f32[12,2,8,128]{3,2,1,0:T(8,128)S(1)}, u32[]{:S(2)}, u32[]{:S(2)}) collective-permute-start(f32[12,2,8,128]{3,2,1,0:T(8,128)S(1)} %collective-permute-done.5.left_ref), channel_id=1, source_target_pairs={{0,16},{16,32},{32,48},{48,64},{64,80},{80,96},{96,112},{112,128},... | collective-permute-start | bytes 294920 | tf_op jit(solution)/shard_map/ppermute | solution.py:615
  28.7 6.0 %collective-permute-start.7 = (f32[12,2,8,128]{3,2,1,0:T(8,128)S(1)}, f32[12,2,8,128]{3,2,1,0:T(8,128)S(1)}, u32[]{:S(2)}, u32[]{:S(2)}) collective-permute-start(f32[12,2,8,128]{3,2,1,0:T(8,128)S(1)} %collective-permute-done.4.right_ref), channel_id=1, source_target_pairs={{0,496},{16,0},{32,16},{48,32},{64,48},{80,64},{96,80},{112,96},{1... | collective-permute-start | bytes 294920 | tf_op jit(solution)/shard_map/ppermute | solution.py:615
